TPU v7x, 32 devices: a whole 2x2x4 slice. The times are simulated.
32 devices in a mesh: fsdp: 8 (over z, y), tp: 4 (over x, core).
Axes of the slice: x: 2, y: 2, z: 4, core: 2. Of those that a mesh axis runs over, the one named last changes fastest.
Arguments:
- hidden: bfloat16 [2, 576, 16384], P(None, 'fsdp', 'tp'), may hold values from -6 to 6
- queries: bfloat16 [2, 576, 16384], P(None, 'fsdp', 'tp'), may hold values from -256 to 256
- cache_keys: bfloat16 [576, 32, 1024], P('fsdp', None, 'tp'), may hold values from -6 to 6
- cache_values: bfloat16 [576, 32, 1024], P('fsdp', None, 'tp'), may hold values from -6 to 6
- new_values: bfloat16 [2, 576, 1024], P(None, 'fsdp', 'tp'), may hold values from -6 to 6
- lengths: int32 [576], P('fsdp'), may hold values from 2 to 32, as said below
- base_weight: bfloat16 [16384, 1024], P(None, 'tp'), may hold values from -0.046875 to 0.046875
- delta_values: bfloat16 [16384, 1024], P(('fsdp', 'tp')), may hold values from -4 to 4
- delta_scales: bfloat16 [128, 8], P('fsdp', 'tp'), may hold values from 0.0019989014 to 0.019897461
- block_order: int32 [128], replicated, may hold values from 0 to 127, each once
Outputs:
- attended: bfloat16 [2, 576, 16384], P(None, 'fsdp', 'tp')
- new_keys: bfloat16 [2, 576, 1024], P(None, 'fsdp', 'tp')
Inputs may be any that keep to these rules, and one draw needn't show every extreme that they name: `lengths`: every row has at least two valid cached positions; some row holds 32. `block_order`: A permutation of the block rows.
All inputs are finite; a program needn't handle non-finite values.
Results may differ from a plain program's by a relative error of at most 0.0056.
Values may be sent and summed in bfloat16 or wider, within the bound.
No kernel may reach another device: no remote copies, remote signals or barrier semaphores. Data moves between devices by JAX's collectives and lax.ppermute only.
A program may use at most 128 MiB of HBM per device.

v0:
```python
import math

import jax
import jax.numpy as jnp
from jax import lax
from jax.sharding import PartitionSpec as P

HD = 128
KVH = 8
QH = 128
BLK = 128


def per_device(
    hidden,
    queries,
    cache_keys,
    cache_values,
    new_values,
    lengths,
    base_weight,
    delta_values,
    delta_scales,
    block_order,
):
    columns = base_weight.shape[1]
    whole_rows = lax.all_gather(delta_values, "tp", axis=0, tiled=True)
    local_rows = lax.dynamic_slice_in_dim(whole_rows, lax.axis_index("tp") * columns, columns, 1)
    col_blocks = columns // BLK
    local_blocks = local_rows.shape[0] // BLK
    scaled = (
        local_rows.reshape(local_blocks, BLK, col_blocks, BLK).astype(jnp.float32)
        * delta_scales.astype(jnp.float32)[:, None, :, None]
    )
    pieces = scaled.reshape(local_blocks, BLK, columns).astype(jnp.bfloat16)
    gathered = lax.all_gather(pieces, "fsdp", axis=0, tiled=True)
    total_rows = gathered.shape[0]
    positions = jnp.arange(total_rows)
    inverse = jnp.sum(
        jnp.where(block_order[None, :] == positions[:, None], positions[None, :], 0), axis=1
    )
    ordered = jnp.take(gathered, inverse, axis=0)
    refreshed = (
        base_weight.astype(jnp.float32)
        + ordered.reshape(total_rows * BLK, columns).astype(jnp.float32)
    ).astype(jnp.bfloat16)
    steps_count, rows_count = (hidden.shape[0], hidden.shape[1])
    start_keys = jnp.zeros((steps_count, rows_count, columns), jnp.float32)
    piece = lax.all_gather(hidden, "tp", axis=2, tiled=True)
    width = piece.shape[2]
    product = jnp.dot(
        piece.reshape(steps_count * rows_count, width),
        refreshed,
        preferred_element_type=jnp.float32,
    )
    keys_sum = product.reshape(start_keys.shape)
    new_keys = keys_sum.astype(jnp.bfloat16)
    heads_here = columns // HD
    group = QH // KVH
    factor = 1.0 / math.sqrt(HD)
    capacity = cache_keys.shape[1]
    query = queries.reshape(steps_count, rows_count, heads_here, group, HD)
    ckeys = cache_keys.reshape(rows_count, capacity, heads_here, HD)
    cvals = cache_values.reshape(rows_count, capacity, heads_here, HD)
    nkeys = new_keys.reshape(steps_count, rows_count, heads_here, HD)
    nvals = new_values.reshape(steps_count, rows_count, heads_here, HD)
    cached = (
        jnp.einsum("srhgd,rchd->srhgc", query, ckeys, preferred_element_type=jnp.float32) * factor
    )
    fresh = (
        jnp.einsum("srhgd,urhd->srhgu", query, nkeys, preferred_element_type=jnp.float32) * factor
    )
    cache_mask = jnp.arange(capacity)[None, :] < lengths[:, None]
    step_mask = jnp.arange(steps_count)[None, :] <= jnp.arange(steps_count)[:, None]
    cached = jnp.where(cache_mask[None, :, None, None, :], cached, -1e30)
    fresh = jnp.where(step_mask[:, None, None, None, :], fresh, -1e30)
    joined = jnp.concatenate([cached, fresh], axis=4)
    top = jnp.max(joined, axis=4, keepdims=True)
    expo = jnp.exp(joined - top)
    weights = (expo / jnp.sum(expo, axis=4, keepdims=True)).astype(jnp.bfloat16)
    result = jnp.einsum(
        "srhgc,rchd->srhgd", weights[..., :capacity], cvals, preferred_element_type=jnp.float32
    )
    result = result + jnp.einsum(
        "srhgu,urhd->srhgd", weights[..., capacity:], nvals, preferred_element_type=jnp.float32
    )
    attended = result.reshape(steps_count, rows_count, heads_here * group * HD).astype(jnp.bfloat16)
    return (attended, new_keys)


def solution(mesh):
    in_specs = (
        P(None, "fsdp", "tp"),
        P(None, "fsdp", "tp"),
        P("fsdp", None, "tp"),
        P("fsdp", None, "tp"),
        P(None, "fsdp", "tp"),
        P("fsdp"),
        P(None, "tp"),
        P(("fsdp", "tp"), None),
        P("fsdp", "tp"),
        P(),
    )
    out_specs = (P(None, "fsdp", "tp"), P(None, "fsdp", "tp"))
    return jax.shard_map(
        per_device, mesh=mesh, in_specs=in_specs, out_specs=out_specs, check_vma=False
    )
```

profile of v0, /device:TPU:0, one launch (start us, length us, event | category | flops | bytes accessed | tf_op | source)
XLA Modules:
  0.0 245.7 jit_solution(5047294887954039864)
XLA Ops:
  7.2 0.0 all-gather.4.cloned.1.call-start
  7.2 0.7 all-gather.4.cloned.1.call-update
  7.9 0.0 all-gather.6.cloned.1.call-start
  7.9 0.7 copy.78
  8.7 0.1 mul.35
  8.8 38.0 %all-gather.4.cloned.1.call-done = bf16[2048,1024]{1,0:T(8,128)(2,1)} async-done(((bf16[512,1024]{1,0:T(8,128)(2,1)}), bf16[2048,1024]{1,0:T(8,128)(2,1)}) %all-gather.4.cloned.1.call-update) | async-done | bytes 4194320 | tf_op jit(solution)/shard_map/all_gather | solution.py:27
  46.8 1.3 constant_dynamic-slice_fusion
  48.1 0.0 copy-start.1
  48.1 1.3 fusion.2
  49.4 0.0 all-gather.6.cloned.1.call-update
  49.4 0.0 all-gather.8.cloned.1.call-start
  49.4 0.7 all-gather.8.cloned.1.call-update
  50.1 0.0 copy-done.1
  50.1 0.2 copy.101
  50.4 0.3 copy-done.2
  50.7 1.1 reshape.90
  51.8 0.5 copy-done.3
  52.4 0.3 reshape.93
  52.7 1.5 reshape.94
  54.2 0.0 copy-done.7
  54.2 0.1 select_reduce_fusion
  54.4 0.0 copy-done.6
  54.4 0.1 iota_compare_fusion.1
  54.5 4.2 %fusion.18 = (f32[2,72,2,16]{3,0,2,1:T(2,128)}, f32[2,72,2,16,32]{4,3,0,2,1:T(8,128)}) fusion(bf16[2,72,2,16,128]{4,3,2,1,0:T(8,128)(2,1)S(1)} %bitcast.37, bf16[72,32,2,128,1]{3,2,1,0,4:T(2,128)(2,1)} %bitcast.42, pred[72,32]{1,0:T(8,128)(4,1)S(1)} %iota_compare_fusion.1), kind=kOutput, calls=%fused_computation.38 | convolution fusion | flops 38186496 | bytes 2969856 | tf_op jit(solution)/shard_map/srhgd,rchd->srhgc/dot_general | solution.py:68
  58.7 0.1 broadcast_bitcast_fusion
  58.8 115.7 %all-gather.6.cloned.1.call-done = bf16[128,128,256]{2,1,0:T(8,128)(2,1)} async-done(((bf16[16,128,256]{2,1,0:T(8,128)(2,1)}), bf16[128,128,256]{2,1,0:T(8,128)(2,1)}) %all-gather.6.cloned.1.call-update) | async-done | bytes 8388624 | tf_op jit(solution)/shard_map/all_gather | solution.py:36
  174.5 10.4 %gather_fusion = bf16[128,128,256]{2,1,0:T(8,128)(2,1)} fusion(bf16[128,128,256]{2,1,0:T(8,128)(2,1)} %all-gather.6.cloned.1.call-done, s32[1024]{0:T(1024)S(1)} %pad_clamp_fusion), kind=kCustom, calls=%fused_computation | custom fusion | bytes 16777728 | tf_op jit(solution)/shard_map/jit(_take)/gather | solution.py:42
  184.9 8.0 %bitcast_select_fusion = bf16[16384,256]{1,0:T(8,128)(2,1)} fusion(bf16[128,128,256]{2,1,0:T(8,128)(2,1)} %gather_fusion, pred[16384]{0:T(1024)(128)(4,1)S(1)} %broadcast_bitcast_fusion), kind=kLoop, calls=%fused_computation.3 | loop fusion | flops 4194304 | bytes 16793600 | tf_op jit(solution)/shard_map/jit(_take)/select_n | solution.py:42
  193.0 18.8 %all-gather.8.cloned.1.call-done = bf16[2,72,16384]{2,1,0:T(8,128)(2,1)} async-done(((bf16[2,72,4096]{2,1,0:T(8,128)(2,1)}), bf16[2,72,16384]{2,1,0:T(8,128)(2,1)}) %all-gather.8.cloned.1.call-update) | async-done | bytes 4718608 | tf_op jit(solution)/shard_map/all_gather | solution.py:49
  211.7 9.3 %fusion.9 = bf16[256,144]{0,1:T(8,128)(2,1)S(1)} fusion(bf16[144,16384]{1,0:T(8,128)(2,1)} %bitcast.36, bf16[16384,256]{1,0:T(8,128)(2,1)} %bitcast_select_fusion, bf16[16384,256]{1,0:T(8,128)(2,1)} %param.16), kind=kOutput, calls=%fused_computation.17 | convolution fusion | flops 1224773632 | bytes 21569536 | tf_op jit(solution)/shard_map/dot_general | solution.py:51
  221.0 0.0 copy-start.4
  221.1 0.6 copy-done.4
  221.7 2.8 %fusion.10 = f32[72,2,2,2,16]{4,2,3,1,0:T(2,128)S(1)} fusion(bf16[2,72,2,16,128]{4,3,2,1,0:T(8,128)(2,1)S(1)} %bitcast.38, bf16[2,72,2,128,1]{3,2,1,0,4:T(2,128)(2,1)S(1)} %bitcast.45), kind=kOutput, calls=%fused_computation.18 | convolution fusion | flops 2359296 | bytes 1290240 | tf_op jit(solution)/shard_map/srhgd,urhd->srhgu/dot_general | solution.py:71
  224.5 0.2 copy.81
  224.7 0.7 fusion.17
  225.4 0.8 copy.83
  226.2 3.0 %copy.82 = f32[2,72,2,16,2]{4,3,0,2,1:T(8,128)S(1)} copy(f32[2,72,2,16,2]{1,3,0,4,2:T(8,128)} %get-tuple-element.3) | data formatting | bytes 73728 | tf_op jit(solution)/shard_map/jit(_where)/select_n | solution.py:76
  229.1 1.1 reduce_max.22
  230.2 0.0 copy-start
  230.2 3.7 %fusion.13 = f32[2,72,2,16]{3,0,2,1:T(2,128)S(1)} fusion(f32[2,72,2,16]{3,0,2,1:T(2,128)S(1)} %reduce_max.22, f32[2,72,2,16,2]{4,3,0,2,1:T(8,128)S(1)} %copy.82, f32[2,72,2,16,32]{4,3,0,2,1:T(8,128)} %get-tuple-element.5), kind=kLoop, calls=%fused_computation.21 | loop fusion | flops 465408 | bytes 663552 | tf_op jit(solution)/shard_map/reduce_sum | solution.py:80
  233.9 0.0 copy-done
  233.9 2.2 divide_convert_fusion
  236.1 0.0 copy-start.5
  236.2 0.5 fusion.5
  236.6 0.4 copy-done.5
  237.0 0.6 fusion.3
  237.6 0.2 copy.87
  237.8 1.4 convert_element_type.61
  (10 shorter events, 0.1 us)
Async XLA Ops:
  7.2 39.6 %all-gather.4.cloned.1.call-start = ((), (), s32[]{:S(2)}) async-start(), calls=%async_computation | async-start | bytes 5242880 | tf_op jit(solution)/shard_map/all_gather | solution.py:27
  7.9 166.6 %all-gather.6.cloned.1.call-start = ((), (), s32[]{:S(2)}) async-start(), calls=%async_computation.1 | async-start | bytes 9437184 | tf_op jit(solution)/shard_map/all_gather | solution.py:36
  48.1 2.1 copy-start.1
  49.4 1.3 copy-start.2
  49.4 162.3 %all-gather.8.cloned.1.call-start = ((), (), s32[]{:S(2)}) async-start(), calls=%async_computation.2 | async-start | bytes 5898240 | tf_op jit(solution)/shard_map/all_gather | solution.py:49
  50.7 1.7 copy-start.3
  50.7 3.5 %copy-start.7 = (s32[128]{0:T(128)S(1)}, s32[128]{0:T(128)}, u32[]{:S(2)}) copy-start(s32[128]{0:T(128)} %param.19) | copy-start | bytes 1540
  50.7 3.7 %copy-start.6 = (s32[72]{0:T(128)S(1)}, s32[72]{0:T(128)}, u32[]{:S(2)}) copy-start(s32[72]{0:T(128)} %param.15) | copy-start | bytes 868
  221.0 0.6 copy-start.4
  230.2 3.7 %copy-start = (f32[2,72,2,16,32]{4,3,0,2,1:T(8,128)S(1)}, f32[2,72,2,16,32]{4,3,0,2,1:T(8,128)}, u32[]{:S(2)}) copy-start(f32[2,72,2,16,32]{4,3,0,2,1:T(8,128)} %get-tuple-element.5) | copy-start | bytes 1769476
  236.1 0.9 copy-start.5
Sparse Core Ops, SparseCore 0:
  9.6 37.1 all-gather.3
  49.5 124.9 all-gather.5
  176.1 35.6 all-gather.7
where the time goes:
time: 246 us
  waiting for transfers between devices  174 us (71%)
  local copies, waits for them, and re-layouts  23.2 us (9%)
  matrix products  17.4 us (7%)
  other arithmetic  17.2 us (7%)
  between operations  13.9 us (6%)
    all_gather x1, waiting for transfers between devices, per_device(): gathered = lax.all_gather(pieces, 'fsdp', axis=0, tiled=True)  116 us
    all_gather x1, waiting for transfers between devices, per_device(): whole_rows = lax.all_gather(delta_values, 'tp', axis=0, tiled=True)  38 us
    all_gather x1, waiting for transfers between devices, per_device(): piece = lax.all_gather(hidden, 'tp', axis=2, tiled=True)  18.8 us
    gather x1, local copies, waits for them, and re-layouts, per_device(): ordered = jnp.take(gathered, inverse, axis=0)  10.4 us
    dot_general x1, matrix products, per_device(): jnp.dot(piece.reshape(steps_count * rows_count, width), refreshed, prefer...  9.31 us
    select_n x2, other arithmetic, per_device(): ordered = jnp.take(gathered, inverse, axis=0)  8.05 us
  transfers between devices with their start and end apart: 3, of which 3 were waited for; matrix products, arithmetic and copies ran while one was open for 11% of the time, Pallas kernels for 0%

commit v1 on v0

v1 whole, which is shorter than its diff:
```python
import functools
import math

import jax
import jax.numpy as jnp
from jax import lax
from jax.experimental import pallas as pl
from jax.experimental.pallas import tpu as pltpu
from jax.sharding import Mesh
from jax.sharding import PartitionSpec as P

HD = 128
KVH = 8
QH = 128
BLK = 128
GROUP = QH // KVH
RB = 8
MIB = 1024 * 1024
GRANT = 57 * MIB
CONTRACT_LAST = (((1,), (1,)), ((), ()))
CONTRACT_FIRST = (((0,), (0,)), ((), ()))


def params(held_bytes):
    return pltpu.CompilerParams(vmem_limit_bytes=min(60 * MIB, 8 * MIB + 2 * held_bytes))


def first_group(part, groups, parts):
    return part * (groups - row_count(groups, parts)) // max(parts - 1, 1)


def row_count(groups, parts):
    return -(-groups // parts)


def scatter_kernel(nx, parts, order_ref, *refs):
    pieces, (o_ref, all_ref, sems) = refs[:-3], refs[-3:]
    nf = o_ref.shape[0]
    per_t = all_ref.shape[2] // BLK
    per_f = order_ref.shape[0] // nf
    per_part = o_ref.shape[2] // BLK
    per_own = max(per_part // nx, 1)
    x = lax.axis_index("tx")
    core = lax.axis_index("core")

    def fetch(i):
        return pltpu.make_async_copy(pieces[i], all_ref.at[i], sems.at[i])

    for i in range(len(pieces)):
        fetch(i).start()
    for i in range(len(pieces)):
        fetch(i).wait()

    t_bits = per_t.bit_length() - 1
    assert per_t == 1 << t_bits and nx & (nx - 1) == 0
    for f in range(nf):
        for at in range(per_part):
            from_group = f * per_f + at
            if parts > 1:
                chip, rest = at // per_own, at % per_own
                from_group = f * per_f + chip * 2 * per_own + core * per_own + rest
            block = order_ref[from_group]
            owner = lax.shift_right_logical(block, t_bits)
            chip = (lax.shift_right_logical(owner, 1) + nx - x) & (nx - 1)
            index = chip * 2 + ((owner & 1) ^ core)
            lanes = pl.ds(pl.multiple_of((block & (per_t - 1)) * BLK, BLK), BLK)
            o_ref[f, :, at * BLK : (at + 1) * BLK] = all_ref[index, :, lanes]


def scatter(order, pieces, nf, split):
    rows, cols = pieces[0].shape
    width = len(pieces) * cols // nf // split
    return pl.pallas_call(
        functools.partial(scatter_kernel, len(pieces) // 2, split),
        out_shape=jax.ShapeDtypeStruct((nf, rows, width), jnp.bfloat16),
        in_specs=[pl.BlockSpec(memory_space=pltpu.SMEM)]
        + [pl.BlockSpec(memory_space=pl.ANY)] * len(pieces),
        out_specs=pl.BlockSpec(memory_space=pltpu.VMEM),
        scratch_shapes=[
            pltpu.VMEM((len(pieces), rows, cols), jnp.bfloat16),
            pltpu.SemaphoreType.DMA((len(pieces),)),
        ],
        compiler_params=params(4 * len(pieces) * rows * cols),
        cost_estimate=pl.CostEstimate(
            flops=0, bytes_accessed=3 * len(pieces) * rows * cols, transcendentals=0
        ),
        name="scatter_columns",
    )(order, *pieces)


def base_kernel(nx, info_ref, base_ref, *refs):
    pieces, (o_ref, held, sems) = refs[:-3], refs[-3:]
    width = pieces[0].shape[1]
    depth = held.shape[1]
    chunks = width // depth

    def fetch(n):
        row = pl.multiple_of(info_ref[n // chunks] * width + n % chunks * depth, depth)
        return pltpu.make_async_copy(base_ref.at[pl.ds(row, depth), :], held.at[n], sems.at[n])

    for n in range(held.shape[0]):
        fetch(n).start()
    total = jnp.zeros((o_ref.shape[0] * o_ref.shape[1], o_ref.shape[2]), jnp.float32)
    for n in range(held.shape[0]):
        lanes = slice(n % chunks * depth, (n % chunks + 1) * depth)
        first = n // chunks * nx
        part = jnp.concatenate(
            [pieces[first + r][:, lanes].astype(jnp.float32) for r in range(nx)], axis=0
        ).astype(jnp.bfloat16)
        fetch(n).wait()
        total = total + jnp.dot(part, held[n], preferred_element_type=jnp.float32)
    o_ref[...] = total.reshape(o_ref.shape)


def base_product(owners, pieces, base, nx):
    rows, width = pieces[0].shape
    cols = base.shape[1]
    quarters = len(pieces) // nx
    depth = min(width, 1024)
    count = quarters * width // depth
    size = nx * rows * cols
    return pl.pallas_call(
        functools.partial(base_kernel, nx),
        out_shape=jax.ShapeDtypeStruct((nx, rows, cols), jnp.float32),
        in_specs=[
            pl.BlockSpec(memory_space=pltpu.SMEM),
            pl.BlockSpec(memory_space=pl.ANY),
        ]
        + [pl.BlockSpec(memory_space=pltpu.VMEM)] * len(pieces),
        out_specs=pl.BlockSpec(memory_space=pltpu.VMEM),
        scratch_shapes=[
            pltpu.VMEM((count, depth, cols), jnp.bfloat16),
            pltpu.SemaphoreType.DMA((count,)),
        ],
        compiler_params=pltpu.CompilerParams(vmem_limit_bytes=GRANT),
        cost_estimate=pl.CostEstimate(
            flops=2 * size * width * quarters,
            bytes_accessed=2 * quarters * width * (cols + nx * rows) + 4 * size,
            transcendentals=0,
        ),
        name="base_keys",
    )(owners, base, *pieces)


def product_kernel(spread, part, step, s_ref, *refs):
    o_ref, scaled_ref = refs[-2:]
    x_ref, ws = refs[0], refs[1 : 1 + spread]
    earlier = refs[1 + spread : -2]
    nx, own, cols = ws[0].shape
    x = lax.axis_index("tx")
    core = lax.axis_index("core")
    for q in range(nx):
        total = earlier[0][q] if earlier else jnp.zeros((x_ref.shape[0], cols), jnp.float32)
        source = lax.rem(q + nx - x, nx)
        for d, w_ref in enumerate(ws):
            w = w_ref[q]
            at = 0
            if spread > 1:
                chip = lax.rem(x + d, nx)
                at = pl.multiple_of(chip * own, BLK)
                first = (chip * 2 + lax.bitwise_xor(core, part)) * (own // BLK)
                for b in range(own // BLK):
                    rows = slice(b * BLK, (b + 1) * BLK)
                    for c in range(cols // BLK):
                        lanes = slice(c * BLK, (c + 1) * BLK)
                        values = w_ref[q, rows, lanes].astype(jnp.float32)
                        values = values * s_ref[source, first + b, c]
                        scaled_ref[q, d, rows, lanes] = values.astype(jnp.bfloat16)
                w = scaled_ref[q, d]
            total = total + jnp.dot(
                x_ref[:, pl.ds(at, own)], w, preferred_element_type=jnp.float32
            )
        if step == "last":
            nf, _, rows, _ = o_ref.shape
            o_ref[:, q] = total.reshape(nf, rows, cols).astype(jnp.bfloat16)
        else:
            o_ref[q] = total


def product(scales, x, ws, nf, part=0, earlier=None, last=True):
    total, depth = x.shape
    nx, own, cols = ws[0].shape
    rows = total // nf
    made = nx * total * cols
    read = total * depth + len(ws) * ws[0].size
    before = [] if earlier is None else [earlier]
    out = jax.ShapeDtypeStruct((nx, total, cols), jnp.float32)
    if last:
        out = jax.ShapeDtypeStruct((nf, nx, rows, cols), jnp.bfloat16)
    return pl.pallas_call(
        functools.partial(product_kernel, len(ws), part, "last" if last else "first"),
        out_shape=out,
        in_specs=[pl.BlockSpec(memory_space=pltpu.SMEM)]
        + [pl.BlockSpec(memory_space=pltpu.VMEM)] * (1 + len(ws) + len(before)),
        out_specs=pl.BlockSpec(memory_space=pltpu.VMEM),
        scratch_shapes=[pltpu.VMEM((nx, len(ws), own, cols), jnp.bfloat16)],
        compiler_params=params(4 * read + 8 * made),
        cost_estimate=pl.CostEstimate(
            flops=2 * made * depth,
            bytes_accessed=2 * read + 6 * made,
            transcendentals=0,
        ),
        name="partial_keys",
    )(scales, x, *ws, *before)


def cached_kernel(len_ref, q_ref, ck_ref, cv_ref, qp_ref, acc_ref, ml_ref):
    step = pl.program_id(0)
    steps, taken = q_ref.shape[:2]
    cap = ck_ref.shape[1]
    heads = ck_ref.shape[2] // HD
    many = steps * GROUP * RB
    factor = 1.0 / math.sqrt(HD)
    place = lax.broadcasted_iota(jnp.int32, (cap, many), 0)
    row = lax.rem(lax.broadcasted_iota(jnp.int32, (cap, many), 1), RB)
    chains = [(i, h) for i in range(taken) for h in range(heads)]
    scores = []
    for i, h in chains:
        lanes = slice(h * HD, (h + 1) * HD)
        q = jnp.concatenate(
            [
                q_ref[s, i, :, (h * GROUP + g) * HD : (h * GROUP + g + 1) * HD].astype(jnp.float32)
                for s in range(steps)
                for g in range(GROUP)
            ],
            axis=0,
        ).astype(jnp.bfloat16)
        qp_ref[i, h] = q
        k = ck_ref[i * RB : (i + 1) * RB, :, lanes].reshape(RB * cap, HD)
        scores.append(
            lax.dot_general(k, q, CONTRACT_LAST, preferred_element_type=jnp.float32)
        )
    weights = []
    for (i, h), sc in zip(chains, scores):
        if h == 0:
            bias = jnp.concatenate(
                [
                    jnp.where(
                        (row == r) & (place < len_ref[(step * taken + i) * RB + r]), 0.0, -1e30
                    )
                    for r in range(RB)
                ],
                axis=0,
            )
        sc = sc * factor + bias
        top = jnp.max(sc, axis=0, keepdims=True)
        expo = jnp.exp(sc - top)
        ml_ref[i, h, 0:1, :] = top
        ml_ref[i, h, 1:2, :] = jnp.sum(expo, axis=0, keepdims=True)
        weights.append(expo.astype(jnp.bfloat16))
    for (i, h), expo in zip(chains, weights):
        v = cv_ref[i * RB : (i + 1) * RB, :, h * HD : (h + 1) * HD].reshape(RB * cap, HD)
        acc_ref[i, h] = lax.dot_general(
            v, expo, CONTRACT_FIRST, preferred_element_type=jnp.float32
        )


def taken_at_once(batches):
    return 3 if batches % 3 == 0 else 1


def cached(lengths, queries, cache_keys, cache_values):
    steps, batches, _, width = queries.shape
    cap, cols = cache_keys.shape[1:]
    heads = cols // HD
    many = steps * GROUP * RB
    scores = batches * heads * many * RB * cap
    n = taken_at_once(batches)
    return pl.pallas_call(
        cached_kernel,
        grid=(batches // n,),
        out_shape=(
            jax.ShapeDtypeStruct((batches, heads, many, HD), jnp.bfloat16),
            jax.ShapeDtypeStruct((batches, heads, HD, many), jnp.float32),
            jax.ShapeDtypeStruct((batches, heads, 2, many), jnp.float32),
        ),
        in_specs=[
            pl.BlockSpec(memory_space=pltpu.SMEM),
            pl.BlockSpec((steps, n, RB, width), lambda i: (0, i, 0, 0)),
            pl.BlockSpec((n * RB, cap, cols), lambda i: (i, 0, 0)),
            pl.BlockSpec((n * RB, cap, cols), lambda i: (i, 0, 0)),
        ],
        out_specs=(
            pl.BlockSpec((n, heads, many, HD), lambda i: (i, 0, 0, 0)),
            pl.BlockSpec((n, heads, HD, many), lambda i: (i, 0, 0, 0)),
            pl.BlockSpec((n, heads, 2, many), lambda i: (i, 0, 0, 0)),
        ),
        compiler_params=pltpu.CompilerParams(vmem_limit_bytes=GRANT),
        cost_estimate=pl.CostEstimate(
            flops=4 * scores * HD,
            bytes_accessed=4 * cache_keys.size + 8 * queries.size,
            transcendentals=scores,
        ),
        name="attend_cached",
    )(lengths, queries, cache_keys, cache_values)


def merge_kernel(nx, parts_ref, near_ref, far_ref, qp_ref, acc_ref, ml_ref, nv_ref, o_ref, nk_ref, held, eye):
    step = pl.program_id(0)
    steps, batches = nk_ref.shape[0], nk_ref.shape[1]
    taken, heads = acc_ref.shape[:2]
    many = steps * GROUP * RB
    factor = 1.0 / math.sqrt(HD)

    @pl.when(step == 0)
    def _():
        me = lax.axis_index("tx")
        for x in range(nx):
            for k in range(parts_ref.shape[2] // RB):
                g = first_group(x, steps * batches, nx) + k
                rows = slice(k * RB, (k + 1) * RB)
                at = lax.rem(x + nx - me, nx)
                total = near_ref[0, g * RB : (g + 1) * RB, :] + far_ref[at, rows, :]
                for f in range(parts_ref.shape[0]):
                    total = total + parts_ref[f, x, rows, :].astype(jnp.float32)
                rounded = total.astype(jnp.bfloat16)
                nk_ref[g // batches, g % batches] = rounded
                held[g // batches, g % batches] = rounded.astype(jnp.float32)
        line = lax.broadcasted_iota(jnp.int32, (many, many), 0)
        lane = lax.broadcasted_iota(jnp.int32, (many, many), 1)
        eye[...] = jnp.where(line == lane, 1.0, 0.0).astype(jnp.bfloat16)

    key = lax.broadcasted_iota(jnp.int32, (steps * RB, many), 0)
    lane = lax.broadcasted_iota(jnp.int32, (steps * RB, many), 1)
    same_row = lax.rem(key, RB) == lax.rem(lane, RB)
    known = lax.div(key, RB) <= lax.div(lane, GROUP * RB)
    bias = jnp.where(same_row & known, 0.0, -1e30)
    chains = [(i, h) for i in range(taken) for h in range(heads)]
    scores = []
    for i, h in chains:
        lanes = slice(h * HD, (h + 1) * HD)
        keys = jnp.concatenate([held[u, step * taken + i, :, lanes] for u in range(steps)], axis=0)
        scores.append(
            lax.dot_general(
                keys.astype(jnp.bfloat16),
                qp_ref[i, h],
                CONTRACT_LAST,
                preferred_element_type=jnp.float32,
            )
        )
    added, scales = [], []
    for (i, h), sn in zip(chains, scores):
        lanes = slice(h * HD, (h + 1) * HD)
        values = jnp.concatenate(
            [nv_ref[u, i, :, lanes].astype(jnp.float32) for u in range(steps)], axis=0
        )
        sn = sn * factor + bias
        old = ml_ref[i, h, 0:1, :]
        top = jnp.maximum(old, jnp.max(sn, axis=0, keepdims=True))
        keep = jnp.exp(old - top)
        expo = jnp.exp(sn - top)
        whole = ml_ref[i, h, 1:2, :] * keep + jnp.sum(expo, axis=0, keepdims=True)
        inverse = 1.0 / whole
        scales.append(keep * inverse)
        added.append(
            lax.dot_general(
                values.astype(jnp.bfloat16),
                (expo * inverse).astype(jnp.bfloat16),
                CONTRACT_FIRST,
                preferred_element_type=jnp.float32,
            )
        )
    turned = [
        (acc_ref[i, h] * scale + more).astype(jnp.bfloat16)
        for (i, h), scale, more in zip(chains, scales, added)
    ]
    for (i, h), out in zip(chains, turned):
        out = lax.dot_general(
            eye[...], out, CONTRACT_LAST, preferred_element_type=jnp.float32
        ).astype(jnp.bfloat16)
        for s in range(steps):
            for g in range(GROUP):
                at = (s * GROUP + g) * RB
                o_ref[s, i, :, (h * GROUP + g) * HD : (h * GROUP + g + 1) * HD] = out[
                    at : at + RB
                ]


def merge(parts, near, far, packed, sums, tops, new_values):
    batches, heads, many, _ = packed.shape
    steps, _, _, cols = new_values.shape
    width = many // steps // RB * heads * HD
    n = taken_at_once(batches)
    return pl.pallas_call(
        functools.partial(merge_kernel, parts.shape[1]),
        grid=(batches // n,),
        out_shape=(
            jax.ShapeDtypeStruct((steps, batches, RB, width), jnp.bfloat16),
            jax.ShapeDtypeStruct(new_values.shape, jnp.bfloat16),
        ),
        in_specs=[
            pl.BlockSpec(parts.shape, lambda i: (0, 0, 0, 0)),
            pl.BlockSpec(near.shape, lambda i: (0, 0, 0)),
            pl.BlockSpec(far.shape, lambda i: (0, 0, 0)),
            pl.BlockSpec((n, heads, many, HD), lambda i: (i, 0, 0, 0)),
            pl.BlockSpec((n, heads, HD, many), lambda i: (i, 0, 0, 0)),
            pl.BlockSpec((n, heads, 2, many), lambda i: (i, 0, 0, 0)),
            pl.BlockSpec((steps, n, RB, cols), lambda i: (0, i, 0, 0)),
        ],
        out_specs=(
            pl.BlockSpec((steps, n, RB, width), lambda i: (0, i, 0, 0)),
            pl.BlockSpec(new_values.shape, lambda i: (0, 0, 0, 0)),
        ),
        scratch_shapes=[
            pltpu.VMEM(new_values.shape, jnp.float32),
            pltpu.VMEM((many, many), jnp.bfloat16),
        ],
        compiler_params=pltpu.CompilerParams(vmem_limit_bytes=GRANT),
        cost_estimate=pl.CostEstimate(
            flops=4 * packed.size * many,
            bytes_accessed=8 * packed.size + 4 * parts.size,
            transcendentals=packed.size // 8,
        ),
        name="attend_new",
    )(parts, near, far, packed, sums, tops, new_values)


def shift_of(nx, d):
    return [(s, (s - d) % nx) for s in range(nx)]


def part_of(array, start, size, dim):
    starts = [0] * array.ndim
    starts[dim] = start
    sizes = list(array.shape)
    sizes[dim] = size
    return lax.dynamic_slice(array, starts, sizes, allow_negative_indices=False)


def after(arrays, earlier):
    return list(lax.optimization_barrier((*arrays, earlier))[:-1])


def swap(piece):
    return lax.ppermute(piece, "core", [(0, 1), (1, 0)])


def per_device(
    nf,
    nx,
    hidden,
    queries,
    cache_keys,
    cache_values,
    new_values,
    lengths,
    base_weight,
    delta_values,
    delta_scales,
    block_order,
):
    steps, rows, width = hidden.shape
    cols = base_weight.shape[1]
    batches = rows // RB
    count = row_count(steps * batches, nx)
    x = lax.axis_index("tx")
    core = lax.axis_index("core")
    depth = 2 * nx * width // nf
    own = delta_values.shape[0]
    split = 2 if own % BLK == 0 else 1

    flat = hidden.reshape(steps * rows, width)
    slices = []
    for d in range(nx):
        start = first_group(lax.rem(x + d, nx), steps * batches, nx) * RB
        slices.append(part_of(flat, start, count * RB, 0))
    held = [[None] * nx for _ in range(nx)]
    for d in range(nx):
        came = lax.ppermute(slices[-d % nx], "tx", shift_of(nx, d)) if d else slices[0]
        held[d][0] = (came, swap(came))
    mine = scatter(block_order, [p for d in range(nx) for p in held[d][0]], nf, split)

    def to_shift(d, e):
        return [(s * 2 + c, (s - d) % nx * 2 + (c ^ e)) for s in range(nx) for c in range(2)]

    shifts = [(d, e) for d in range(nx) for e in range(2)]
    sent = []
    for e in range(2):
        to = lax.bitwise_xor(core, e)
        sent.append(
            jnp.stack([part_of(delta_values, (2 * q + to) * cols, cols, 1) for q in range(nx)])
        )
    behind = after(sent, held[-1][0][0])
    ws = [sent[0]]
    for d, e in shifts[1:]:
        ws.append(lax.ppermute((behind if d else sent)[e], ("tx", "core"), to_shift(d, e)))
    arrived = ws[1:]
    scales = [delta_scales]
    scales += [lax.ppermute(delta_scales, "tx", shift_of(nx, d)) for d in range(1, nx)]
    scales = jnp.stack(scales).astype(jnp.float32)
    if split == 1:
        by_chip = jnp.repeat(jnp.roll(scales, x, axis=0), BLK, axis=2)
        whole = jnp.zeros((nx, depth, cols), jnp.bfloat16)
        for (d, e), piece in zip(shifts, ws):
            at = (lax.rem(x + d, nx) * 2 + lax.bitwise_xor(core, e)) * own
            factor = jnp.take(by_chip, (at + jnp.arange(own)) // BLK, axis=1)
            piece = (piece.astype(jnp.float32) * factor).astype(jnp.bfloat16)
            whole = lax.dynamic_update_slice_in_dim(whole, piece, at, 1)
        ws = [whole]

    (soon,) = after([flat], mine)
    late = []
    for d in range(1, nx):
        for r in range(1, nx):
            start = first_group(lax.rem(x + (r - d) % nx, nx), steps * batches, nx) * RB
            late.append(part_of(soon, start, count * RB, 0))
            (piece,) = after(late[-1:], arrived[-1])
            came = lax.ppermute(piece, "tx", shift_of(nx, d))
            held[d][r] = (came, swap(came))

    owners = [lax.rem(x + d, nx) * 2 + lax.bitwise_xor(core, e) for d, e in shifts]
    first, then = after([jnp.stack(owners[:2]), lengths], mine)
    for piece in late:
        (first,) = after([first], piece)
    near = base_product(first, [flat, swap(soon)], base_weight, 1)
    shape = (steps, batches, RB)
    share = cached(
        then, queries.reshape(shape + queries.shape[2:]), cache_keys, cache_values
    )
    mine = lax.all_to_all(mine, "fsdp", 0, 0, tiled=True)
    xs = [mine.reshape(nf * count * RB, depth // split)]
    for earlier in (*arrived, near, share[0]):
        xs = after(xs, earlier)
    if split > 1:
        xs.append(swap(xs[0]))
        partial = product(scales, xs[0], ws[0::2], nf, 0, last=False)
        partial = product(scales, xs[1], ws[1::2], nf, 1, partial)
    else:
        partial = product(scales, xs[0], ws, nf)
    parts = lax.all_to_all(
        partial.reshape(nf * nx, count * RB, cols), ("fsdp", "tx"), 0, 0, tiled=True
    ).reshape(nf, nx, count * RB, cols)
    (rest,) = after([jnp.stack(owners[2:])], partial)
    ordered = [held[d][r][e] for d in range(1, nx) for e in range(2) for r in range(nx)]
    far = base_product(rest, ordered, base_weight, nx)
    attended, new_keys = merge(parts, near, far, *share, new_values.reshape(shape + (cols,)))
    return (attended.reshape(queries.shape), new_keys.reshape(steps, rows, cols))


def solution(mesh):
    nf, nt = mesh.shape["fsdp"], mesh.shape["tp"]
    fine = Mesh(mesh.devices.reshape(nf, nt // 2, 2), ("fsdp", "tx", "core"))
    tp = ("tx", "core")
    in_specs = (
        P(None, "fsdp", tp),
        P(None, "fsdp", tp),
        P("fsdp", None, tp),
        P("fsdp", None, tp),
        P(None, "fsdp", tp),
        P("fsdp"),
        P(None, tp),
        P(("fsdp", "tx", "core"), None),
        P("fsdp", tp),
        P(),
    )
    out_specs = (P(None, "fsdp", tp), P(None, "fsdp", tp))
    return jax.shard_map(
        functools.partial(per_device, nf, nt // 2),
        mesh=fine,
        in_specs=in_specs,
        out_specs=out_specs,
        check_vma=False,
    )
```

time: 246 us -> 95.6 us (0.39)
  waiting for transfers between devices: 174 us -> 38.2 us
  Pallas kernels: 0 us -> 28.2 us
  starting transfers between devices: 0.12 us -> 18 us
  matrix products: 17.4 us -> 0 us
  local copies, waits for them, and re-layouts: 23.2 us -> 7.83 us
  other arithmetic: 17.2 us -> 2.07 us
  between operations: 13.9 us -> 0.81 us
    all_gather x3 -> x0, waiting for transfers between devices: 172 us -> none  [the longest x1 116 us: per_device(): gathered = lax.all_gather(pieces, 'fsdp', axis=0, tiled=True)]
    pallas_call x0 -> x7, Pallas kernels: none -> 28.2 us  [the longest x2 10.7 us: base_product(): pl.pallas_call(functools.partial(base_kernel, nx), out_shape=jax.ShapeDty...]
    ppermute x0 -> x11, waiting for transfers between devices: none -> 23 us  [the longest x1 13.3 us: per_device(): lax.ppermute(slices[-d % nx], 'tx', shift_of(nx, d))]
    dot_general x5 -> x0, matrix products: 17.4 us -> none  [the longest x1 9.31 us: per_device(): jnp.dot(piece.reshape(steps_count * rows_count, width), refreshed, prefer...]
    all_to_all x0 -> x2, waiting for transfers between devices: none -> 15.2 us  [the longest x1 12.3 us: per_device(): mine = lax.all_to_all(mine, 'fsdp', 0, 0, tiled=True)]
    all_to_all x0 -> x2, starting transfers between devices: none -> 10.9 us  [the longest x1 6.23 us: per_device(): mine = lax.all_to_all(mine, 'fsdp', 0, 0, tiled=True)]
    gather x1 -> x0, local copies, waits for them, and re-layouts: 10.4 us -> none  [per_device(): ordered = jnp.take(gathered, inverse, axis=0)]
    select_n x2 -> x0, other arithmetic: 8.05 us -> none  [per_device(): ordered = jnp.take(gathered, inverse, axis=0)]
  transfers between devices with their start and end apart: 3 -> 13, of which waited for: 3 -> 7; matrix products, arithmetic and copies ran while one was open for 11% -> 4% of each run, Pallas kernels for 0% -> 22%
where the time goes in v1:
time: 95.6 us; the launch traced here: 95 us
  waiting for transfers between devices  38.2 us (40%)
  Pallas kernels  28.2 us (29%)
  starting transfers between devices  18 us (19%)
  local copies, waits for them, and re-layouts  7.83 us (8%)
  other arithmetic  2.07 us (2%)
    ppermute x1, waiting for transfers between devices, per_device(): lax.ppermute(slices[-d % nx], 'tx', shift_of(nx, d))  13.3 us
    all_to_all x1, waiting for transfers between devices, per_device(): mine = lax.all_to_all(mine, 'fsdp', 0, 0, tiled=True)  12.3 us
    pallas_call x2, Pallas kernels, base_product(): pl.pallas_call(functools.partial(base_kernel, nx), out_shape=jax.ShapeDty...  10.7 us
    all_to_all x1, starting transfers between devices, per_device(): mine = lax.all_to_all(mine, 'fsdp', 0, 0, tiled=True)  6.23 us
    pallas_call x1, Pallas kernels, cached(): pl.pallas_call(cached_kernel, grid=(batches // n,), out_shape=(jax.ShapeD...  5.58 us
    pallas_call x1, Pallas kernels, merge(): pl.pallas_call(functools.partial(merge_kernel, parts.shape[1]), grid=(bat...  5.23 us
    all_to_all x1, starting transfers between devices, per_device(): lax.all_to_all(partial.reshape(nf * nx, count * RB, cols), ('fsdp', 'tx')...  4.68 us
    ppermute x1, waiting for transfers between devices, per_device(): came = lax.ppermute(piece, 'tx', shift_of(nx, d))  4.51 us
  transfers between devices with their start and end apart: 13, of which 7 were waited for; matrix products, arithmetic and copies ran while one was open for 4% of the time, Pallas kernels for 22%

profile of v1, /device:TPU:0, one launch (start us, length us, event | category | flops | bytes accessed | tf_op | source)
XLA Modules:
  0.0 95.0 jit_solution(7981939534139539278)
XLA Ops:
  0.6 1.3 %constant_dynamic-slice_fusion.1 = (bf16[72,4096]{1,0:T(8,128)(2,1)S(1)}, bf16[72,4096]{1,0:T(8,128)(2,1)S(1)}) fusion(bf16[144,4096]{1,0:T(8,128)(2,1)} %bitcast.2.refs_0_, s32[]{:T(128)S(6)} %mul.31, s32[]{:T(128)S(6)} %mul.30), kind=kLoop, calls=%fused_computation.7 | loop fusion | bytes 2359304 | tf_op jit(solution)/shard_map/dynamic_slice | solution.py:427
  2.0 3.0 %collective-permute-start.2 = (bf16[72,4096]{1,0:T(8,128)(2,1)S(1)}, bf16[72,4096]{1,0:T(8,128)(2,1)S(1)}, u32[]{:S(2)}, u32[]{:S(2)}) collective-permute-start(bf16[72,4096]{1,0:T(8,128)(2,1)S(1)} %get-tuple-element.38), channel_id=1, source_target_pairs={{0,2},{2,0},{1,3},{3,1},{4,6},{6,4},{5,7},{7,5},{8,10},{10,8},{9,1... | collective-permute-start | bytes 1769480 | tf_op jit(solution)/shard_map/ppermute | solution.py:469
  5.0 0.0 collective-permute-start.1
  5.0 13.3 %collective-permute-done.2.refs_2_.refs_0_ = bf16[72,4096]{1,0:T(8,128)(2,1)S(1)} collective-permute-done((bf16[72,4096]{1,0:T(8,128)(2,1)S(1)}, bf16[72,4096]{1,0:T(8,128)(2,1)S(1)}, u32[]{:S(2)}, u32[]{:S(2)}) %collective-permute-start.2) | collective-permute-done | bytes 589856 | tf_op jit(solution)/shard_map/ppermute | solution.py:469
  18.3 0.0 collective-permute-start.3
  18.3 0.0 collective-permute-done.1.refs_1_
  18.3 2.0 %collective-permute-done.3.refs_3_.refs_2_ = bf16[72,4096]{1,0:T(8,128)(2,1)S(1)} collective-permute-done((bf16[72,4096]{1,0:T(8,128)(2,1)S(1)}, bf16[72,4096]{1,0:T(8,128)(2,1)S(1)}, u32[]{:S(2)}, u32[]{:S(2)}) %collective-permute-start.3) | collective-permute-done | bytes 589856 | tf_op jit(solution)/shard_map/ppermute | solution.py:435
  20.3 0.0 copy-done.6
  20.3 2.4 %scatter_columns.1 = bf16[8,72,1024]{2,1,0:T(8,128)(2,1)} custom-call(s32[128]{0:T(128)S(1)} %copy-done.6, bf16[72,4096]{1,0:T(8,128)(2,1)S(1)} %get-tuple-element.39.refs_0_, bf16[72,4096]{1,0:T(8,128)(2,1)S(1)} %collective-permute-done.1.refs_1_, bf16[72,4096]{1,0:T(8,128)(2,1)S(1)} %collective-permute-done.2.refs_2_.refs_0_, ...), custom_call_target="tpu_custom_call" | custom-call | bytes 3538944 | tf_op jit(solution)/shard_map/scatter_columns/pallas_call | solution.py:73
  22.8 0.0 copy-start.8
  22.8 6.2 %all-to-all-start = ((bf16[8,72,1024]{2,1,0:T(8,128)(2,1)}), bf16[8,72,1024]{2,1,0:T(8,128)(2,1)S(1)}, u32[]{:S(2)}, u32[]{:S(2)}) async-start(bf16[8,72,1024]{2,1,0:T(8,128)(2,1)} %scatter_columns.1), calls=%async_computation | async-start | bytes 2359296 | tf_op jit(solution)/shard_map/all_to_all | solution.py:520
  29.0 0.0 collective-permute-start.7
  29.1 0.1 dynamic-slice_bitcast_fusion.1
  29.2 0.8 pad_maximum_fusion
  30.1 0.5 collective-permute-start.4
  30.5 0.6 pad_add_fusion.info_ref
  31.1 0.1 pad_maximum_fusion.1.refs_1_
  31.2 1.6 %collective-permute-start.5 = (bf16[2,512,256]{2,1,0:T(8,128)(2,1)S(1)}, bf16[2,512,256]{2,1,0:T(8,128)(2,1)S(1)}, u32[]{:S(2)}, u32[]{:S(2)}) collective-permute-start(bf16[2,512,256]{2,1,0:T(8,128)(2,1)S(1)} %pad_maximum_fusion.1.refs_1_), channel_id=1, source_target_pairs={{0,2},{1,3},{2,0},{3,1},{4,6},{5,7},{6,4},{7,5},{8,10},{9,11},{10,... | collective-permute-start | bytes 1572872 | tf_op jit(solution)/shard_map/ppermute | solution.py:486
  32.7 0.0 collective-permute-start.6
  32.7 1.9 %constant_dynamic-slice_fusion = bf16[72,4096]{1,0:T(8,128)(2,1)} fusion(bf16[144,4096]{1,0:T(8,128)(2,1)} %bitcast.2.refs_0_, s32[]{:T(128)S(6)} %mul.30), kind=kLoop, calls=%fused_computation.6 | loop fusion | bytes 1179652 | tf_op jit(solution)/shard_map/dynamic_slice | solution.py:427
  34.7 5.6 %attend_cached.1 = (bf16[9,2,256,128]{3,2,1,0:T(8,128)(2,1)}, f32[9,2,128,256]{3,2,1,0:T(8,128)}, f32[9,2,2,256]{3,2,1,0:T(2,128)}) custom-call(s32[72]{0:T(128)} %len_ref, bf16[2,9,8,4096]{3,2,1,0:T(8,128)(2,1)} %bitcast.25, bf16[72,32,256]{2,1,0:T(8,128)(2,1)} %ck_ref.1, bf16[72,32,256]{2,1,0:T(8,128)(2,1)} %cv_ref.1), custom_call_target="tpu_custom_call" | custom-call | flops 603979776 | bytes 7077888 | tf_op jit(solution)/shard_map/attend_cached/pallas_call | solution.py:269
  40.2 0.0 collective-permute-done.7.refs_1_
  40.2 5.4 %base_keys.2.near_ref = f32[1,144,256]{2,1,0:T(8,128)} custom-call(s32[2]{0:T(128)} %pad_add_fusion.info_ref, bf16[16384,256]{1,0:T(8,128)(2,1)} %base_ref.3, bf16[144,4096]{1,0:T(8,128)(2,1)} %bitcast.2.refs_0_, bf16[144,4096]{1,0:T(8,128)(2,1)} %collective-permute-done.7.refs_1_), custom_call_target="tpu_custom_call" | custom-call | flops 603979776 | bytes 6701056 | tf_op jit(solution)/shard_map/base_keys/pallas_call | solution.py:122
  45.6 0.0 collective-permute-done.4.refs_1_
  45.6 12.3 %all-to-all-done = bf16[8,72,1024]{2,1,0:T(8,128)(2,1)S(1)} async-done(((bf16[8,72,1024]{2,1,0:T(8,128)(2,1)}), bf16[8,72,1024]{2,1,0:T(8,128)(2,1)S(1)}, u32[]{:S(2)}, u32[]{:S(2)}) %all-to-all-start) | async-done | bytes 1179680 | tf_op jit(solution)/shard_map/all_to_all | solution.py:520
  57.9 0.0 collective-permute-done.5.refs_2_
  57.9 0.8 copy-done.4
  58.7 0.0 collective-permute-done.6.refs_2_
  58.7 0.8 copy-done.2
  59.5 0.0 collective-permute-start.8
  59.5 1.5 %collective-permute-start = (bf16[16,2]{0,1:T(2,128)(2,1)S(1)}, bf16[16,2]{0,1:T(2,128)(2,1)S(1)}, u32[]{:S(2)}, u32[]{:S(2)}) collective-permute-start(bf16[16,2]{0,1:T(2,128)(2,1)S(1)} %copy-done.10), channel_id=1, source_target_pairs={{0,2},{2,0},{1,3},{3,1},{4,6},{6,4},{5,7},{7,5},{8,10},{10,8},{9,1... | collective-permute-start | bytes 200 | tf_op jit(solution)/shard_map/ppermute | solution.py:489
  61.0 0.5 collective-permute-start.9
  61.5 1.5 %collective-permute-done = bf16[16,2]{0,1:T(2,128)(2,1)S(1)} collective-permute-done((bf16[16,2]{0,1:T(2,128)(2,1)S(1)}, bf16[16,2]{0,1:T(2,128)(2,1)S(1)}, u32[]{:S(2)}, u32[]{:S(2)}) %collective-permute-start) | collective-permute-done | bytes 96 | tf_op jit(solution)/shard_map/ppermute | solution.py:489
  63.1 0.1 copy.14
  63.2 1.0 %copy-done.5 = bf16[2,512,256]{2,1,0:T(8,128)(2,1)S(1)} copy-done((bf16[2,512,256]{2,1,0:T(8,128)(2,1)S(1)}, bf16[2,512,256]{2,1,0:T(8,128)(2,1)}, u32[]{:S(2)}) %copy-start.5) | copy-done | bytes 524312
  64.2 1.7 %partial_keys.2.refs_3_ = f32[2,576,256]{2,1,0:T(8,128)S(1)} custom-call(f32[2,16,2]{2,1,0:T(8,128)S(1)} %convert_element_type.3.s_ref, bf16[576,1024]{1,0:T(8,128)(2,1)S(1)} %bitcast.23, bf16[2,512,256]{2,1,0:T(8,128)(2,1)S(1)} %pad_maximum_fusion.1.refs_1_, bf16[2,512,256]{2,1,0:T(8,128)(2,1)S(1)} %copy-done.5), custom_call_target="tpu_custom_call" | custom-call | flops 603979776 | bytes 3997696 | tf_op jit(solution)/shard_map/partial_keys/pallas_call | solution.py:190
  66.0 0.0 collective-permute-done.8.refs_0_
  66.0 2.5 %partial_keys.3 = bf16[8,2,72,256]{3,2,1,0:T(8,128)(2,1)} custom-call(f32[2,16,2]{2,1,0:T(8,128)S(1)} %convert_element_type.3.s_ref, bf16[576,1024]{1,0:T(8,128)(2,1)S(1)} %collective-permute-done.8.refs_0_, bf16[2,512,256]{2,1,0:T(8,128)(2,1)S(1)} %collective-permute-done.4.refs_1_, bf16[2,512,256]{2,1,0:T(8,128)(2,1)S(1)} %copy-done.3, ...), custom_call_target="tpu_custom_call" | custom-call | flops 603979776 | bytes 3997696 | tf_op jit(solution)/shard_map/partial_keys/pallas_call | solution.py:190
  68.5 4.7 %all-to-all-start.1 = ((bf16[16,72,256]{2,1,0:T(8,128)(2,1)}), bf16[16,72,256]{2,1,0:T(8,128)(2,1)S(1)}, u32[]{:S(2)}, u32[]{:S(2)}) async-start(bf16[16,72,256]{2,1,0:T(8,128)(2,1)} %bitcast.11), calls=%async_computation.1 | async-start | bytes 1179648 | tf_op jit(solution)/shard_map/all_to_all | solution.py:530
  73.2 4.5 %collective-permute-done.9.refs_1_ = bf16[72,4096]{1,0:T(8,128)(2,1)} collective-permute-done((bf16[72,4096]{1,0:T(8,128)(2,1)}, bf16[72,4096]{1,0:T(8,128)(2,1)}, u32[]{:S(2)}, u32[]{:S(2)}) %collective-permute-start.9) | collective-permute-done | bytes 589856 | tf_op jit(solution)/shard_map/ppermute | solution.py:508
  77.7 0.0 collective-permute-start.10
  77.7 0.6 pad_add_fusion.1.info_ref
  78.3 1.6 %collective-permute-done.10.refs_3_ = bf16[72,4096]{1,0:T(8,128)(2,1)S(1)} collective-permute-done((bf16[72,4096]{1,0:T(8,128)(2,1)}, bf16[72,4096]{1,0:T(8,128)(2,1)S(1)}, u32[]{:S(2)}, u32[]{:S(2)}) %collective-permute-start.10) | collective-permute-done | bytes 589856 | tf_op jit(solution)/shard_map/ppermute | solution.py:435
  79.9 0.8 copy-done.9
  80.7 5.3 %base_keys.3.far_ref = f32[2,72,256]{2,1,0:T(8,128)} custom-call(s32[2]{0:T(128)} %pad_add_fusion.1.info_ref, bf16[16384,256]{1,0:T(8,128)(2,1)} %base_ref.3, bf16[72,4096]{1,0:T(8,128)(2,1)} %copy-done, bf16[72,4096]{1,0:T(8,128)(2,1)} %collective-permute-done.9.refs_1_, bf16[72,4096]{1,0:T(8,128)(2,1)} %copy-done.1, bf16[72,4096]{1,0:T(8,128)(2,1)} %copy-done.9), custom_call_target="tpu_custom_call" | custom-call | flops 603979776 | bytes 6701056 | tf_op jit(solution)/shard_map/base_keys/pallas_call | solution.py:122
  86.1 2.9 %all-to-all-done.1 = bf16[16,72,256]{2,1,0:T(8,128)(2,1)S(1)} async-done(((bf16[16,72,256]{2,1,0:T(8,128)(2,1)}), bf16[16,72,256]{2,1,0:T(8,128)(2,1)S(1)}, u32[]{:S(2)}, u32[]{:S(2)}) %all-to-all-start.1) | async-done | bytes 589856 | tf_op jit(solution)/shard_map/all_to_all | solution.py:530
  89.0 0.8 copy-done.7
  89.8 5.2 %attend_new.1 = (bf16[2,9,8,4096]{3,2,1,0:T(8,128)(2,1)}, bf16[2,9,8,256]{3,2,1,0:T(8,128)(2,1)}) custom-call(bf16[8,2,72,256]{3,2,1,0:T(8,128)(2,1)} %bitcast.24, f32[1,144,256]{2,1,0:T(8,128)} %base_keys.2.near_ref, f32[2,72,256]{2,1,0:T(8,128)} %base_keys.3.far_ref, bf16[9,2,256,128]{3,2,1,0:T(8,128)(2,1)} %get-tuple-element.30.qp_ref, ...), custom_call_target="tpu_custom_call" | custom-call | flops 603979776 | bytes 5898240 | tf_op jit(solution)/shard_map/attend_new/pallas_call | solution.py:384
  (17 shorter events, 0.0 us)
Async XLA Ops:
  0.6 19.7 %copy-start.6 = (s32[128]{0:T(128)S(1)}, s32[128]{0:T(128)}, u32[]{:S(2)}) copy-start(s32[128]{0:T(128)} %order_ref.1) | copy-start | bytes 1540
  2.0 16.3 %collective-permute-start.2 = (bf16[72,4096]{1,0:T(8,128)(2,1)S(1)}, bf16[72,4096]{1,0:T(8,128)(2,1)S(1)}, u32[]{:S(2)}, u32[]{:S(2)}) collective-permute-start(bf16[72,4096]{1,0:T(8,128)(2,1)S(1)} %get-tuple-element.38), channel_id=1, source_target_pairs={{0,2},{2,0},{1,3},{3,1},{4,6},{6,4},{5,7},{7,5},{8,10},{10,8},{9,1... | collective-permute-start | bytes 1769480 | tf_op jit(solution)/shard_map/ppermute | solution.py:469
  5.0 13.3 %collective-permute-start.1 = (bf16[72,4096]{1,0:T(8,128)(2,1)S(1)}, bf16[72,4096]{1,0:T(8,128)(2,1)S(1)}, u32[]{:S(2)}, u32[]{:S(2)}) collective-permute-start(bf16[72,4096]{1,0:T(8,128)(2,1)S(1)} %get-tuple-element.39.refs_0_), channel_id=1, source_target_pairs={{0,1},{1,0},{2,3},{3,2},{4,5},{5,4},{6,7},{7,6},{8,9},{9,8},{10,11... | collective-permute-start | bytes 1769480 | tf_op jit(solution)/shard_map/ppermute | solution.py:435
  18.3 4.4 %copy-start = (bf16[72,4096]{1,0:T(8,128)(2,1)}, bf16[72,4096]{1,0:T(8,128)(2,1)S(1)}, u32[]{:S(2)}) copy-start(bf16[72,4096]{1,0:T(8,128)(2,1)S(1)} %collective-permute-done.2.refs_2_.refs_0_) | copy-start | bytes 1769476
  18.3 2.0 %collective-permute-start.3 = (bf16[72,4096]{1,0:T(8,128)(2,1)S(1)}, bf16[72,4096]{1,0:T(8,128)(2,1)S(1)}, u32[]{:S(2)}, u32[]{:S(2)}) collective-permute-start(bf16[72,4096]{1,0:T(8,128)(2,1)S(1)} %collective-permute-done.2.refs_2_.refs_0_), channel_id=1, source_target_pairs={{0,1},{1,0},{2,3},{3,2},{4,5},{5,4},{6,7},{7,6},{8,9},{9,8},{10,11... | collective-permute-start | bytes 1769480 | tf_op jit(solution)/shard_map/ppermute | solution.py:435
  20.3 2.4 %copy-start.1 = (bf16[72,4096]{1,0:T(8,128)(2,1)}, bf16[72,4096]{1,0:T(8,128)(2,1)S(1)}, u32[]{:S(2)}) copy-start(bf16[72,4096]{1,0:T(8,128)(2,1)S(1)} %collective-permute-done.3.refs_3_.refs_2_) | copy-start | bytes 1769476
  22.8 6.3 %copy-start.8 = (bf16[512,1024]{1,0:T(8,128)(2,1)S(1)}, bf16[512,1024]{1,0:T(8,128)(2,1)}, u32[]{:S(2)}) copy-start(bf16[512,1024]{1,0:T(8,128)(2,1)} %param.17) | copy-start | bytes 3145732
  22.8 35.1 %all-to-all-start = ((bf16[8,72,1024]{2,1,0:T(8,128)(2,1)}), bf16[8,72,1024]{2,1,0:T(8,128)(2,1)S(1)}, u32[]{:S(2)}, u32[]{:S(2)}) async-start(bf16[8,72,1024]{2,1,0:T(8,128)(2,1)} %scatter_columns.1), calls=%async_computation | async-start | bytes 2359296 | tf_op jit(solution)/shard_map/all_to_all | solution.py:520
  29.0 11.2 %collective-permute-start.7 = (bf16[144,4096]{1,0:T(8,128)(2,1)}, bf16[144,4096]{1,0:T(8,128)(2,1)}, u32[]{:S(2)}, u32[]{:S(2)}) collective-permute-start(bf16[144,4096]{1,0:T(8,128)(2,1)} %bitcast.2.refs_0_), channel_id=1, source_target_pairs={{0,1},{1,0},{2,3},{3,2},{4,5},{5,4},{6,7},{7,6},{8,9},{9,8},{10,11... | collective-permute-start | bytes 3538952 | tf_op jit(solution)/shard_map/ppermute | solution.py:435
  30.1 15.5 %collective-permute-start.4 = (bf16[2,512,256]{2,1,0:T(8,128)(2,1)}, bf16[2,512,256]{2,1,0:T(8,128)(2,1)S(1)}, u32[]{:S(2)}, u32[]{:S(2)}) collective-permute-start(bf16[2,512,256]{2,1,0:T(8,128)(2,1)} %pad_maximum_fusion), channel_id=1, source_target_pairs={{0,1},{1,0},{2,3},{3,2},{4,5},{5,4},{6,7},{7,6},{8,9},{9,8},{10,11... | collective-permute-start | bytes 1572872 | tf_op jit(solution)/shard_map/ppermute | solution.py:486
  31.2 26.7 %collective-permute-start.5 = (bf16[2,512,256]{2,1,0:T(8,128)(2,1)S(1)}, bf16[2,512,256]{2,1,0:T(8,128)(2,1)S(1)}, u32[]{:S(2)}, u32[]{:S(2)}) collective-permute-start(bf16[2,512,256]{2,1,0:T(8,128)(2,1)S(1)} %pad_maximum_fusion.1.refs_1_), channel_id=1, source_target_pairs={{0,2},{1,3},{2,0},{3,1},{4,6},{5,7},{6,4},{7,5},{8,10},{9,11},{10,... | collective-permute-start | bytes 1572872 | tf_op jit(solution)/shard_map/ppermute | solution.py:486
  32.7 26.0 %collective-permute-start.6 = (bf16[2,512,256]{2,1,0:T(8,128)(2,1)}, bf16[2,512,256]{2,1,0:T(8,128)(2,1)S(1)}, u32[]{:S(2)}, u32[]{:S(2)}) collective-permute-start(bf16[2,512,256]{2,1,0:T(8,128)(2,1)} %pad_maximum_fusion), channel_id=1, source_target_pairs={{0,3},{1,2},{2,1},{3,0},{4,7},{5,6},{6,5},{7,4},{8,11},{9,10},{10,... | collective-permute-start | bytes 1572872 | tf_op jit(solution)/shard_map/ppermute | solution.py:486
  40.2 19.3 %copy-start.10 = (bf16[16,2]{0,1:T(2,128)(2,1)S(1)}, bf16[16,2]{0,1:T(2,128)(2,1)}, u32[]{:S(2)}) copy-start(bf16[16,2]{0,1:T(2,128)(2,1)} %param.18) | copy-start | bytes 196
  57.9 0.8 copy-start.4
  58.7 0.8 copy-start.2
  59.5 6.4 %collective-permute-start.8 = (bf16[576,1024]{1,0:T(8,128)(2,1)S(1)}, bf16[576,1024]{1,0:T(8,128)(2,1)S(1)}, u32[]{:S(2)}, u32[]{:S(2)}) collective-permute-start(bf16[576,1024]{1,0:T(8,128)(2,1)S(1)} %bitcast.22), channel_id=1, source_target_pairs={{0,1},{1,0},{2,3},{3,2},{4,5},{5,4},{6,7},{7,6},{8,9},{9,8},{10,11... | collective-permute-start | bytes 3538952 | tf_op jit(solution)/shard_map/ppermute | solution.py:435
  59.5 3.5 %collective-permute-start = (bf16[16,2]{0,1:T(2,128)(2,1)S(1)}, bf16[16,2]{0,1:T(2,128)(2,1)S(1)}, u32[]{:S(2)}, u32[]{:S(2)}) collective-permute-start(bf16[16,2]{0,1:T(2,128)(2,1)S(1)} %copy-done.10), channel_id=1, source_target_pairs={{0,2},{2,0},{1,3},{3,1},{4,6},{6,4},{5,7},{7,5},{8,10},{10,8},{9,1... | collective-permute-start | bytes 200 | tf_op jit(solution)/shard_map/ppermute | solution.py:489
  61.0 16.7 %collective-permute-start.9 = (bf16[72,4096]{1,0:T(8,128)(2,1)}, bf16[72,4096]{1,0:T(8,128)(2,1)}, u32[]{:S(2)}, u32[]{:S(2)}) collective-permute-start(bf16[72,4096]{1,0:T(8,128)(2,1)} %constant_dynamic-slice_fusion), channel_id=1, source_target_pairs={{0,2},{2,0},{1,3},{3,1},{4,6},{6,4},{5,7},{7,5},{8,10},{10,8},{9,1... | collective-permute-start | bytes 1769480 | tf_op jit(solution)/shard_map/ppermute | solution.py:508
  63.2 1.0 %copy-start.5 = (bf16[2,512,256]{2,1,0:T(8,128)(2,1)S(1)}, bf16[2,512,256]{2,1,0:T(8,128)(2,1)}, u32[]{:S(2)}) copy-start(bf16[2,512,256]{2,1,0:T(8,128)(2,1)} %copy-done.4) | copy-start | bytes 1572868
  64.2 1.7 %copy-start.3 = (bf16[2,512,256]{2,1,0:T(8,128)(2,1)S(1)}, bf16[2,512,256]{2,1,0:T(8,128)(2,1)}, u32[]{:S(2)}) copy-start(bf16[2,512,256]{2,1,0:T(8,128)(2,1)} %copy-done.2) | copy-start | bytes 1572868
  68.5 20.5 %all-to-all-start.1 = ((bf16[16,72,256]{2,1,0:T(8,128)(2,1)}), bf16[16,72,256]{2,1,0:T(8,128)(2,1)S(1)}, u32[]{:S(2)}, u32[]{:S(2)}) async-start(bf16[16,72,256]{2,1,0:T(8,128)(2,1)} %bitcast.11), calls=%async_computation.1 | async-start | bytes 1179648 | tf_op jit(solution)/shard_map/all_to_all | solution.py:530
  77.7 2.2 %collective-permute-start.10 = (bf16[72,4096]{1,0:T(8,128)(2,1)}, bf16[72,4096]{1,0:T(8,128)(2,1)S(1)}, u32[]{:S(2)}, u32[]{:S(2)}) collective-permute-start(bf16[72,4096]{1,0:T(8,128)(2,1)} %collective-permute-done.9.refs_1_), channel_id=1, source_target_pairs={{0,1},{1,0},{2,3},{3,2},{4,5},{5,4},{6,7},{7,6},{8,9},{9,8},{10,11... | collective-permute-start | bytes 1769480 | tf_op jit(solution)/shard_map/ppermute | solution.py:435
  79.9 0.8 copy-start.9
  89.0 0.8 copy-start.7

commit v2 on v1

--- a/solution.py
+++ b/solution.py
@@ -17,6 +17,8 @@
 RB = 8
 MIB = 1024 * 1024
 GRANT = 57 * MIB
+MIDDLE = 52 * MIB
+BESIDE = pl.CostEstimate(flops=0, bytes_accessed=1024, transcendentals=0)
 CONTRACT_LAST = (((1,), (1,)), ((), ()))
 CONTRACT_FIRST = (((0,), (0,)), ((), ()))
 
@@ -44,7 +46,10 @@
     core = lax.axis_index("core")
 
     def fetch(i):
-        return pltpu.make_async_copy(pieces[i], all_ref.at[i], sems.at[i])
+        piece = pieces[i]
+        if len(piece.shape) == 3:
+            piece = piece.at[x]
+        return pltpu.make_async_copy(piece, all_ref.at[i], sems.at[i])
 
     for i in range(len(pieces)):
         fetch(i).start()
@@ -68,7 +73,7 @@
 
 
 def scatter(order, pieces, nf, split):
-    rows, cols = pieces[0].shape
+    rows, cols = pieces[-1].shape
     width = len(pieces) * cols // nf // split
     return pl.pallas_call(
         functools.partial(scatter_kernel, len(pieces) // 2, split),
@@ -88,87 +93,121 @@
     )(order, *pieces)
 
 
-def base_kernel(nx, info_ref, base_ref, *refs):
-    pieces, (o_ref, held, sems) = refs[:-3], refs[-3:]
-    width = pieces[0].shape[1]
+def base_kernel(plan, info_ref, base_ref, *refs):
+    count = sum(len(targets) for targets in plan)
+    made = 1 + max(max(targets) for targets in plan)
+    pieces, outs, taken = refs[:count], refs[count : count + made], refs[count + made : -2]
+    held, sems = refs[-2:]
     depth = held.shape[1]
+    width = taken[0].shape[1]
     chunks = width // depth
+    total = held.shape[0]
+
+    def take(i):
+        return pltpu.make_async_copy(pieces[i], taken[i], sems.at[total + i])
 
     def fetch(n):
         row = pl.multiple_of(info_ref[n // chunks] * width + n % chunks * depth, depth)
         return pltpu.make_async_copy(base_ref.at[pl.ds(row, depth), :], held.at[n], sems.at[n])
 
-    for n in range(held.shape[0]):
-        fetch(n).start()
-    total = jnp.zeros((o_ref.shape[0] * o_ref.shape[1], o_ref.shape[2]), jnp.float32)
-    for n in range(held.shape[0]):
-        lanes = slice(n % chunks * depth, (n % chunks + 1) * depth)
-        first = n // chunks * nx
-        part = jnp.concatenate(
-            [pieces[first + r][:, lanes].astype(jnp.float32) for r in range(nx)], axis=0
-        ).astype(jnp.bfloat16)
-        fetch(n).wait()
-        total = total + jnp.dot(part, held[n], preferred_element_type=jnp.float32)
-    o_ref[...] = total.reshape(o_ref.shape)
-
-
-def base_product(owners, pieces, base, nx):
-    rows, width = pieces[0].shape
+    firsts = [sum(len(targets) for targets in plan[:q]) for q in range(len(plan))]
+    for q, targets in enumerate(plan):
+        for r in range(len(targets)):
+            take(firsts[q] + r).start()
+        for j in range(chunks):
+            fetch(q * chunks + j).start()
+    sums = [jnp.zeros(o_ref.shape, jnp.float32) for o_ref in outs]
+    for q, targets in enumerate(plan):
+        for r in range(len(targets)):
+            take(firsts[q] + r).wait()
+        for j in range(chunks):
+            n = q * chunks + j
+            fetch(n).wait()
+            for r, target in enumerate(targets):
+                part = taken[firsts[q] + r][:, j * depth : (j + 1) * depth]
+                sums[target] = sums[target] + jnp.dot(
+                    part, held[n], preferred_element_type=jnp.float32
+                )
+    for o_ref, value in zip(outs, sums):
+        o_ref[...] = value
+
+
+def base_product(owners, plan, pieces, base, grant):
+    width = pieces[0].shape[1]
     cols = base.shape[1]
-    quarters = len(pieces) // nx
     depth = min(width, 1024)
-    count = quarters * width // depth
-    size = nx * rows * cols
+    count = len(plan) * width // depth
+    rows = {}
+    for target, piece in zip([t for targets in plan for t in targets], pieces):
+        rows[target] = piece.shape[0]
     return pl.pallas_call(
-        functools.partial(base_kernel, nx),
-        out_shape=jax.ShapeDtypeStruct((nx, rows, cols), jnp.float32),
-        in_specs=[
-            pl.BlockSpec(memory_space=pltpu.SMEM),
-            pl.BlockSpec(memory_space=pl.ANY),
-        ]
-        + [pl.BlockSpec(memory_space=pltpu.VMEM)] * len(pieces),
-        out_specs=pl.BlockSpec(memory_space=pltpu.VMEM),
-        scratch_shapes=[
+        functools.partial(base_kernel, plan),
+        out_shape=tuple(
+            jax.ShapeDtypeStruct((rows[t], cols), jnp.float32) for t in range(len(rows))
+        ),
+        in_specs=[pl.BlockSpec(memory_space=pltpu.SMEM)]
+        + [pl.BlockSpec(memory_space=pl.ANY)] * (1 + len(pieces)),
+        out_specs=(pl.BlockSpec(memory_space=pltpu.VMEM),) * len(rows),
+        scratch_shapes=[pltpu.VMEM(piece.shape, jnp.bfloat16) for piece in pieces]
+        + [
             pltpu.VMEM((count, depth, cols), jnp.bfloat16),
-            pltpu.SemaphoreType.DMA((count,)),
+            pltpu.SemaphoreType.DMA((count + len(pieces),)),
         ],
-        compiler_params=pltpu.CompilerParams(vmem_limit_bytes=GRANT),
-        cost_estimate=pl.CostEstimate(
-            flops=2 * size * width * quarters,
-            bytes_accessed=2 * quarters * width * (cols + nx * rows) + 4 * size,
-            transcendentals=0,
-        ),
+        compiler_params=pltpu.CompilerParams(vmem_limit_bytes=grant),
+        cost_estimate=BESIDE,
         name="base_keys",
     )(owners, base, *pieces)
 
 
-def product_kernel(spread, part, step, s_ref, *refs):
-    o_ref, scaled_ref = refs[-2:]
+def scale_kernel(nx, shifts, *refs):
+    scales, refs = refs[:nx], refs[nx:]
+    pieces, outs = refs[: len(shifts)], refs[len(shifts) :]
+    own, cols = pieces[0].shape[1:]
+    x = lax.axis_index("tx")
+    core = lax.axis_index("core")
+    for (d, e), piece, o_ref in zip(shifts, pieces, outs):
+        first = (lax.rem(x + d, nx) * 2 + lax.bitwise_xor(core, e)) * (own // BLK)
+        for q in range(nx):
+            source = lax.rem(q + nx - x, nx)
+            for b in range(own // BLK):
+                rows = slice(b * BLK, (b + 1) * BLK)
+                for c in range(cols // BLK):
+                    lanes = slice(c * BLK, (c + 1) * BLK)
+                    factor = scales[0][first + b, c]
+                    for n in range(1, nx):
+                        factor = jnp.where(source == n, scales[n][first + b, c], factor)
+                    values = piece[q, rows, lanes].astype(jnp.float32) * factor
+                    o_ref[q, rows, lanes] = values.astype(jnp.bfloat16)
+
+
+def scale_rows(scales, shifts, pieces):
+    size = len(pieces) * pieces[0].size
+    return pl.pallas_call(
+        functools.partial(scale_kernel, pieces[0].shape[0], shifts),
+        out_shape=tuple(jax.ShapeDtypeStruct(p.shape, jnp.bfloat16) for p in pieces),
+        in_specs=[pl.BlockSpec(memory_space=pltpu.SMEM)] * len(scales)
+        + [pl.BlockSpec(memory_space=pltpu.VMEM)] * len(pieces),
+        out_specs=(pl.BlockSpec(memory_space=pltpu.VMEM),) * len(pieces),
+        compiler_params=params(4 * size),
+        cost_estimate=BESIDE,
+        name="scale_rows",
+    )(*scales, *pieces)
+
+
+def product_kernel(spread, step, *refs):
+    o_ref = refs[-1]
     x_ref, ws = refs[0], refs[1 : 1 + spread]
-    earlier = refs[1 + spread : -2]
+    earlier = refs[1 + spread : -1]
     nx, own, cols = ws[0].shape
     x = lax.axis_index("tx")
-    core = lax.axis_index("core")
     for q in range(nx):
         total = earlier[0][q] if earlier else jnp.zeros((x_ref.shape[0], cols), jnp.float32)
-        source = lax.rem(q + nx - x, nx)
         for d, w_ref in enumerate(ws):
-            w = w_ref[q]
             at = 0
             if spread > 1:
-                chip = lax.rem(x + d, nx)
-                at = pl.multiple_of(chip * own, BLK)
-                first = (chip * 2 + lax.bitwise_xor(core, part)) * (own // BLK)
-                for b in range(own // BLK):
-                    rows = slice(b * BLK, (b + 1) * BLK)
-                    for c in range(cols // BLK):
-                        lanes = slice(c * BLK, (c + 1) * BLK)
-                        values = w_ref[q, rows, lanes].astype(jnp.float32)
-                        values = values * s_ref[source, first + b, c]
-                        scaled_ref[q, d, rows, lanes] = values.astype(jnp.bfloat16)
-                w = scaled_ref[q, d]
+                at = pl.multiple_of(lax.rem(x + d, nx) * own, BLK)
             total = total + jnp.dot(
-                x_ref[:, pl.ds(at, own)], w, preferred_element_type=jnp.float32
+                x_ref[:, pl.ds(at, own)], w_ref[q], preferred_element_type=jnp.float32
             )
         if step == "last":
             nf, _, rows, _ = o_ref.shape
@@ -177,9 +216,9 @@
             o_ref[q] = total
 
 
-def product(scales, x, ws, nf, part=0, earlier=None, last=True):
+def product(x, ws, nf, earlier=None, last=True):
     total, depth = x.shape
-    nx, own, cols = ws[0].shape
+    nx, _, cols = ws[0].shape
     rows = total // nf
     made = nx * total * cols
     read = total * depth + len(ws) * ws[0].size
@@ -188,20 +227,18 @@
     if last:
         out = jax.ShapeDtypeStruct((nf, nx, rows, cols), jnp.bfloat16)
     return pl.pallas_call(
-        functools.partial(product_kernel, len(ws), part, "last" if last else "first"),
+        functools.partial(product_kernel, len(ws), "last" if last else "first"),
         out_shape=out,
-        in_specs=[pl.BlockSpec(memory_space=pltpu.SMEM)]
-        + [pl.BlockSpec(memory_space=pltpu.VMEM)] * (1 + len(ws) + len(before)),
+        in_specs=[pl.BlockSpec(memory_space=pltpu.VMEM)] * (1 + len(ws) + len(before)),
         out_specs=pl.BlockSpec(memory_space=pltpu.VMEM),
-        scratch_shapes=[pltpu.VMEM((nx, len(ws), own, cols), jnp.bfloat16)],
-        compiler_params=params(4 * read + 8 * made),
+        compiler_params=params(2 * read + 8 * made),
         cost_estimate=pl.CostEstimate(
             flops=2 * made * depth,
             bytes_accessed=2 * read + 6 * made,
             transcendentals=0,
         ),
         name="partial_keys",
-    )(scales, x, *ws, *before)
+    )(x, *ws, *before)
 
 
 def cached_kernel(len_ref, q_ref, ck_ref, cv_ref, qp_ref, acc_ref, ml_ref):
@@ -264,7 +301,6 @@
     cap, cols = cache_keys.shape[1:]
     heads = cols // HD
     many = steps * GROUP * RB
-    scores = batches * heads * many * RB * cap
     n = taken_at_once(batches)
     return pl.pallas_call(
         cached_kernel,
@@ -285,17 +321,14 @@
             pl.BlockSpec((n, heads, HD, many), lambda i: (i, 0, 0, 0)),
             pl.BlockSpec((n, heads, 2, many), lambda i: (i, 0, 0, 0)),
         ),
-        compiler_params=pltpu.CompilerParams(vmem_limit_bytes=GRANT),
-        cost_estimate=pl.CostEstimate(
-            flops=4 * scores * HD,
-            bytes_accessed=4 * cache_keys.size + 8 * queries.size,
-            transcendentals=scores,
-        ),
+        compiler_params=pltpu.CompilerParams(vmem_limit_bytes=MIDDLE),
+        cost_estimate=BESIDE,
         name="attend_cached",
     )(lengths, queries, cache_keys, cache_values)
 
 
-def merge_kernel(nx, parts_ref, near_ref, far_ref, qp_ref, acc_ref, ml_ref, nv_ref, o_ref, nk_ref, held, eye):
+def merge_kernel(nx, parts_ref, near_ref, far_ref, *refs):
+    late_refs, (qp_ref, acc_ref, ml_ref, nv_ref, o_ref, nk_ref, held, eye) = refs[: nx - 1], refs[nx - 1 :]
     step = pl.program_id(0)
     steps, batches = nk_ref.shape[0], nk_ref.shape[1]
     taken, heads = acc_ref.shape[:2]
@@ -310,7 +343,11 @@
                 g = first_group(x, steps * batches, nx) + k
                 rows = slice(k * RB, (k + 1) * RB)
                 at = lax.rem(x + nx - me, nx)
-                total = near_ref[0, g * RB : (g + 1) * RB, :] + far_ref[at, rows, :]
+                total = near_ref[g * RB : (g + 1) * RB, :]
+                far = far_ref[rows, :]
+                for r, late_ref in enumerate(late_refs):
+                    far = jnp.where(at == r + 1, late_ref[rows, :], far)
+                total = total + far
                 for f in range(parts_ref.shape[0]):
                     total = total + parts_ref[f, x, rows, :].astype(jnp.float32)
                 rounded = total.astype(jnp.bfloat16)
@@ -376,7 +413,7 @@
                 ]
 
 
-def merge(parts, near, far, packed, sums, tops, new_values):
+def merge(parts, near, far, late, packed, sums, tops, new_values):
     batches, heads, many, _ = packed.shape
     steps, _, _, cols = new_values.shape
     width = many // steps // RB * heads * HD
@@ -390,8 +427,7 @@
         ),
         in_specs=[
             pl.BlockSpec(parts.shape, lambda i: (0, 0, 0, 0)),
-            pl.BlockSpec(near.shape, lambda i: (0, 0, 0)),
-            pl.BlockSpec(far.shape, lambda i: (0, 0, 0)),
+            *(pl.BlockSpec(part.shape, lambda i: (0, 0)) for part in (near, far, *late)),
             pl.BlockSpec((n, heads, many, HD), lambda i: (i, 0, 0, 0)),
             pl.BlockSpec((n, heads, HD, many), lambda i: (i, 0, 0, 0)),
             pl.BlockSpec((n, heads, 2, many), lambda i: (i, 0, 0, 0)),
@@ -412,7 +448,7 @@
             transcendentals=packed.size // 8,
         ),
         name="attend_new",
-    )(parts, near, far, packed, sums, tops, new_values)
+    )(parts, near, far, *late, packed, sums, tops, new_values)
 
 
 def shift_of(nx, d):
@@ -459,17 +495,6 @@
     own = delta_values.shape[0]
     split = 2 if own % BLK == 0 else 1
 
-    flat = hidden.reshape(steps * rows, width)
-    slices = []
-    for d in range(nx):
-        start = first_group(lax.rem(x + d, nx), steps * batches, nx) * RB
-        slices.append(part_of(flat, start, count * RB, 0))
-    held = [[None] * nx for _ in range(nx)]
-    for d in range(nx):
-        came = lax.ppermute(slices[-d % nx], "tx", shift_of(nx, d)) if d else slices[0]
-        held[d][0] = (came, swap(came))
-    mine = scatter(block_order, [p for d in range(nx) for p in held[d][0]], nf, split)
-
     def to_shift(d, e):
         return [(s * 2 + c, (s - d) % nx * 2 + (c ^ e)) for s in range(nx) for c in range(2)]
 
@@ -480,16 +505,42 @@
         sent.append(
             jnp.stack([part_of(delta_values, (2 * q + to) * cols, cols, 1) for q in range(nx)])
         )
+    scales = [delta_scales.astype(jnp.float32)]
+    scales += [lax.ppermute(scales[0], "tx", shift_of(nx, d)) for d in range(1, nx)]
+
+    flat = hidden.reshape(steps * rows, width)
+    whole_rows = swap(flat)
+
+    def rows_of(array, d):
+        start = first_group(lax.rem(x + d, nx), steps * batches, nx) * RB
+        return part_of(array, start, count * RB, 0)
+
+    held = [[None] * nx for _ in range(nx)]
+    for d in range(1, nx):
+        came = lax.ppermute(rows_of(flat, (-d) % nx), "tx", shift_of(nx, d))
+        ready = [came]
+        for early in (*sent, scales[d]):
+            ready = after(ready, early)
+        held[d][0] = (came, swap(ready[0]))
+    if nx == steps and count * RB == rows:
+        pieces = [hidden, whole_rows.reshape(hidden.shape)]
+    else:
+        pieces = [rows_of(flat, 0), rows_of(whole_rows, 0)]
+    pieces += [p for d in range(1, nx) for p in held[d][0]]
+    mine = scatter(block_order, pieces, nf, split)
+
     behind = after(sent, held[-1][0][0])
     ws = [sent[0]]
     for d, e in shifts[1:]:
         ws.append(lax.ppermute((behind if d else sent)[e], ("tx", "core"), to_shift(d, e)))
     arrived = ws[1:]
-    scales = [delta_scales]
-    scales += [lax.ppermute(delta_scales, "tx", shift_of(nx, d)) for d in range(1, nx)]
-    scales = jnp.stack(scales).astype(jnp.float32)
+    if split > 1:
+        ws = [
+            *scale_rows(scales, shifts[:2], ws[:2]),
+            *scale_rows(scales, shifts[2:], ws[2:]),
+        ]
     if split == 1:
-        by_chip = jnp.repeat(jnp.roll(scales, x, axis=0), BLK, axis=2)
+        by_chip = jnp.repeat(jnp.roll(jnp.stack(scales), x, axis=0), BLK, axis=2)
         whole = jnp.zeros((nx, depth, cols), jnp.bfloat16)
         for (d, e), piece in zip(shifts, ws):
             at = (lax.rem(x + d, nx) * 2 + lax.bitwise_xor(core, e)) * own
@@ -509,31 +560,34 @@
             held[d][r] = (came, swap(came))
 
     owners = [lax.rem(x + d, nx) * 2 + lax.bitwise_xor(core, e) for d, e in shifts]
-    first, then = after([jnp.stack(owners[:2]), lengths], mine)
-    for piece in late:
+    owners = jnp.stack(owners)
+    first, then = after([owners, lengths], mine)
+    for piece in (*late, *ws[:1]):
         (first,) = after([first], piece)
-    near = base_product(first, [flat, swap(soon)], base_weight, 1)
+    early = [held[d][0][e] for d in range(1, nx) for e in range(2)]
+    plan = ((0,),) * 2 + ((1,),) * len(early)
+    near, far = base_product(first, plan, [flat, whole_rows, *early], base_weight, MIDDLE)
     shape = (steps, batches, RB)
     share = cached(
         then, queries.reshape(shape + queries.shape[2:]), cache_keys, cache_values
     )
     mine = lax.all_to_all(mine, "fsdp", 0, 0, tiled=True)
     xs = [mine.reshape(nf * count * RB, depth // split)]
-    for earlier in (*arrived, near, share[0]):
+    for earlier in (*arrived, near, far, share[0]):
         xs = after(xs, earlier)
     if split > 1:
         xs.append(swap(xs[0]))
-        partial = product(scales, xs[0], ws[0::2], nf, 0, last=False)
-        partial = product(scales, xs[1], ws[1::2], nf, 1, partial)
+        partial = product(xs[0], ws[0::2], nf, last=False)
+        partial = product(xs[1], ws[1::2], nf, partial)
     else:
-        partial = product(scales, xs[0], ws, nf)
+        partial = product(xs[0], ws, nf)
     parts = lax.all_to_all(
         partial.reshape(nf * nx, count * RB, cols), ("fsdp", "tx"), 0, 0, tiled=True
     ).reshape(nf, nx, count * RB, cols)
-    (rest,) = after([jnp.stack(owners[2:])], partial)
-    ordered = [held[d][r][e] for d in range(1, nx) for e in range(2) for r in range(nx)]
-    far = base_product(rest, ordered, base_weight, nx)
-    attended, new_keys = merge(parts, near, far, *share, new_values.reshape(shape + (cols,)))
+    remaining = [held[d][r][e] for d in range(1, nx) for e in range(2) for r in range(1, nx)]
+    plan = (tuple(range(nx - 1)),) * (2 * (nx - 1))
+    late = base_product(after([owners[2:]], partial)[0], plan, remaining, base_weight, GRANT)
+    attended, new_keys = merge(parts, near, far, late, *share, new_values.reshape(shape + (cols,)))
     return (attended.reshape(queries.shape), new_keys.reshape(steps, rows, cols))
 
 

time: 95.6 us -> 91.9 us (0.961)
  waiting for transfers between devices: 38.2 us -> 32.8 us
  local copies, waits for them, and re-layouts: 7.83 us -> 11 us
  starting transfers between devices: 18 us -> 16.4 us
    ppermute x1, waiting for transfers between devices: 4.51 us -> 10.9 us  [per_device(): came = lax.ppermute(piece, 'tx', shift_of(nx, d))]
    ppermute x2, waiting for transfers between devices: 14.8 us -> 10.3 us  [the longest x1 10.2 us: per_device(): came = lax.ppermute(rows_of(flat, -d % nx), 'tx', shift_of(nx, d))]
    all_to_all x1, waiting for transfers between devices: 12.3 us -> 7.93 us  [per_device(): mine = lax.all_to_all(mine, 'fsdp', 0, 0, tiled=True)]
    unnamed x22 -> x35, local copies, waits for them, and re-layouts: 4.29 us -> 7.64 us
    all_to_all x1, waiting for transfers between devices: 2.91 us -> 0.01 us  [per_device(): lax.all_to_all(partial.reshape(nf * nx, count * RB, cols), ('fsdp', 'tx')...]
    ppermute x2, starting transfers between devices: 4.5 us -> 3.15 us  [the longest x1 3 us: per_device(): came = lax.ppermute(rows_of(flat, -d % nx), 'tx', shift_of(nx, d))]
    dynamic_slice x2, local copies, waits for them, and re-layouts: 3.28 us -> 2.09 us  [part_of(): return lax.dynamic_slice(array, starts, sizes, allow_negative_indices=False)]
    another operation x1, local copies, waits for them, and re-layouts: 0.15 us -> 1.27 us  [per_device(): jnp.stack([part_of(delta_values, (2 * q + to) * cols, cols, 1) for q in r...]
  transfers between devices with their start and end apart: 13 -> 12, of which waited for: 7 -> 7; matrix products, arithmetic and copies ran while one was open for 4% -> 5% of each run, Pallas kernels for 22% -> 22%
where the time goes in v2:
time: 91.9 us; the launch traced here: 91.3 us
  waiting for transfers between devices  32.8 us (36%)
  Pallas kernels  27.9 us (30%)
  starting transfers between devices  16.4 us (18%)
  local copies, waits for them, and re-layouts  11 us (12%)
  other arithmetic  2.45 us (3%)
    ppermute x1, waiting for transfers between devices, per_device(): came = lax.ppermute(piece, 'tx', shift_of(nx, d))  10.9 us
    ppermute x1, waiting for transfers between devices, per_device(): came = lax.ppermute(rows_of(flat, -d % nx), 'tx', shift_of(nx, d))  10.2 us
    pallas_call x2, Pallas kernels, base_product(): pl.pallas_call(functools.partial(base_kernel, plan), out_shape=tuple((jax...  9.66 us
    all_to_all x1, waiting for transfers between devices, per_device(): mine = lax.all_to_all(mine, 'fsdp', 0, 0, tiled=True)  7.93 us
    unnamed x35, local copies, waits for them, and re-layouts  7.64 us
    all_to_all x1, starting transfers between devices, per_device(): mine = lax.all_to_all(mine, 'fsdp', 0, 0, tiled=True)  6.09 us
    pallas_call x1, Pallas kernels, cached(): pl.pallas_call(cached_kernel, grid=(batches // n,), out_shape=(jax.ShapeD...  5.44 us
    pallas_call x1, Pallas kernels, merge(): pl.pallas_call(functools.partial(merge_kernel, parts.shape[1]), grid=(bat...  5.24 us
  transfers between devices with their start and end apart: 12, of which 7 were waited for; matrix products, arithmetic and copies ran while one was open for 5% of the time, Pallas kernels for 22%

profile of v2, /device:TPU:0, one launch (start us, length us, event | category | flops | bytes accessed | tf_op | source)
XLA Modules:
  0.0 91.3 jit_solution(1776240299215924274)
XLA Ops:
  0.6 0.0 copy-start
  0.7 1.2 %constant_dynamic-slice_fusion.1 = bf16[72,4096]{1,0:T(8,128)(2,1)S(1)} fusion(bf16[144,4096]{1,0:T(8,128)(2,1)} %bitcast.21, s32[]{:T(128)S(6)} %mul.28), kind=kLoop, calls=%fused_computation.7 | loop fusion | bytes 1179652 | tf_op jit(solution)/shard_map/dynamic_slice | solution.py:463
  1.9 3.0 %collective-permute-start.1 = (bf16[72,4096]{1,0:T(8,128)(2,1)S(1)}, bf16[72,4096]{1,0:T(8,128)(2,1)S(1)}, u32[]{:S(2)}, u32[]{:S(2)}) collective-permute-start(bf16[72,4096]{1,0:T(8,128)(2,1)S(1)} %constant_dynamic-slice_fusion.1), channel_id=1, source_target_pairs={{0,2},{2,0},{1,3},{3,1},{4,6},{6,4},{5,7},{7,5},{8,10},{10,8},{9,1... | collective-permute-start | bytes 1769480 | tf_op jit(solution)/shard_map/ppermute | solution.py:520
  4.9 0.1 copy.12
  5.0 0.2 collective-permute-start.2
  5.1 1.3 %dynamic-slice_bitcast_fusion.1 = (bf16[1,512,256]{2,1,0:T(8,128)(2,1)S(1)}, bf16[1,512,256]{2,1,0:T(8,128)(2,1)S(1)}, bf16[1,512,256]{2,1,0:T(8,128)(2,1)S(1)}, bf16[1,512,256]{2,1,0:T(8,128)(2,1)S(1)}) fusion(bf16[512,1024]{1,0:T(8,128)(2,1)} %param.17, s32[]{:T(128)S(6)} %mul.31, s32[]{:T(128)S(6)} %mul.30, s32[]{:T(128)S(6)} %mul.29, s32[]{:T(128)S(6)} %mul.32), kind=kLoop, calls=%fused_computation.3 | loop fusion | bytes 2097168 | tf_op jit(solution)/shard_map/stack | solution.py:506
  6.4 0.0 copy-start.11
  6.4 0.8 pad_maximum_fusion.1
  7.2 0.9 pad_maximum_fusion.refs_2_
  8.1 10.2 %collective-permute-done.1.refs_2_ = bf16[72,4096]{1,0:T(8,128)(2,1)S(1)} collective-permute-done((bf16[72,4096]{1,0:T(8,128)(2,1)S(1)}, bf16[72,4096]{1,0:T(8,128)(2,1)S(1)}, u32[]{:S(2)}, u32[]{:S(2)}) %collective-permute-start.1) | collective-permute-done | bytes 589856 | tf_op jit(solution)/shard_map/ppermute | solution.py:520
  18.3 0.1 collective-permute-done.2.refs_1_
  18.4 0.0 collective-permute-start.3
  18.4 2.0 %collective-permute-done.3.refs_3_ = bf16[72,4096]{1,0:T(8,128)(2,1)S(1)} collective-permute-done((bf16[72,4096]{1,0:T(8,128)(2,1)S(1)}, bf16[72,4096]{1,0:T(8,128)(2,1)S(1)}, u32[]{:S(2)}, u32[]{:S(2)}) %collective-permute-start.3) | collective-permute-done | bytes 589856 | tf_op jit(solution)/shard_map/ppermute | solution.py:471
  20.4 0.0 collective-permute-done.refs_1_
  20.4 2.4 %scatter_columns.1 = bf16[8,72,1024]{2,1,0:T(8,128)(2,1)} custom-call(s32[128]{0:T(128)S(1)} %copy-done.11, bf16[2,72,4096]{2,1,0:T(8,128)(2,1)S(1)} %copy-done, bf16[2,72,4096]{2,1,0:T(8,128)(2,1)S(1)} %bitcast.25, bf16[72,4096]{1,0:T(8,128)(2,1)S(1)} %collective-permute-done.1.refs_2_, bf16[72,4096]{1,0:T(8,128)(2,1)S(1)} %collective-permute-done.3.refs_3_), custom_call_target="tpu_custom_call" | custom-call | bytes 3538944 | tf_op jit(solution)/shard_map/scatter_columns/pallas_call | solution.py:78
  22.8 6.1 %all-to-all-start = ((bf16[8,72,1024]{2,1,0:T(8,128)(2,1)}), bf16[8,72,1024]{2,1,0:T(8,128)(2,1)S(1)}, u32[]{:S(2)}, u32[]{:S(2)}) async-start(bf16[8,72,1024]{2,1,0:T(8,128)(2,1)} %scatter_columns.1), calls=%async_computation | async-start | bytes 2359296 | tf_op jit(solution)/shard_map/all_to_all | solution.py:574
  28.9 0.0 collective-permute-start.4
  29.0 0.0 copy-start.12
  29.0 1.6 %collective-permute-start.5 = (bf16[2,512,256]{2,1,0:T(8,128)(2,1)}, bf16[2,512,256]{2,1,0:T(8,128)(2,1)}, u32[]{:S(2)}, u32[]{:S(2)}) collective-permute-start(bf16[2,512,256]{2,1,0:T(8,128)(2,1)} %pad_maximum_fusion.refs_2_), channel_id=1, source_target_pairs={{0,2},{1,3},{2,0},{3,1},{4,6},{5,7},{6,4},{7,5},{8,10},{9,11},{10,... | collective-permute-start | bytes 1572872 | tf_op jit(solution)/shard_map/ppermute | solution.py:535
  30.5 0.3 collective-permute-start.6
  30.8 0.1 pad_add_fusion.info_ref
  30.9 0.3 collective-permute-done.4.refs_3_
  31.2 1.0 %copy-done.2 = bf16[2,512,256]{2,1,0:T(8,128)(2,1)S(1)} copy-done((bf16[2,512,256]{2,1,0:T(8,128)(2,1)S(1)}, bf16[2,512,256]{2,1,0:T(8,128)(2,1)}, u32[]{:S(2)}) %copy-start.2) | copy-done | bytes 524312
  32.2 1.3 %scale_rows.2 = (bf16[2,512,256]{2,1,0:T(8,128)(2,1)S(1)}, bf16[2,512,256]{2,1,0:T(8,128)(2,1)S(1)}) custom-call(f32[16,2]{1,0:T(8,128)S(1)} %convert_element_type.3.refs_0_, f32[16,2]{1,0:T(8,128)S(1)} %collective-permute-done.2.refs_1_, bf16[2,512,256]{2,1,0:T(8,128)(2,1)S(1)} %copy-done.2, bf16[2,512,256]{2,1,0:T(8,128)(2,1)} %collective-permute-done.4.refs_3_), custom_call_target="tpu_custom_call" | custom-call | bytes 1024 | tf_op jit(solution)/shard_map/scale_rows/pallas_call | solution.py:185
  33.5 0.8 copy-done.4
  34.4 0.8 copy-done.6
  35.2 0.9 constant_dynamic-slice_fusion
  36.1 5.4 %attend_cached.1 = (bf16[9,2,256,128]{3,2,1,0:T(8,128)(2,1)S(1)}, f32[9,2,128,256]{3,2,1,0:T(8,128)}, f32[9,2,2,256]{3,2,1,0:T(2,128)S(1)}) custom-call(s32[72]{0:T(128)S(1)} %copy-done.12, bf16[2,9,8,4096]{3,2,1,0:T(8,128)(2,1)} %bitcast.29, bf16[72,32,256]{2,1,0:T(8,128)(2,1)} %ck_ref.1, bf16[72,32,256]{2,1,0:T(8,128)(2,1)} %cv_ref.1), custom_call_target="tpu_custom_call" | custom-call | bytes 1024 | tf_op jit(solution)/shard_map/attend_cached/pallas_call | solution.py:305
  41.5 1.0 %copy-done.3 = bf16[9,2,256,128]{3,2,1,0:T(8,128)(2,1)} copy-done((bf16[9,2,256,128]{3,2,1,0:T(8,128)(2,1)}, bf16[9,2,256,128]{3,2,1,0:T(8,128)(2,1)S(1)}, u32[]{:S(2)}) %copy-start.3) | copy-done | bytes 1179672
  42.5 0.6 copy-done.10
  43.2 5.4 %base_keys.2 = (f32[144,256]{1,0:T(8,128)S(1)}, f32[72,256]{1,0:T(8,128)S(1)}) custom-call(s32[4]{0:T(128)S(1)} %pad_add_fusion.info_ref, bf16[16384,256]{1,0:T(8,128)(2,1)} %base_ref.3, bf16[144,4096]{1,0:T(8,128)(2,1)} %bitcast.22, bf16[144,4096]{1,0:T(8,128)(2,1)} %copy-done.1, bf16[72,4096]{1,0:T(8,128)(2,1)S(1)} %collective-permute-done.1.refs_2_, ...), custom_call_target="tpu_custom_call" | custom-call | bytes 1024 | tf_op jit(solution)/shard_map/base_keys/pallas_call | solution.py:143
  48.6 0.7 copy-done.8
  49.2 0.6 copy-done.9
  49.9 7.9 %all-to-all-done = bf16[8,72,1024]{2,1,0:T(8,128)(2,1)S(1)} async-done(((bf16[8,72,1024]{2,1,0:T(8,128)(2,1)}), bf16[8,72,1024]{2,1,0:T(8,128)(2,1)S(1)}, u32[]{:S(2)}, u32[]{:S(2)}) %all-to-all-start) | async-done | bytes 1179680 | tf_op jit(solution)/shard_map/all_to_all | solution.py:574
  57.8 0.0 collective-permute-done.5.refs_2_
  57.8 1.4 %scale_rows.3 = (bf16[2,512,256]{2,1,0:T(8,128)(2,1)S(1)}, bf16[2,512,256]{2,1,0:T(8,128)(2,1)S(1)}) custom-call(f32[16,2]{1,0:T(8,128)S(1)} %convert_element_type.3.refs_0_, f32[16,2]{1,0:T(8,128)S(1)} %collective-permute-done.2.refs_1_, bf16[2,512,256]{2,1,0:T(8,128)(2,1)} %collective-permute-done.5.refs_2_, ...), custom_call_target="tpu_custom_call" | custom-call | bytes 1024 | tf_op jit(solution)/shard_map/scale_rows/pallas_call | solution.py:185
  59.3 1.6 %collective-permute-start.8 = (bf16[72,4096]{1,0:T(8,128)(2,1)}, bf16[72,4096]{1,0:T(8,128)(2,1)S(1)}, u32[]{:S(2)}, u32[]{:S(2)}) collective-permute-start(bf16[72,4096]{1,0:T(8,128)(2,1)} %constant_dynamic-slice_fusion), channel_id=1, source_target_pairs={{0,2},{2,0},{1,3},{3,1},{4,6},{6,4},{5,7},{7,5},{8,10},{10,8},{9,1... | collective-permute-start | bytes 1769480 | tf_op jit(solution)/shard_map/ppermute | solution.py:559
  60.8 0.8 partial_keys.2.refs_3_
  61.6 0.2 copy-done.5
  61.9 1.6 %partial_keys.3 = bf16[8,2,72,256]{3,2,1,0:T(8,128)(2,1)} custom-call(bf16[576,1024]{1,0:T(8,128)(2,1)S(1)} %collective-permute-done.7.refs_0_, bf16[2,512,256]{2,1,0:T(8,128)(2,1)S(1)} %copy-done.5, bf16[2,512,256]{2,1,0:T(8,128)(2,1)S(1)} %get-tuple-element.52.refs_2_, f32[2,576,256]{2,1,0:T(8,128)S(1)} %partial_keys.2.refs_3_), custom_call_target="tpu_custom_call" | custom-call | flops 603979776 | bytes 3997696 | tf_op jit(solution)/shard_map/partial_keys/pallas_call | solution.py:229
  63.5 3.8 %all-to-all-start.1 = ((bf16[16,72,256]{2,1,0:T(8,128)(2,1)}), bf16[16,72,256]{2,1,0:T(8,128)(2,1)S(1)}, u32[]{:S(2)}, u32[]{:S(2)}) async-start(bf16[16,72,256]{2,1,0:T(8,128)(2,1)} %bitcast.12), calls=%async_computation.1 | async-start | bytes 1179648 | tf_op jit(solution)/shard_map/all_to_all | solution.py:584
  67.2 10.9 %collective-permute-done.8.refs_0_ = bf16[72,4096]{1,0:T(8,128)(2,1)S(1)} collective-permute-done((bf16[72,4096]{1,0:T(8,128)(2,1)}, bf16[72,4096]{1,0:T(8,128)(2,1)S(1)}, u32[]{:S(2)}, u32[]{:S(2)}) %collective-permute-start.8) | collective-permute-done | bytes 589856 | tf_op jit(solution)/shard_map/ppermute | solution.py:559
  78.2 0.7 pad_add_fusion.1.info_ref
  78.8 1.3 %collective-permute-done.9.refs_1_ = bf16[72,4096]{1,0:T(8,128)(2,1)S(1)} collective-permute-done((bf16[72,4096]{1,0:T(8,128)(2,1)S(1)}, bf16[72,4096]{1,0:T(8,128)(2,1)S(1)}, u32[]{:S(2)}, u32[]{:S(2)}) %collective-permute-start.9) | collective-permute-done | bytes 589856 | tf_op jit(solution)/shard_map/ppermute | solution.py:471
  80.2 0.8 copy-done.15
  81.0 4.3 %base_keys.3.refs_0_ = f32[72,256]{1,0:T(8,128)} custom-call(s32[2]{0:T(128)} %pad_add_fusion.1.info_ref, bf16[16384,256]{1,0:T(8,128)(2,1)} %base_ref.3, bf16[72,4096]{1,0:T(8,128)(2,1)} %copy-done.14, bf16[72,4096]{1,0:T(8,128)(2,1)} %copy-done.15), custom_call_target="tpu_custom_call" | custom-call | bytes 1024 | tf_op jit(solution)/shard_map/base_keys/pallas_call | solution.py:143
  85.3 0.8 copy-done.13
  86.1 5.2 %attend_new.1 = (bf16[2,9,8,4096]{3,2,1,0:T(8,128)(2,1)}, bf16[2,9,8,256]{3,2,1,0:T(8,128)(2,1)}) custom-call(bf16[8,2,72,256]{3,2,1,0:T(8,128)(2,1)} %bitcast.28, f32[144,256]{1,0:T(8,128)} %copy-done.8, f32[72,256]{1,0:T(8,128)} %copy-done.9, f32[72,256]{1,0:T(8,128)} %base_keys.3.refs_0_, bf16[9,2,256,128]{3,2,1,0:T(8,128)(2,1)} %copy-done.3, ...), custom_call_target="tpu_custom_call" | custom-call | flops 603979776 | bytes 5898240 | tf_op jit(solution)/shard_map/attend_new/pallas_call | solution.py:421
  (28 shorter events, 0.1 us)
Async XLA Ops:
  0.6 4.2 %copy-start = (bf16[2,72,4096]{2,1,0:T(8,128)(2,1)S(1)}, bf16[2,72,4096]{2,1,0:T(8,128)(2,1)}, u32[]{:S(2)}) copy-start(bf16[2,72,4096]{2,1,0:T(8,128)(2,1)} %refs_0_.1) | copy-start | bytes 3538948
  0.6 4.2 %copy-start.16 = (bf16[16,2]{0,1:T(2,128)(2,1)S(1)}, bf16[16,2]{0,1:T(2,128)(2,1)}, u32[]{:S(2)}) copy-start(bf16[16,2]{0,1:T(2,128)(2,1)} %param.18) | copy-start | bytes 196
  1.9 16.4 %collective-permute-start.1 = (bf16[72,4096]{1,0:T(8,128)(2,1)S(1)}, bf16[72,4096]{1,0:T(8,128)(2,1)S(1)}, u32[]{:S(2)}, u32[]{:S(2)}) collective-permute-start(bf16[72,4096]{1,0:T(8,128)(2,1)S(1)} %constant_dynamic-slice_fusion.1), channel_id=1, source_target_pairs={{0,2},{2,0},{1,3},{3,1},{4,6},{6,4},{5,7},{7,5},{8,10},{10,8},{9,1... | collective-permute-start | bytes 1769480 | tf_op jit(solution)/shard_map/ppermute | solution.py:520
  4.9 15.5 %collective-permute-start = (bf16[144,4096]{1,0:T(8,128)(2,1)S(1)}, bf16[144,4096]{1,0:T(8,128)(2,1)S(1)}, u32[]{:S(2)}, u32[]{:S(2)}) collective-permute-start(bf16[144,4096]{1,0:T(8,128)(2,1)S(1)} %bitcast.23), channel_id=1, source_target_pairs={{0,1},{1,0},{2,3},{3,2},{4,5},{5,4},{6,7},{7,6},{8,9},{9,8},{10,11... | collective-permute-start | bytes 3538952 | tf_op jit(solution)/shard_map/ppermute | solution.py:471
  5.0 13.4 %collective-permute-start.2 = (f32[16,2]{1,0:T(8,128)S(1)}, f32[16,2]{1,0:T(8,128)S(1)}, u32[]{:S(2)}, u32[]{:S(2)}) collective-permute-start(f32[16,2]{1,0:T(8,128)S(1)} %convert_element_type.3.refs_0_), channel_id=1, source_target_pairs={{0,2},{2,0},{1,3},{3,1},{4,6},{6,4},{5,7},{7,5},{8,10},{10,8},{9,1... | collective-permute-start | bytes 392 | tf_op jit(solution)/shard_map/ppermute | solution.py:509
  6.4 14.0 %copy-start.11 = (s32[128]{0:T(128)S(1)}, s32[128]{0:T(128)}, u32[]{:S(2)}) copy-start(s32[128]{0:T(128)} %order_ref.1) | copy-start | bytes 1540
  18.4 2.0 %collective-permute-start.3 = (bf16[72,4096]{1,0:T(8,128)(2,1)S(1)}, bf16[72,4096]{1,0:T(8,128)(2,1)S(1)}, u32[]{:S(2)}, u32[]{:S(2)}) collective-permute-start(bf16[72,4096]{1,0:T(8,128)(2,1)S(1)} %collective-permute-done.1.refs_2_), channel_id=1, source_target_pairs={{0,1},{1,0},{2,3},{3,2},{4,5},{5,4},{6,7},{7,6},{8,9},{9,8},{10,11... | collective-permute-start | bytes 1769480 | tf_op jit(solution)/shard_map/ppermute | solution.py:471
  20.4 2.4 %copy-start.1 = (bf16[144,4096]{1,0:T(8,128)(2,1)}, bf16[144,4096]{1,0:T(8,128)(2,1)S(1)}, u32[]{:S(2)}) copy-start(bf16[144,4096]{1,0:T(8,128)(2,1)S(1)} %collective-permute-done.refs_1_) | copy-start | bytes 3538948
  22.8 35.0 %all-to-all-start = ((bf16[8,72,1024]{2,1,0:T(8,128)(2,1)}), bf16[8,72,1024]{2,1,0:T(8,128)(2,1)S(1)}, u32[]{:S(2)}, u32[]{:S(2)}) async-start(bf16[8,72,1024]{2,1,0:T(8,128)(2,1)} %scatter_columns.1), calls=%async_computation | async-start | bytes 2359296 | tf_op jit(solution)/shard_map/all_to_all | solution.py:574
  28.9 2.3 %collective-permute-start.4 = (bf16[2,512,256]{2,1,0:T(8,128)(2,1)}, bf16[2,512,256]{2,1,0:T(8,128)(2,1)}, u32[]{:S(2)}, u32[]{:S(2)}) collective-permute-start(bf16[2,512,256]{2,1,0:T(8,128)(2,1)} %pad_maximum_fusion.1), channel_id=1, source_target_pairs={{0,1},{1,0},{2,3},{3,2},{4,5},{5,4},{6,7},{7,6},{8,9},{9,8},{10,11... | collective-permute-start | bytes 1572872 | tf_op jit(solution)/shard_map/ppermute | solution.py:535
  29.0 7.1 %copy-start.12 = (s32[72]{0:T(128)S(1)}, s32[72]{0:T(128)}, u32[]{:S(2)}) copy-start(s32[72]{0:T(128)} %len_ref) | copy-start | bytes 868
  29.0 28.8 %collective-permute-start.5 = (bf16[2,512,256]{2,1,0:T(8,128)(2,1)}, bf16[2,512,256]{2,1,0:T(8,128)(2,1)}, u32[]{:S(2)}, u32[]{:S(2)}) collective-permute-start(bf16[2,512,256]{2,1,0:T(8,128)(2,1)} %pad_maximum_fusion.refs_2_), channel_id=1, source_target_pairs={{0,2},{1,3},{2,0},{3,1},{4,6},{5,7},{6,4},{7,5},{8,10},{9,11},{10,... | collective-permute-start | bytes 1572872 | tf_op jit(solution)/shard_map/ppermute | solution.py:535
  30.5 27.3 %collective-permute-start.6 = (bf16[2,512,256]{2,1,0:T(8,128)(2,1)}, bf16[2,512,256]{2,1,0:T(8,128)(2,1)}, u32[]{:S(2)}, u32[]{:S(2)}) collective-permute-start(bf16[2,512,256]{2,1,0:T(8,128)(2,1)} %pad_maximum_fusion.1), channel_id=1, source_target_pairs={{0,3},{1,2},{2,1},{3,0},{4,7},{5,6},{6,5},{7,4},{8,11},{9,10},{10,... | collective-permute-start | bytes 1572872 | tf_op jit(solution)/shard_map/ppermute | solution.py:535
  31.2 1.0 %copy-start.2 = (bf16[2,512,256]{2,1,0:T(8,128)(2,1)S(1)}, bf16[2,512,256]{2,1,0:T(8,128)(2,1)}, u32[]{:S(2)}) copy-start(bf16[2,512,256]{2,1,0:T(8,128)(2,1)} %pad_maximum_fusion.refs_2_) | copy-start | bytes 1572868
  33.5 0.9 copy-start.4
  34.4 0.8 copy-start.6
  41.5 1.0 %copy-start.3 = (bf16[9,2,256,128]{3,2,1,0:T(8,128)(2,1)}, bf16[9,2,256,128]{3,2,1,0:T(8,128)(2,1)S(1)}, u32[]{:S(2)}) copy-start(bf16[9,2,256,128]{3,2,1,0:T(8,128)(2,1)S(1)} %get-tuple-element.49.refs_1_) | copy-start | bytes 3538948
  42.5 0.6 copy-start.10
  48.6 0.7 copy-start.8
  49.2 0.6 copy-start.9
  49.9 11.0 %copy-start.7 = (bf16[2,512,256]{2,1,0:T(8,128)(2,1)S(1)}, bf16[2,512,256]{2,1,0:T(8,128)(2,1)}, u32[]{:S(2)}) copy-start(bf16[2,512,256]{2,1,0:T(8,128)(2,1)} %copy-done.6) | copy-start | bytes 1572868
  57.8 3.8 %collective-permute-start.7 = (bf16[576,1024]{1,0:T(8,128)(2,1)S(1)}, bf16[576,1024]{1,0:T(8,128)(2,1)S(1)}, u32[]{:S(2)}, u32[]{:S(2)}) collective-permute-start(bf16[576,1024]{1,0:T(8,128)(2,1)S(1)} %bitcast.26), channel_id=1, source_target_pairs={{0,1},{1,0},{2,3},{3,2},{4,5},{5,4},{6,7},{7,6},{8,9},{9,8},{10,11... | collective-permute-start | bytes 3538952 | tf_op jit(solution)/shard_map/ppermute | solution.py:471
  59.3 18.9 %collective-permute-start.8 = (bf16[72,4096]{1,0:T(8,128)(2,1)}, bf16[72,4096]{1,0:T(8,128)(2,1)S(1)}, u32[]{:S(2)}, u32[]{:S(2)}) collective-permute-start(bf16[72,4096]{1,0:T(8,128)(2,1)} %constant_dynamic-slice_fusion), channel_id=1, source_target_pairs={{0,2},{2,0},{1,3},{3,1},{4,6},{6,4},{5,7},{7,5},{8,10},{10,8},{9,1... | collective-permute-start | bytes 1769480 | tf_op jit(solution)/shard_map/ppermute | solution.py:559
  60.8 1.0 %copy-start.5 = (bf16[2,512,256]{2,1,0:T(8,128)(2,1)S(1)}, bf16[2,512,256]{2,1,0:T(8,128)(2,1)}, u32[]{:S(2)}) copy-start(bf16[2,512,256]{2,1,0:T(8,128)(2,1)} %copy-done.4) | copy-start | bytes 1572868
  63.5 21.8 %all-to-all-start.1 = ((bf16[16,72,256]{2,1,0:T(8,128)(2,1)}), bf16[16,72,256]{2,1,0:T(8,128)(2,1)S(1)}, u32[]{:S(2)}, u32[]{:S(2)}) async-start(bf16[16,72,256]{2,1,0:T(8,128)(2,1)} %bitcast.12), calls=%async_computation.1 | async-start | bytes 1179648 | tf_op jit(solution)/shard_map/all_to_all | solution.py:584
  78.2 2.0 %copy-start.14 = (bf16[72,4096]{1,0:T(8,128)(2,1)}, bf16[72,4096]{1,0:T(8,128)(2,1)S(1)}, u32[]{:S(2)}) copy-start(bf16[72,4096]{1,0:T(8,128)(2,1)S(1)} %collective-permute-done.8.refs_0_) | copy-start | bytes 1769476
  78.2 2.0 %collective-permute-start.9 = (bf16[72,4096]{1,0:T(8,128)(2,1)S(1)}, bf16[72,4096]{1,0:T(8,128)(2,1)S(1)}, u32[]{:S(2)}, u32[]{:S(2)}) collective-permute-start(bf16[72,4096]{1,0:T(8,128)(2,1)S(1)} %collective-permute-done.8.refs_0_), channel_id=1, source_target_pairs={{0,1},{1,0},{2,3},{3,2},{4,5},{5,4},{6,7},{7,6},{8,9},{9,8},{10,11... | collective-permute-start | bytes 1769480 | tf_op jit(solution)/shard_map/ppermute | solution.py:471
  80.2 0.8 copy-start.15
  85.3 0.8 copy-start.13

commit v3 on v2

--- a/solution.py
+++ b/solution.py
@@ -18,6 +18,7 @@
 MIB = 1024 * 1024
 GRANT = 57 * MIB
 MIDDLE = 52 * MIB
+LATE = 55 * MIB
 BESIDE = pl.CostEstimate(flops=0, bytes_accessed=1024, transcendentals=0)
 CONTRACT_LAST = (((1,), (1,)), ((), ()))
 CONTRACT_FIRST = (((0,), (0,)), ((), ()))
@@ -36,7 +37,7 @@
 
 
 def scatter_kernel(nx, parts, order_ref, *refs):
-    pieces, (o_ref, all_ref, sems) = refs[:-3], refs[-3:]
+    pieces, (out_ref, o_ref, all_ref, sems) = refs[:-4], refs[-4:]
     nf = o_ref.shape[0]
     per_t = all_ref.shape[2] // BLK
     per_f = order_ref.shape[0] // nf
@@ -50,6 +51,9 @@
         if len(piece.shape) == 3:
             piece = piece.at[x]
         return pltpu.make_async_copy(piece, all_ref.at[i], sems.at[i])
+
+    def send(f):
+        return pltpu.make_async_copy(o_ref.at[f], out_ref.at[f], sems.at[len(pieces) + f])
 
     for i in range(len(pieces)):
         fetch(i).start()
@@ -70,6 +74,9 @@
             index = chip * 2 + ((owner & 1) ^ core)
             lanes = pl.ds(pl.multiple_of((block & (per_t - 1)) * BLK, BLK), BLK)
             o_ref[f, :, at * BLK : (at + 1) * BLK] = all_ref[index, :, lanes]
+        send(f).start()
+    for f in range(nf):
+        send(f).wait()
 
 
 def scatter(order, pieces, nf, split):
@@ -80,10 +87,11 @@
         out_shape=jax.ShapeDtypeStruct((nf, rows, width), jnp.bfloat16),
         in_specs=[pl.BlockSpec(memory_space=pltpu.SMEM)]
         + [pl.BlockSpec(memory_space=pl.ANY)] * len(pieces),
-        out_specs=pl.BlockSpec(memory_space=pltpu.VMEM),
+        out_specs=pl.BlockSpec(memory_space=pl.ANY),
         scratch_shapes=[
+            pltpu.VMEM((nf, rows, width), jnp.bfloat16),
             pltpu.VMEM((len(pieces), rows, cols), jnp.bfloat16),
-            pltpu.SemaphoreType.DMA((len(pieces),)),
+            pltpu.SemaphoreType.DMA((len(pieces) + nf,)),
         ],
         compiler_params=params(4 * len(pieces) * rows * cols),
         cost_estimate=pl.CostEstimate(
@@ -535,10 +543,7 @@
         ws.append(lax.ppermute((behind if d else sent)[e], ("tx", "core"), to_shift(d, e)))
     arrived = ws[1:]
     if split > 1:
-        ws = [
-            *scale_rows(scales, shifts[:2], ws[:2]),
-            *scale_rows(scales, shifts[2:], ws[2:]),
-        ]
+        ws[:2] = scale_rows(scales, shifts[:2], ws[:2])
     if split == 1:
         by_chip = jnp.repeat(jnp.roll(jnp.stack(scales), x, axis=0), BLK, axis=2)
         whole = jnp.zeros((nx, depth, cols), jnp.bfloat16)
@@ -571,9 +576,13 @@
     share = cached(
         then, queries.reshape(shape + queries.shape[2:]), cache_keys, cache_values
     )
+    if split > 1:
+        for earlier in (near, far, share[0]):
+            scales = after(scales, earlier)
+        ws[2:] = scale_rows(scales, shifts[2:], ws[2:])
     mine = lax.all_to_all(mine, "fsdp", 0, 0, tiled=True)
     xs = [mine.reshape(nf * count * RB, depth // split)]
-    for earlier in (*arrived, near, far, share[0]):
+    for earlier in (*arrived[:1], *ws[-2:], near, far, share[0]):
         xs = after(xs, earlier)
     if split > 1:
         xs.append(swap(xs[0]))
@@ -586,7 +595,7 @@
     ).reshape(nf, nx, count * RB, cols)
     remaining = [held[d][r][e] for d in range(1, nx) for e in range(2) for r in range(1, nx)]
     plan = (tuple(range(nx - 1)),) * (2 * (nx - 1))
-    late = base_product(after([owners[2:]], partial)[0], plan, remaining, base_weight, GRANT)
+    late = base_product(after([owners[2:]], partial)[0], plan, remaining, base_weight, LATE)
     attended, new_keys = merge(parts, near, far, late, *share, new_values.reshape(shape + (cols,)))
     return (attended.reshape(queries.shape), new_keys.reshape(steps, rows, cols))
 

time: 91.9 us -> 90.8 us (0.988)
  waiting for transfers between devices: 32.8 us -> 29.5 us
  local copies, waits for them, and re-layouts: 11 us -> 12.5 us
  starting transfers between devices: 16.4 us -> 17.6 us
    all_to_all x1, waiting for transfers between devices: 7.93 us -> 1.7 us  [per_device(): mine = lax.all_to_all(mine, 'fsdp', 0, 0, tiled=True)]
    ppermute x1, waiting for transfers between devices: 10.9 us -> 6.38 us  [per_device(): came = lax.ppermute(piece, 'tx', shift_of(nx, d))]
    ppermute x3, waiting for transfers between devices: 0.3 us -> 4.76 us  [per_device(): lax.ppermute((behind if d else sent)[e], ('tx', 'core'), to_shift(d, e))]
    all_to_all x1, waiting for transfers between devices: 0.01 us -> 3.15 us  [per_device(): lax.all_to_all(partial.reshape(nf * nx, count * RB, cols), ('fsdp', 'tx')...]
    unnamed x35 -> x41, local copies, waits for them, and re-layouts: 7.64 us -> 9.15 us
    all_to_all x1, starting transfers between devices: 3.75 us -> 4.98 us  [per_device(): lax.all_to_all(partial.reshape(nf * nx, count * RB, cols), ('fsdp', 'tx')...]
  transfers between devices with their start and end apart: 12 -> 12, of which waited for: 7 -> 9; matrix products, arithmetic and copies ran while one was open for 5% -> 5% of each run, Pallas kernels for 22% -> 22%
where the time goes in v3:
time: 90.8 us; the launch traced here: 90.3 us
  waiting for transfers between devices  29.5 us (32%)
  Pallas kernels  27.3 us (30%)
  starting transfers between devices  17.6 us (19%)
  local copies, waits for them, and re-layouts  12.5 us (14%)
  other arithmetic  2.49 us (3%)
    ppermute x1, waiting for transfers between devices, per_device(): came = lax.ppermute(rows_of(flat, -d % nx), 'tx', shift_of(nx, d))  10.1 us
    pallas_call x2, Pallas kernels, base_product(): pl.pallas_call(functools.partial(base_kernel, plan), out_shape=tuple((jax...  9.67 us
    unnamed x41, local copies, waits for them, and re-layouts  9.15 us
    ppermute x1, waiting for transfers between devices, per_device(): came = lax.ppermute(piece, 'tx', shift_of(nx, d))  6.38 us
    all_to_all x1, starting transfers between devices, per_device(): mine = lax.all_to_all(mine, 'fsdp', 0, 0, tiled=True)  6.09 us
    pallas_call x1, Pallas kernels, cached(): pl.pallas_call(cached_kernel, grid=(batches // n,), out_shape=(jax.ShapeD...  5.49 us
    pallas_call x1, Pallas kernels, merge(): pl.pallas_call(functools.partial(merge_kernel, parts.shape[1]), grid=(bat...  5.24 us
    all_to_all x1, starting transfers between devices, per_device(): lax.all_to_all(partial.reshape(nf * nx, count * RB, cols), ('fsdp', 'tx')...  4.98 us
  transfers between devices with their start and end apart: 12, of which 9 were waited for; matrix products, arithmetic and copies ran while one was open for 5% of the time, Pallas kernels for 22%

profile of v3, /device:TPU:0, one launch (start us, length us, event | category | flops | bytes accessed | tf_op | source)
XLA Modules:
  0.0 90.3 jit_solution(886675948145796414)
XLA Ops:
  0.6 0.0 copy-start
  0.7 1.2 %constant_dynamic-slice_fusion.1 = bf16[72,4096]{1,0:T(8,128)(2,1)S(1)} fusion(bf16[144,4096]{1,0:T(8,128)(2,1)} %bitcast.21, s32[]{:T(128)S(6)} %mul.28), kind=kLoop, calls=%fused_computation.7 | loop fusion | bytes 1179652 | tf_op jit(solution)/shard_map/dynamic_slice | solution.py:471
  1.9 3.0 %collective-permute-start.1 = (bf16[72,4096]{1,0:T(8,128)(2,1)S(1)}, bf16[72,4096]{1,0:T(8,128)(2,1)S(1)}, u32[]{:S(2)}, u32[]{:S(2)}) collective-permute-start(bf16[72,4096]{1,0:T(8,128)(2,1)S(1)} %constant_dynamic-slice_fusion.1), channel_id=1, source_target_pairs={{0,2},{2,0},{1,3},{3,1},{4,6},{6,4},{5,7},{7,5},{8,10},{10,8},{9,1... | collective-permute-start | bytes 1769480 | tf_op jit(solution)/shard_map/ppermute | solution.py:528
  4.9 0.1 copy.12
  5.0 0.2 collective-permute-start.2
  5.1 1.3 %dynamic-slice_bitcast_fusion.1 = (bf16[1,512,256]{2,1,0:T(8,128)(2,1)S(1)}, bf16[1,512,256]{2,1,0:T(8,128)(2,1)S(1)}, bf16[1,512,256]{2,1,0:T(8,128)(2,1)S(1)}, bf16[1,512,256]{2,1,0:T(8,128)(2,1)S(1)}) fusion(bf16[512,1024]{1,0:T(8,128)(2,1)} %param.17, s32[]{:T(128)S(6)} %mul.31, s32[]{:T(128)S(6)} %mul.30, s32[]{:T(128)S(6)} %mul.29, s32[]{:T(128)S(6)} %mul.32), kind=kLoop, calls=%fused_computation.3 | loop fusion | bytes 2097168 | tf_op jit(solution)/shard_map/stack | solution.py:514
  6.4 0.0 copy-start.13
  6.4 0.9 pad_maximum_fusion.1
  7.3 0.9 pad_maximum_fusion.refs_2_
  8.1 10.1 %collective-permute-done.1.refs_2_ = bf16[72,4096]{1,0:T(8,128)(2,1)S(1)} collective-permute-done((bf16[72,4096]{1,0:T(8,128)(2,1)S(1)}, bf16[72,4096]{1,0:T(8,128)(2,1)S(1)}, u32[]{:S(2)}, u32[]{:S(2)}) %collective-permute-start.1) | collective-permute-done | bytes 589856 | tf_op jit(solution)/shard_map/ppermute | solution.py:528
  18.3 0.1 collective-permute-done.2.refs_1_
  18.4 0.0 collective-permute-start.3
  18.4 2.0 %collective-permute-done.3.refs_3_ = bf16[72,4096]{1,0:T(8,128)(2,1)S(1)} collective-permute-done((bf16[72,4096]{1,0:T(8,128)(2,1)S(1)}, bf16[72,4096]{1,0:T(8,128)(2,1)S(1)}, u32[]{:S(2)}, u32[]{:S(2)}) %collective-permute-start.3) | collective-permute-done | bytes 589856 | tf_op jit(solution)/shard_map/ppermute | solution.py:479
  20.4 0.0 collective-permute-done.refs_1_
  20.4 2.2 %scatter_columns.1 = bf16[8,72,1024]{2,1,0:T(8,128)(2,1)} custom-call(s32[128]{0:T(128)S(1)} %copy-done.13, bf16[2,72,4096]{2,1,0:T(8,128)(2,1)S(1)} %copy-done, bf16[2,72,4096]{2,1,0:T(8,128)(2,1)S(1)} %bitcast.25, bf16[72,4096]{1,0:T(8,128)(2,1)S(1)} %collective-permute-done.1.refs_2_, bf16[72,4096]{1,0:T(8,128)(2,1)S(1)} %collective-permute-done.3.refs_3_), custom_call_target="tpu_custom_call" | custom-call | bytes 3538944 | tf_op jit(solution)/shard_map/scatter_columns/pallas_call | solution.py:85
  22.6 6.1 %all-to-all-start = ((bf16[8,72,1024]{2,1,0:T(8,128)(2,1)}), bf16[8,72,1024]{2,1,0:T(8,128)(2,1)S(1)}, u32[]{:S(2)}, u32[]{:S(2)}) async-start(bf16[8,72,1024]{2,1,0:T(8,128)(2,1)} %scatter_columns.1), calls=%async_computation | async-start | bytes 2359296 | tf_op jit(solution)/shard_map/all_to_all | solution.py:583
  28.7 1.6 %collective-permute-start.5 = (bf16[2,512,256]{2,1,0:T(8,128)(2,1)}, bf16[2,512,256]{2,1,0:T(8,128)(2,1)S(1)}, u32[]{:S(2)}, u32[]{:S(2)}) collective-permute-start(bf16[2,512,256]{2,1,0:T(8,128)(2,1)} %pad_maximum_fusion.refs_2_), channel_id=1, source_target_pairs={{0,2},{1,3},{2,0},{3,1},{4,6},{5,7},{6,4},{7,5},{8,10},{9,11},{10,... | collective-permute-start | bytes 1572872 | tf_op jit(solution)/shard_map/ppermute | solution.py:543
  30.3 0.3 collective-permute-start.6
  30.6 0.1 pad_add_fusion.info_ref
  30.6 0.3 collective-permute-done.4.refs_3_
  30.9 1.0 %copy-done.2 = bf16[2,512,256]{2,1,0:T(8,128)(2,1)S(1)} copy-done((bf16[2,512,256]{2,1,0:T(8,128)(2,1)S(1)}, bf16[2,512,256]{2,1,0:T(8,128)(2,1)}, u32[]{:S(2)}) %copy-start.2) | copy-done | bytes 524312
  32.0 1.3 %scale_rows.2 = (bf16[2,512,256]{2,1,0:T(8,128)(2,1)S(1)}, bf16[2,512,256]{2,1,0:T(8,128)(2,1)S(1)}) custom-call(f32[16,2]{1,0:T(8,128)S(1)} %convert_element_type.3.refs_0_, f32[16,2]{1,0:T(8,128)S(1)} %collective-permute-done.2.refs_1_, bf16[2,512,256]{2,1,0:T(8,128)(2,1)S(1)} %copy-done.2, bf16[2,512,256]{2,1,0:T(8,128)(2,1)} %collective-permute-done.4.refs_3_), custom_call_target="tpu_custom_call" | custom-call | bytes 1024 | tf_op jit(solution)/shard_map/scale_rows/pallas_call | solution.py:193
  33.3 0.8 copy-done.4
  34.1 0.8 copy-done.6
  34.9 0.9 constant_dynamic-slice_fusion
  35.7 5.4 %base_keys.2 = (f32[144,256]{1,0:T(8,128)S(1)}, f32[72,256]{1,0:T(8,128)S(1)}) custom-call(s32[4]{0:T(128)S(1)} %pad_add_fusion.info_ref, bf16[16384,256]{1,0:T(8,128)(2,1)} %base_ref.3, bf16[144,4096]{1,0:T(8,128)(2,1)} %bitcast.22, bf16[144,4096]{1,0:T(8,128)(2,1)} %copy-done.1, bf16[72,4096]{1,0:T(8,128)(2,1)S(1)} %collective-permute-done.1.refs_2_, ...), custom_call_target="tpu_custom_call" | custom-call | bytes 1024 | tf_op jit(solution)/shard_map/base_keys/pallas_call | solution.py:151
  41.1 0.6 copy-done.10
  41.8 0.6 copy-done.11
  42.4 5.5 %attend_cached.1 = (bf16[9,2,256,128]{3,2,1,0:T(8,128)(2,1)S(1)}, f32[9,2,128,256]{3,2,1,0:T(8,128)}, f32[9,2,2,256]{3,2,1,0:T(2,128)S(1)}) custom-call(s32[72]{0:T(128)S(1)} %copy-done.14, bf16[2,9,8,4096]{3,2,1,0:T(8,128)(2,1)} %bitcast.29, bf16[72,32,256]{2,1,0:T(8,128)(2,1)} %ck_ref.1, bf16[72,32,256]{2,1,0:T(8,128)(2,1)} %cv_ref.1), custom_call_target="tpu_custom_call" | custom-call | bytes 1024 | tf_op jit(solution)/shard_map/attend_cached/pallas_call | solution.py:313
  47.9 1.0 %copy-done.3 = bf16[9,2,256,128]{3,2,1,0:T(8,128)(2,1)} copy-done((bf16[9,2,256,128]{3,2,1,0:T(8,128)(2,1)}, bf16[9,2,256,128]{3,2,1,0:T(8,128)(2,1)S(1)}, u32[]{:S(2)}) %copy-start.3) | copy-done | bytes 1179672
  48.9 0.6 copy-done.12
  49.6 4.5 %collective-permute-done.6.refs_3_ = bf16[2,512,256]{2,1,0:T(8,128)(2,1)S(1)} collective-permute-done((bf16[2,512,256]{2,1,0:T(8,128)(2,1)}, bf16[2,512,256]{2,1,0:T(8,128)(2,1)S(1)}, u32[]{:S(2)}, u32[]{:S(2)}) %collective-permute-start.6) | collective-permute-done | bytes 524320 | tf_op jit(solution)/shard_map/ppermute | solution.py:543
  54.0 1.0 %scale_rows.3 = (bf16[2,512,256]{2,1,0:T(8,128)(2,1)S(1)}, bf16[2,512,256]{2,1,0:T(8,128)(2,1)S(1)}) custom-call(f32[16,2]{1,0:T(8,128)S(1)} %convert_element_type.3.refs_0_, f32[16,2]{1,0:T(8,128)S(1)} %collective-permute-done.2.refs_1_, bf16[2,512,256]{2,1,0:T(8,128)(2,1)S(1)} %collective-permute-done.5.refs_2_, ...), custom_call_target="tpu_custom_call" | custom-call | bytes 1024 | tf_op jit(solution)/shard_map/scale_rows/pallas_call | solution.py:193
  55.1 0.8 copy-done.8
  55.9 1.7 %all-to-all-done = bf16[8,72,1024]{2,1,0:T(8,128)(2,1)S(1)} async-done(((bf16[8,72,1024]{2,1,0:T(8,128)(2,1)}), bf16[8,72,1024]{2,1,0:T(8,128)(2,1)S(1)}, u32[]{:S(2)}, u32[]{:S(2)}) %all-to-all-start) | async-done | bytes 1179680 | tf_op jit(solution)/shard_map/all_to_all | solution.py:583
  57.6 1.6 %collective-permute-start.8 = (bf16[72,4096]{1,0:T(8,128)(2,1)S(1)}, bf16[72,4096]{1,0:T(8,128)(2,1)S(1)}, u32[]{:S(2)}, u32[]{:S(2)}) collective-permute-start(bf16[72,4096]{1,0:T(8,128)(2,1)S(1)} %copy-done.18), channel_id=1, source_target_pairs={{0,2},{2,0},{1,3},{3,1},{4,6},{6,4},{5,7},{7,5},{8,10},{10,8},{9,1... | collective-permute-start | bytes 1769480 | tf_op jit(solution)/shard_map/ppermute | solution.py:564
  59.1 1.0 %copy-done.9 = bf16[2,512,256]{2,1,0:T(8,128)(2,1)S(1)} copy-done((bf16[2,512,256]{2,1,0:T(8,128)(2,1)S(1)}, bf16[2,512,256]{2,1,0:T(8,128)(2,1)}, u32[]{:S(2)}) %copy-start.9) | copy-done | bytes 524312
  60.2 0.8 partial_keys.2.refs_3_
  61.0 1.6 %partial_keys.3 = bf16[8,2,72,256]{3,2,1,0:T(8,128)(2,1)} custom-call(bf16[576,1024]{1,0:T(8,128)(2,1)S(1)} %collective-permute-done.7.refs_0_, bf16[2,512,256]{2,1,0:T(8,128)(2,1)S(1)} %copy-done.5, bf16[2,512,256]{2,1,0:T(8,128)(2,1)S(1)} %get-tuple-element.60.refs_2_, f32[2,576,256]{2,1,0:T(8,128)S(1)} %partial_keys.2.refs_3_), custom_call_target="tpu_custom_call" | custom-call | flops 603979776 | bytes 3997696 | tf_op jit(solution)/shard_map/partial_keys/pallas_call | solution.py:237
  62.6 5.0 %all-to-all-start.1 = ((bf16[16,72,256]{2,1,0:T(8,128)(2,1)}), bf16[16,72,256]{2,1,0:T(8,128)(2,1)S(1)}, u32[]{:S(2)}, u32[]{:S(2)}) async-start(bf16[16,72,256]{2,1,0:T(8,128)(2,1)} %bitcast.12), calls=%async_computation.1 | async-start | bytes 1179648 | tf_op jit(solution)/shard_map/all_to_all | solution.py:593
  67.6 6.4 %collective-permute-done.8.refs_0_ = bf16[72,4096]{1,0:T(8,128)(2,1)S(1)} collective-permute-done((bf16[72,4096]{1,0:T(8,128)(2,1)S(1)}, bf16[72,4096]{1,0:T(8,128)(2,1)S(1)}, u32[]{:S(2)}, u32[]{:S(2)}) %collective-permute-start.8) | collective-permute-done | bytes 589856 | tf_op jit(solution)/shard_map/ppermute | solution.py:564
  74.0 0.7 pad_add_fusion.1.info_ref
  74.6 1.3 %collective-permute-done.9.refs_1_ = bf16[72,4096]{1,0:T(8,128)(2,1)S(1)} collective-permute-done((bf16[72,4096]{1,0:T(8,128)(2,1)S(1)}, bf16[72,4096]{1,0:T(8,128)(2,1)S(1)}, u32[]{:S(2)}, u32[]{:S(2)}) %collective-permute-start.9) | collective-permute-done | bytes 589856 | tf_op jit(solution)/shard_map/ppermute | solution.py:479
  76.0 0.8 copy-done.17
  76.8 4.3 %base_keys.3.refs_0_ = f32[72,256]{1,0:T(8,128)} custom-call(s32[2]{0:T(128)} %pad_add_fusion.1.info_ref, bf16[16384,256]{1,0:T(8,128)(2,1)} %base_ref.3, bf16[72,4096]{1,0:T(8,128)(2,1)} %copy-done.16, bf16[72,4096]{1,0:T(8,128)(2,1)} %copy-done.17), custom_call_target="tpu_custom_call" | custom-call | bytes 1024 | tf_op jit(solution)/shard_map/base_keys/pallas_call | solution.py:151
  81.0 3.2 %all-to-all-done.1 = bf16[16,72,256]{2,1,0:T(8,128)(2,1)S(1)} async-done(((bf16[16,72,256]{2,1,0:T(8,128)(2,1)}), bf16[16,72,256]{2,1,0:T(8,128)(2,1)S(1)}, u32[]{:S(2)}, u32[]{:S(2)}) %all-to-all-start.1) | async-done | bytes 589856 | tf_op jit(solution)/shard_map/all_to_all | solution.py:593
  84.2 0.8 copy-done.15
  85.0 5.2 %attend_new.1 = (bf16[2,9,8,4096]{3,2,1,0:T(8,128)(2,1)}, bf16[2,9,8,256]{3,2,1,0:T(8,128)(2,1)}) custom-call(bf16[8,2,72,256]{3,2,1,0:T(8,128)(2,1)} %bitcast.28, f32[144,256]{1,0:T(8,128)} %copy-done.10, f32[72,256]{1,0:T(8,128)} %copy-done.11, f32[72,256]{1,0:T(8,128)} %base_keys.3.refs_0_, bf16[9,2,256,128]{3,2,1,0:T(8,128)(2,1)} %copy-done.3, ...), custom_call_target="tpu_custom_call" | custom-call | flops 603979776 | bytes 5898240 | tf_op jit(solution)/shard_map/attend_new/pallas_call | solution.py:429
  (34 shorter events, 0.1 us)
Async XLA Ops:
  0.6 4.2 %copy-start = (bf16[2,72,4096]{2,1,0:T(8,128)(2,1)S(1)}, bf16[2,72,4096]{2,1,0:T(8,128)(2,1)}, u32[]{:S(2)}) copy-start(bf16[2,72,4096]{2,1,0:T(8,128)(2,1)} %refs_0_.1) | copy-start | bytes 3538948
  0.6 4.2 %copy-start.19 = (bf16[16,2]{0,1:T(2,128)(2,1)S(1)}, bf16[16,2]{0,1:T(2,128)(2,1)}, u32[]{:S(2)}) copy-start(bf16[16,2]{0,1:T(2,128)(2,1)} %param.18) | copy-start | bytes 196
  1.9 16.4 %collective-permute-start.1 = (bf16[72,4096]{1,0:T(8,128)(2,1)S(1)}, bf16[72,4096]{1,0:T(8,128)(2,1)S(1)}, u32[]{:S(2)}, u32[]{:S(2)}) collective-permute-start(bf16[72,4096]{1,0:T(8,128)(2,1)S(1)} %constant_dynamic-slice_fusion.1), channel_id=1, source_target_pairs={{0,2},{2,0},{1,3},{3,1},{4,6},{6,4},{5,7},{7,5},{8,10},{10,8},{9,1... | collective-permute-start | bytes 1769480 | tf_op jit(solution)/shard_map/ppermute | solution.py:528
  4.9 15.5 %collective-permute-start = (bf16[144,4096]{1,0:T(8,128)(2,1)S(1)}, bf16[144,4096]{1,0:T(8,128)(2,1)S(1)}, u32[]{:S(2)}, u32[]{:S(2)}) collective-permute-start(bf16[144,4096]{1,0:T(8,128)(2,1)S(1)} %bitcast.23), channel_id=1, source_target_pairs={{0,1},{1,0},{2,3},{3,2},{4,5},{5,4},{6,7},{7,6},{8,9},{9,8},{10,11... | collective-permute-start | bytes 3538952 | tf_op jit(solution)/shard_map/ppermute | solution.py:479
  5.0 13.4 %collective-permute-start.2 = (f32[16,2]{1,0:T(8,128)S(1)}, f32[16,2]{1,0:T(8,128)S(1)}, u32[]{:S(2)}, u32[]{:S(2)}) collective-permute-start(f32[16,2]{1,0:T(8,128)S(1)} %convert_element_type.3.refs_0_), channel_id=1, source_target_pairs={{0,2},{2,0},{1,3},{3,1},{4,6},{6,4},{5,7},{7,5},{8,10},{10,8},{9,1... | collective-permute-start | bytes 392 | tf_op jit(solution)/shard_map/ppermute | solution.py:517
  6.4 14.0 %copy-start.13 = (s32[128]{0:T(128)S(1)}, s32[128]{0:T(128)}, u32[]{:S(2)}) copy-start(s32[128]{0:T(128)} %order_ref.1) | copy-start | bytes 1540
  18.4 2.0 %collective-permute-start.3 = (bf16[72,4096]{1,0:T(8,128)(2,1)S(1)}, bf16[72,4096]{1,0:T(8,128)(2,1)S(1)}, u32[]{:S(2)}, u32[]{:S(2)}) collective-permute-start(bf16[72,4096]{1,0:T(8,128)(2,1)S(1)} %collective-permute-done.1.refs_2_), channel_id=1, source_target_pairs={{0,1},{1,0},{2,3},{3,2},{4,5},{5,4},{6,7},{7,6},{8,9},{9,8},{10,11... | collective-permute-start | bytes 1769480 | tf_op jit(solution)/shard_map/ppermute | solution.py:479
  20.4 2.2 %copy-start.1 = (bf16[144,4096]{1,0:T(8,128)(2,1)}, bf16[144,4096]{1,0:T(8,128)(2,1)S(1)}, u32[]{:S(2)}) copy-start(bf16[144,4096]{1,0:T(8,128)(2,1)S(1)} %collective-permute-done.refs_1_) | copy-start | bytes 3538948
  22.6 35.0 %all-to-all-start = ((bf16[8,72,1024]{2,1,0:T(8,128)(2,1)}), bf16[8,72,1024]{2,1,0:T(8,128)(2,1)S(1)}, u32[]{:S(2)}, u32[]{:S(2)}) async-start(bf16[8,72,1024]{2,1,0:T(8,128)(2,1)} %scatter_columns.1), calls=%async_computation | async-start | bytes 2359296 | tf_op jit(solution)/shard_map/all_to_all | solution.py:583
  28.7 2.3 %collective-permute-start.4 = (bf16[2,512,256]{2,1,0:T(8,128)(2,1)}, bf16[2,512,256]{2,1,0:T(8,128)(2,1)}, u32[]{:S(2)}, u32[]{:S(2)}) collective-permute-start(bf16[2,512,256]{2,1,0:T(8,128)(2,1)} %pad_maximum_fusion.1), channel_id=1, source_target_pairs={{0,1},{1,0},{2,3},{3,2},{4,5},{5,4},{6,7},{7,6},{8,9},{9,8},{10,11... | collective-permute-start | bytes 1572872 | tf_op jit(solution)/shard_map/ppermute | solution.py:543
  28.7 20.8 %collective-permute-start.5 = (bf16[2,512,256]{2,1,0:T(8,128)(2,1)}, bf16[2,512,256]{2,1,0:T(8,128)(2,1)S(1)}, u32[]{:S(2)}, u32[]{:S(2)}) collective-permute-start(bf16[2,512,256]{2,1,0:T(8,128)(2,1)} %pad_maximum_fusion.refs_2_), channel_id=1, source_target_pairs={{0,2},{1,3},{2,0},{3,1},{4,6},{5,7},{6,4},{7,5},{8,10},{9,11},{10,... | collective-permute-start | bytes 1572872 | tf_op jit(solution)/shard_map/ppermute | solution.py:543
  30.3 23.7 %collective-permute-start.6 = (bf16[2,512,256]{2,1,0:T(8,128)(2,1)}, bf16[2,512,256]{2,1,0:T(8,128)(2,1)S(1)}, u32[]{:S(2)}, u32[]{:S(2)}) collective-permute-start(bf16[2,512,256]{2,1,0:T(8,128)(2,1)} %pad_maximum_fusion.1), channel_id=1, source_target_pairs={{0,3},{1,2},{2,1},{3,0},{4,7},{5,6},{6,5},{7,4},{8,11},{9,10},{10,... | collective-permute-start | bytes 1572872 | tf_op jit(solution)/shard_map/ppermute | solution.py:543
  30.9 1.0 %copy-start.2 = (bf16[2,512,256]{2,1,0:T(8,128)(2,1)S(1)}, bf16[2,512,256]{2,1,0:T(8,128)(2,1)}, u32[]{:S(2)}) copy-start(bf16[2,512,256]{2,1,0:T(8,128)(2,1)} %pad_maximum_fusion.refs_2_) | copy-start | bytes 1572868
  33.3 0.8 copy-start.4
  34.1 0.8 copy-start.6
  35.7 6.7 %copy-start.14 = (s32[72]{0:T(128)S(1)}, s32[72]{0:T(128)}, u32[]{:S(2)}) copy-start(s32[72]{0:T(128)} %len_ref) | copy-start | bytes 868
  41.1 0.7 copy-start.10
  41.8 0.6 copy-start.11
  42.4 15.1 %copy-start.18 = (bf16[72,4096]{1,0:T(8,128)(2,1)S(1)}, bf16[72,4096]{1,0:T(8,128)(2,1)}, u32[]{:S(2)}) copy-start(bf16[72,4096]{1,0:T(8,128)(2,1)} %constant_dynamic-slice_fusion) | copy-start | bytes 1769476
  47.9 1.0 %copy-start.3 = (bf16[9,2,256,128]{3,2,1,0:T(8,128)(2,1)}, bf16[9,2,256,128]{3,2,1,0:T(8,128)(2,1)S(1)}, u32[]{:S(2)}) copy-start(bf16[9,2,256,128]{3,2,1,0:T(8,128)(2,1)S(1)} %get-tuple-element.53.refs_1_) | copy-start | bytes 3538948
  48.9 0.6 copy-start.12
  49.5 9.6 %copy-start.7 = (bf16[2,512,256]{2,1,0:T(8,128)(2,1)S(1)}, bf16[2,512,256]{2,1,0:T(8,128)(2,1)}, u32[]{:S(2)}) copy-start(bf16[2,512,256]{2,1,0:T(8,128)(2,1)} %copy-done.6) | copy-start | bytes 1572868
  55.0 0.8 copy-start.8
  57.6 3.4 %copy-start.5 = (bf16[2,512,256]{2,1,0:T(8,128)(2,1)S(1)}, bf16[2,512,256]{2,1,0:T(8,128)(2,1)}, u32[]{:S(2)}) copy-start(bf16[2,512,256]{2,1,0:T(8,128)(2,1)} %copy-done.4) | copy-start | bytes 1572868
  57.6 3.4 %collective-permute-start.7 = (bf16[576,1024]{1,0:T(8,128)(2,1)S(1)}, bf16[576,1024]{1,0:T(8,128)(2,1)S(1)}, u32[]{:S(2)}, u32[]{:S(2)}) collective-permute-start(bf16[576,1024]{1,0:T(8,128)(2,1)S(1)} %bitcast.26), channel_id=1, source_target_pairs={{0,1},{1,0},{2,3},{3,2},{4,5},{5,4},{6,7},{7,6},{8,9},{9,8},{10,11... | collective-permute-start | bytes 3538952 | tf_op jit(solution)/shard_map/ppermute | solution.py:479
  57.6 16.4 %collective-permute-start.8 = (bf16[72,4096]{1,0:T(8,128)(2,1)S(1)}, bf16[72,4096]{1,0:T(8,128)(2,1)S(1)}, u32[]{:S(2)}, u32[]{:S(2)}) collective-permute-start(bf16[72,4096]{1,0:T(8,128)(2,1)S(1)} %copy-done.18), channel_id=1, source_target_pairs={{0,2},{2,0},{1,3},{3,1},{4,6},{6,4},{5,7},{7,5},{8,10},{10,8},{9,1... | collective-permute-start | bytes 1769480 | tf_op jit(solution)/shard_map/ppermute | solution.py:564
  59.1 1.0 %copy-start.9 = (bf16[2,512,256]{2,1,0:T(8,128)(2,1)S(1)}, bf16[2,512,256]{2,1,0:T(8,128)(2,1)}, u32[]{:S(2)}) copy-start(bf16[2,512,256]{2,1,0:T(8,128)(2,1)} %copy-done.8) | copy-start | bytes 1572868
  62.6 21.6 %all-to-all-start.1 = ((bf16[16,72,256]{2,1,0:T(8,128)(2,1)}), bf16[16,72,256]{2,1,0:T(8,128)(2,1)S(1)}, u32[]{:S(2)}, u32[]{:S(2)}) async-start(bf16[16,72,256]{2,1,0:T(8,128)(2,1)} %bitcast.12), calls=%async_computation.1 | async-start | bytes 1179648 | tf_op jit(solution)/shard_map/all_to_all | solution.py:593
  73.9 2.0 %copy-start.16 = (bf16[72,4096]{1,0:T(8,128)(2,1)}, bf16[72,4096]{1,0:T(8,128)(2,1)S(1)}, u32[]{:S(2)}) copy-start(bf16[72,4096]{1,0:T(8,128)(2,1)S(1)} %collective-permute-done.8.refs_0_) | copy-start | bytes 1769476
  74.0 2.0 %collective-permute-start.9 = (bf16[72,4096]{1,0:T(8,128)(2,1)S(1)}, bf16[72,4096]{1,0:T(8,128)(2,1)S(1)}, u32[]{:S(2)}, u32[]{:S(2)}) collective-permute-start(bf16[72,4096]{1,0:T(8,128)(2,1)S(1)} %collective-permute-done.8.refs_0_), channel_id=1, source_target_pairs={{0,1},{1,0},{2,3},{3,2},{4,5},{5,4},{6,7},{7,6},{8,9},{9,8},{10,11... | collective-permute-start | bytes 1769480 | tf_op jit(solution)/shard_map/ppermute | solution.py:479
  76.0 0.8 copy-start.17
  84.2 0.8 copy-start.15

commit v4 on v3

--- a/solution.py
+++ b/solution.py
@@ -297,7 +297,7 @@
         v = cv_ref[i * RB : (i + 1) * RB, :, h * HD : (h + 1) * HD].reshape(RB * cap, HD)
         acc_ref[i, h] = lax.dot_general(
             v, expo, CONTRACT_FIRST, preferred_element_type=jnp.float32
-        )
+        ).astype(jnp.bfloat16)
 
 
 def taken_at_once(batches):
@@ -315,7 +315,7 @@
         grid=(batches // n,),
         out_shape=(
             jax.ShapeDtypeStruct((batches, heads, many, HD), jnp.bfloat16),
-            jax.ShapeDtypeStruct((batches, heads, HD, many), jnp.float32),
+            jax.ShapeDtypeStruct((batches, heads, HD, many), jnp.bfloat16),
             jax.ShapeDtypeStruct((batches, heads, 2, many), jnp.float32),
         ),
         in_specs=[
@@ -335,119 +335,148 @@
     )(lengths, queries, cache_keys, cache_values)
 
 
-def merge_kernel(nx, parts_ref, near_ref, far_ref, *refs):
-    late_refs, (qp_ref, acc_ref, ml_ref, nv_ref, o_ref, nk_ref, held, eye) = refs[: nx - 1], refs[nx - 1 :]
-    step = pl.program_id(0)
+def merge_kernel(nx, taken, *refs):
+    count = nx + 6
+    sources, (out_ref, nk_ref), held_refs = refs[:count], refs[count : count + 2], refs[count + 2 :]
+    here, (o_ref, held, eye, sems) = held_refs[:count], held_refs[count:]
+    parts_ref, near_ref, far_ref = here[:3]
+    late_refs, (nv_ref, qp_ref, acc_ref, ml_ref) = here[3 : nx + 2], here[nx + 2 :]
     steps, batches = nk_ref.shape[0], nk_ref.shape[1]
-    taken, heads = acc_ref.shape[:2]
+    heads = acc_ref.shape[1]
     many = steps * GROUP * RB
     factor = 1.0 / math.sqrt(HD)
-
-    @pl.when(step == 0)
-    def _():
-        me = lax.axis_index("tx")
-        for x in range(nx):
-            for k in range(parts_ref.shape[2] // RB):
-                g = first_group(x, steps * batches, nx) + k
-                rows = slice(k * RB, (k + 1) * RB)
-                at = lax.rem(x + nx - me, nx)
-                total = near_ref[g * RB : (g + 1) * RB, :]
-                far = far_ref[rows, :]
-                for r, late_ref in enumerate(late_refs):
-                    far = jnp.where(at == r + 1, late_ref[rows, :], far)
-                total = total + far
-                for f in range(parts_ref.shape[0]):
-                    total = total + parts_ref[f, x, rows, :].astype(jnp.float32)
-                rounded = total.astype(jnp.bfloat16)
-                nk_ref[g // batches, g % batches] = rounded
-                held[g // batches, g % batches] = rounded.astype(jnp.float32)
-        line = lax.broadcasted_iota(jnp.int32, (many, many), 0)
-        lane = lax.broadcasted_iota(jnp.int32, (many, many), 1)
-        eye[...] = jnp.where(line == lane, 1.0, 0.0).astype(jnp.bfloat16)
+    groups = batches // taken
+
+    copies = [
+        pltpu.make_async_copy(sources[i], here[i], sems.at[i]) for i in range(count - 3)
+    ]
+    shares = []
+    for step in range(groups):
+        rows = pl.ds(step * taken, taken)
+        shares.append(
+            [
+                pltpu.make_async_copy(
+                    sources[i].at[rows], here[i].at[rows], sems.at[i + 3 * step]
+                )
+                for i in range(count - 3, count)
+            ]
+        )
+    for copy in [*copies, *(copy for share in shares for copy in share)]:
+        copy.start()
+
+    line = lax.broadcasted_iota(jnp.int32, (many, many), 0)
+    lane = lax.broadcasted_iota(jnp.int32, (many, many), 1)
+    eye[...] = jnp.where(line == lane, 1.0, 0.0).astype(jnp.bfloat16)
+    for copy in copies:
+        copy.wait()
+    me = lax.axis_index("tx")
+    for x in range(nx):
+        for k in range(parts_ref.shape[2] // RB):
+            g = first_group(x, steps * batches, nx) + k
+            rows = slice(k * RB, (k + 1) * RB)
+            at = lax.rem(x + nx - me, nx)
+            total = near_ref[g * RB : (g + 1) * RB, :]
+            far = far_ref[rows, :]
+            for r, late_ref in enumerate(late_refs):
+                far = jnp.where(at == r + 1, late_ref[rows, :], far)
+            total = total + far
+            for f in range(parts_ref.shape[0]):
+                total = total + parts_ref[f, x, rows, :].astype(jnp.float32)
+            rounded = total.astype(jnp.bfloat16)
+            nk_ref[g // batches, g % batches] = rounded
+            held[g // batches, g % batches] = rounded.astype(jnp.float32)
 
     key = lax.broadcasted_iota(jnp.int32, (steps * RB, many), 0)
     lane = lax.broadcasted_iota(jnp.int32, (steps * RB, many), 1)
     same_row = lax.rem(key, RB) == lax.rem(lane, RB)
     known = lax.div(key, RB) <= lax.div(lane, GROUP * RB)
     bias = jnp.where(same_row & known, 0.0, -1e30)
-    chains = [(i, h) for i in range(taken) for h in range(heads)]
-    scores = []
-    for i, h in chains:
-        lanes = slice(h * HD, (h + 1) * HD)
-        keys = jnp.concatenate([held[u, step * taken + i, :, lanes] for u in range(steps)], axis=0)
-        scores.append(
-            lax.dot_general(
-                keys.astype(jnp.bfloat16),
-                qp_ref[i, h],
-                CONTRACT_LAST,
-                preferred_element_type=jnp.float32,
+    leaving = []
+    for step in range(groups):
+        first = step * taken
+        for copy in shares[step]:
+            copy.wait()
+        chains = [(i, h) for i in range(first, first + taken) for h in range(heads)]
+        scores = []
+        for i, h in chains:
+            lanes = slice(h * HD, (h + 1) * HD)
+            keys = jnp.concatenate([held[u, i, :, lanes] for u in range(steps)], axis=0)
+            scores.append(
+                lax.dot_general(
+                    keys.astype(jnp.bfloat16),
+                    qp_ref[i, h],
+                    CONTRACT_LAST,
+                    preferred_element_type=jnp.float32,
+                )
+            )
+        added, scales = [], []
+        for (i, h), sn in zip(chains, scores):
+            lanes = slice(h * HD, (h + 1) * HD)
+            values = jnp.concatenate(
+                [nv_ref[u, i, :, lanes].astype(jnp.float32) for u in range(steps)], axis=0
+            )
+            sn = sn * factor + bias
+            old = ml_ref[i, h, 0:1, :]
+            top = jnp.maximum(old, jnp.max(sn, axis=0, keepdims=True))
+            keep = jnp.exp(old - top)
+            expo = jnp.exp(sn - top)
+            whole = ml_ref[i, h, 1:2, :] * keep + jnp.sum(expo, axis=0, keepdims=True)
+            inverse = 1.0 / whole
+            scales.append(keep * inverse)
+            added.append(
+                lax.dot_general(
+                    values.astype(jnp.bfloat16),
+                    (expo * inverse).astype(jnp.bfloat16),
+                    CONTRACT_FIRST,
+                    preferred_element_type=jnp.float32,
+                )
+            )
+        turned = [
+            (acc_ref[i, h].astype(jnp.float32) * scale + more).astype(jnp.bfloat16)
+            for (i, h), scale, more in zip(chains, scales, added)
+        ]
+        for (i, h), out in zip(chains, turned):
+            out = lax.dot_general(
+                eye[...], out, CONTRACT_LAST, preferred_element_type=jnp.float32
+            ).astype(jnp.bfloat16)
+            for s in range(steps):
+                for g in range(GROUP):
+                    at = (s * GROUP + g) * RB
+                    o_ref[s, i, :, (h * GROUP + g) * HD : (h * GROUP + g + 1) * HD] = out[
+                        at : at + RB
+                    ]
+        rows = pl.ds(first, taken)
+        leaving.append(
+            pltpu.make_async_copy(
+                o_ref.at[:, rows], out_ref.at[:, rows], sems.at[count + 3 * groups + step]
             )
         )
-    added, scales = [], []
-    for (i, h), sn in zip(chains, scores):
-        lanes = slice(h * HD, (h + 1) * HD)
-        values = jnp.concatenate(
-            [nv_ref[u, i, :, lanes].astype(jnp.float32) for u in range(steps)], axis=0
-        )
-        sn = sn * factor + bias
-        old = ml_ref[i, h, 0:1, :]
-        top = jnp.maximum(old, jnp.max(sn, axis=0, keepdims=True))
-        keep = jnp.exp(old - top)
-        expo = jnp.exp(sn - top)
-        whole = ml_ref[i, h, 1:2, :] * keep + jnp.sum(expo, axis=0, keepdims=True)
-        inverse = 1.0 / whole
-        scales.append(keep * inverse)
-        added.append(
-            lax.dot_general(
-                values.astype(jnp.bfloat16),
-                (expo * inverse).astype(jnp.bfloat16),
-                CONTRACT_FIRST,
-                preferred_element_type=jnp.float32,
-            )
-        )
-    turned = [
-        (acc_ref[i, h] * scale + more).astype(jnp.bfloat16)
-        for (i, h), scale, more in zip(chains, scales, added)
-    ]
-    for (i, h), out in zip(chains, turned):
-        out = lax.dot_general(
-            eye[...], out, CONTRACT_LAST, preferred_element_type=jnp.float32
-        ).astype(jnp.bfloat16)
-        for s in range(steps):
-            for g in range(GROUP):
-                at = (s * GROUP + g) * RB
-                o_ref[s, i, :, (h * GROUP + g) * HD : (h * GROUP + g + 1) * HD] = out[
-                    at : at + RB
-                ]
+        leaving[-1].start()
+    for copy in leaving:
+        copy.wait()
 
 
 def merge(parts, near, far, late, packed, sums, tops, new_values):
     batches, heads, many, _ = packed.shape
-    steps, _, _, cols = new_values.shape
+    steps = new_values.shape[0]
     width = many // steps // RB * heads * HD
     n = taken_at_once(batches)
+    made = jax.ShapeDtypeStruct((steps, batches, RB, width), jnp.bfloat16)
+    operands = [parts, near, far, *late, new_values, packed, sums, tops]
     return pl.pallas_call(
-        functools.partial(merge_kernel, parts.shape[1]),
-        grid=(batches // n,),
-        out_shape=(
-            jax.ShapeDtypeStruct((steps, batches, RB, width), jnp.bfloat16),
-            jax.ShapeDtypeStruct(new_values.shape, jnp.bfloat16),
+        functools.partial(merge_kernel, parts.shape[1], n),
+        out_shape=(made, jax.ShapeDtypeStruct(new_values.shape, jnp.bfloat16)),
+        in_specs=[pl.BlockSpec(memory_space=pl.ANY)] * len(operands),
+        out_specs=(
+            pl.BlockSpec(memory_space=pl.ANY),
+            pl.BlockSpec(memory_space=pltpu.VMEM),
         ),
-        in_specs=[
-            pl.BlockSpec(parts.shape, lambda i: (0, 0, 0, 0)),
-            *(pl.BlockSpec(part.shape, lambda i: (0, 0)) for part in (near, far, *late)),
-            pl.BlockSpec((n, heads, many, HD), lambda i: (i, 0, 0, 0)),
-            pl.BlockSpec((n, heads, HD, many), lambda i: (i, 0, 0, 0)),
-            pl.BlockSpec((n, heads, 2, many), lambda i: (i, 0, 0, 0)),
-            pl.BlockSpec((steps, n, RB, cols), lambda i: (0, i, 0, 0)),
-        ],
-        out_specs=(
-            pl.BlockSpec((steps, n, RB, width), lambda i: (0, i, 0, 0)),
-            pl.BlockSpec(new_values.shape, lambda i: (0, 0, 0, 0)),
-        ),
-        scratch_shapes=[
+        scratch_shapes=[pltpu.VMEM(operand.shape, operand.dtype) for operand in operands]
+        + [
+            pltpu.VMEM(made.shape, made.dtype),
             pltpu.VMEM(new_values.shape, jnp.float32),
             pltpu.VMEM((many, many), jnp.bfloat16),
+            pltpu.SemaphoreType.DMA((len(operands) + 4 * (batches // n),)),
         ],
         compiler_params=pltpu.CompilerParams(vmem_limit_bytes=GRANT),
         cost_estimate=pl.CostEstimate(
@@ -456,7 +485,7 @@
             transcendentals=packed.size // 8,
         ),
         name="attend_new",
-    )(parts, near, far, *late, packed, sums, tops, new_values)
+    )(*operands)
 
 
 def shift_of(nx, d):

time: 90.8 us -> 90.6 us (level)
  no operation moved by 1% of the time
where the time goes in v4:
time: 90.6 us; the launch traced here: 90.1 us
  waiting for transfers between devices  29.7 us (33%)
  Pallas kernels  26.9 us (30%)
  starting transfers between devices  17.6 us (19%)
  local copies, waits for them, and re-layouts  12.5 us (14%)
  other arithmetic  2.54 us (3%)
    ppermute x1, waiting for transfers between devices, per_device(): came = lax.ppermute(rows_of(flat, -d % nx), 'tx', shift_of(nx, d))  10.2 us
    pallas_call x2, Pallas kernels, base_product(): pl.pallas_call(functools.partial(base_kernel, plan), out_shape=tuple((jax...  9.67 us
    unnamed x41, local copies, waits for them, and re-layouts  9.15 us
    ppermute x1, waiting for transfers between devices, per_device(): came = lax.ppermute(piece, 'tx', shift_of(nx, d))  6.4 us
    all_to_all x1, starting transfers between devices, per_device(): mine = lax.all_to_all(mine, 'fsdp', 0, 0, tiled=True)  6.09 us
    pallas_call x1, Pallas kernels, cached(): pl.pallas_call(cached_kernel, grid=(batches // n,), out_shape=(jax.ShapeD...  5.27 us
    pallas_call x1, Pallas kernels, merge(): pl.pallas_call(functools.partial(merge_kernel, parts.shape[1], n), out_sh...  5.09 us
    ppermute x3, waiting for transfers between devices, per_device(): lax.ppermute((behind if d else sent)[e], ('tx', 'core'), to_shift(d, e))  4.98 us
  transfers between devices with their start and end apart: 12, of which 9 were waited for; matrix products, arithmetic and copies ran while one was open for 5% of the time, Pallas kernels for 22%

profile of v4, /device:TPU:0, one launch (start us, length us, event | category | flops | bytes accessed | tf_op | source)
XLA Modules:
  0.0 90.1 jit_solution(8131413961092088047)
XLA Ops:
  0.6 0.0 copy-start
  0.7 1.2 %constant_dynamic-slice_fusion.1 = bf16[72,4096]{1,0:T(8,128)(2,1)S(1)} fusion(bf16[144,4096]{1,0:T(8,128)(2,1)} %bitcast.21, s32[]{:T(128)S(6)} %mul.28), kind=kLoop, calls=%fused_computation.7 | loop fusion | bytes 1179652 | tf_op jit(solution)/shard_map/dynamic_slice | solution.py:500
  1.9 3.0 %collective-permute-start.1 = (bf16[72,4096]{1,0:T(8,128)(2,1)S(1)}, bf16[72,4096]{1,0:T(8,128)(2,1)S(1)}, u32[]{:S(2)}, u32[]{:S(2)}) collective-permute-start(bf16[72,4096]{1,0:T(8,128)(2,1)S(1)} %constant_dynamic-slice_fusion.1), channel_id=1, source_target_pairs={{0,2},{2,0},{1,3},{3,1},{4,6},{6,4},{5,7},{7,5},{8,10},{10,8},{9,1... | collective-permute-start | bytes 1769480 | tf_op jit(solution)/shard_map/ppermute | solution.py:557
  4.9 0.1 copy.12
  5.0 0.2 collective-permute-start.2
  5.1 1.3 %dynamic-slice_bitcast_fusion.1 = (bf16[1,512,256]{2,1,0:T(8,128)(2,1)S(1)}, bf16[1,512,256]{2,1,0:T(8,128)(2,1)S(1)}, bf16[1,512,256]{2,1,0:T(8,128)(2,1)S(1)}, bf16[1,512,256]{2,1,0:T(8,128)(2,1)S(1)}) fusion(bf16[512,1024]{1,0:T(8,128)(2,1)} %param.17, s32[]{:T(128)S(6)} %mul.31, s32[]{:T(128)S(6)} %mul.30, s32[]{:T(128)S(6)} %mul.29, s32[]{:T(128)S(6)} %mul.32), kind=kLoop, calls=%fused_computation.3 | loop fusion | bytes 2097168 | tf_op jit(solution)/shard_map/stack | solution.py:543
  6.4 0.0 copy-start.13
  6.4 0.8 pad_maximum_fusion.1
  7.3 0.8 pad_maximum_fusion.refs_2_
  8.1 10.2 %collective-permute-done.1.refs_2_ = bf16[72,4096]{1,0:T(8,128)(2,1)S(1)} collective-permute-done((bf16[72,4096]{1,0:T(8,128)(2,1)S(1)}, bf16[72,4096]{1,0:T(8,128)(2,1)S(1)}, u32[]{:S(2)}, u32[]{:S(2)}) %collective-permute-start.1) | collective-permute-done | bytes 589856 | tf_op jit(solution)/shard_map/ppermute | solution.py:557
  18.3 0.1 collective-permute-done.2.refs_1_
  18.4 0.0 collective-permute-start.3
  18.4 2.0 %collective-permute-done.3.refs_3_ = bf16[72,4096]{1,0:T(8,128)(2,1)S(1)} collective-permute-done((bf16[72,4096]{1,0:T(8,128)(2,1)S(1)}, bf16[72,4096]{1,0:T(8,128)(2,1)S(1)}, u32[]{:S(2)}, u32[]{:S(2)}) %collective-permute-start.3) | collective-permute-done | bytes 589856 | tf_op jit(solution)/shard_map/ppermute | solution.py:508
  20.4 0.0 collective-permute-done.refs_1_
  20.4 2.2 %scatter_columns.1 = bf16[8,72,1024]{2,1,0:T(8,128)(2,1)} custom-call(s32[128]{0:T(128)S(1)} %copy-done.13, bf16[2,72,4096]{2,1,0:T(8,128)(2,1)S(1)} %copy-done, bf16[2,72,4096]{2,1,0:T(8,128)(2,1)S(1)} %bitcast.25, bf16[72,4096]{1,0:T(8,128)(2,1)S(1)} %collective-permute-done.1.refs_2_, bf16[72,4096]{1,0:T(8,128)(2,1)S(1)} %collective-permute-done.3.refs_3_), custom_call_target="tpu_custom_call" | custom-call | bytes 3538944 | tf_op jit(solution)/shard_map/scatter_columns/pallas_call | solution.py:85
  22.6 6.1 %all-to-all-start = ((bf16[8,72,1024]{2,1,0:T(8,128)(2,1)}), bf16[8,72,1024]{2,1,0:T(8,128)(2,1)S(1)}, u32[]{:S(2)}, u32[]{:S(2)}) async-start(bf16[8,72,1024]{2,1,0:T(8,128)(2,1)} %scatter_columns.1), calls=%async_computation | async-start | bytes 2359296 | tf_op jit(solution)/shard_map/all_to_all | solution.py:612
  28.7 1.6 %collective-permute-start.5 = (bf16[2,512,256]{2,1,0:T(8,128)(2,1)}, bf16[2,512,256]{2,1,0:T(8,128)(2,1)S(1)}, u32[]{:S(2)}, u32[]{:S(2)}) collective-permute-start(bf16[2,512,256]{2,1,0:T(8,128)(2,1)} %pad_maximum_fusion.refs_2_), channel_id=1, source_target_pairs={{0,2},{1,3},{2,0},{3,1},{4,6},{5,7},{6,4},{7,5},{8,10},{9,11},{10,... | collective-permute-start | bytes 1572872 | tf_op jit(solution)/shard_map/ppermute | solution.py:572
  30.3 0.3 collective-permute-start.6
  30.6 0.1 pad_add_fusion.info_ref
  30.6 0.3 collective-permute-done.4.refs_3_
  30.9 1.0 %copy-done.2 = bf16[2,512,256]{2,1,0:T(8,128)(2,1)S(1)} copy-done((bf16[2,512,256]{2,1,0:T(8,128)(2,1)S(1)}, bf16[2,512,256]{2,1,0:T(8,128)(2,1)}, u32[]{:S(2)}) %copy-start.2) | copy-done | bytes 524312
  32.0 1.3 %scale_rows.2 = (bf16[2,512,256]{2,1,0:T(8,128)(2,1)S(1)}, bf16[2,512,256]{2,1,0:T(8,128)(2,1)S(1)}) custom-call(f32[16,2]{1,0:T(8,128)S(1)} %convert_element_type.3.refs_0_, f32[16,2]{1,0:T(8,128)S(1)} %collective-permute-done.2.refs_1_, bf16[2,512,256]{2,1,0:T(8,128)(2,1)S(1)} %copy-done.2, bf16[2,512,256]{2,1,0:T(8,128)(2,1)} %collective-permute-done.4.refs_3_), custom_call_target="tpu_custom_call" | custom-call | bytes 1024 | tf_op jit(solution)/shard_map/scale_rows/pallas_call | solution.py:193
  33.3 0.8 copy-done.4
  34.1 0.8 copy-done.6
  34.9 0.9 constant_dynamic-slice_fusion
  35.7 5.4 %base_keys.2 = (f32[144,256]{1,0:T(8,128)S(1)}, f32[72,256]{1,0:T(8,128)S(1)}) custom-call(s32[4]{0:T(128)S(1)} %pad_add_fusion.info_ref, bf16[16384,256]{1,0:T(8,128)(2,1)} %base_ref.3, bf16[144,4096]{1,0:T(8,128)(2,1)} %bitcast.22, bf16[144,4096]{1,0:T(8,128)(2,1)} %copy-done.1, bf16[72,4096]{1,0:T(8,128)(2,1)S(1)} %collective-permute-done.1.refs_2_, ...), custom_call_target="tpu_custom_call" | custom-call | bytes 1024 | tf_op jit(solution)/shard_map/base_keys/pallas_call | solution.py:151
  41.2 0.7 copy-done.10
  41.8 0.6 copy-done.11
  42.4 5.3 %attend_cached.1 = (bf16[9,2,256,128]{3,2,1,0:T(8,128)(2,1)S(1)}, bf16[9,2,128,256]{3,2,1,0:T(8,128)(2,1)}, f32[9,2,2,256]{3,2,1,0:T(2,128)S(1)}) custom-call(s32[72]{0:T(128)S(1)} %copy-done.14, bf16[2,9,8,4096]{3,2,1,0:T(8,128)(2,1)} %bitcast.29, bf16[72,32,256]{2,1,0:T(8,128)(2,1)} %ck_ref.1, bf16[72,32,256]{2,1,0:T(8,128)(2,1)} %cv_ref.1), custom_call_target="tpu_custom_call" | custom-call | bytes 1024 | tf_op jit(solution)/shard_map/attend_cached/pallas_call | solution.py:313
  47.7 1.0 %copy-done.3 = bf16[9,2,256,128]{3,2,1,0:T(8,128)(2,1)} copy-done((bf16[9,2,256,128]{3,2,1,0:T(8,128)(2,1)}, bf16[9,2,256,128]{3,2,1,0:T(8,128)(2,1)S(1)}, u32[]{:S(2)}) %copy-start.3) | copy-done | bytes 1179672
  48.7 0.6 copy-done.12
  49.3 4.7 %collective-permute-done.6.refs_3_ = bf16[2,512,256]{2,1,0:T(8,128)(2,1)S(1)} collective-permute-done((bf16[2,512,256]{2,1,0:T(8,128)(2,1)}, bf16[2,512,256]{2,1,0:T(8,128)(2,1)S(1)}, u32[]{:S(2)}, u32[]{:S(2)}) %collective-permute-start.6) | collective-permute-done | bytes 524320 | tf_op jit(solution)/shard_map/ppermute | solution.py:572
  54.0 1.0 %scale_rows.3 = (bf16[2,512,256]{2,1,0:T(8,128)(2,1)S(1)}, bf16[2,512,256]{2,1,0:T(8,128)(2,1)S(1)}) custom-call(f32[16,2]{1,0:T(8,128)S(1)} %convert_element_type.3.refs_0_, f32[16,2]{1,0:T(8,128)S(1)} %collective-permute-done.2.refs_1_, bf16[2,512,256]{2,1,0:T(8,128)(2,1)S(1)} %collective-permute-done.5.refs_2_, ...), custom_call_target="tpu_custom_call" | custom-call | bytes 1024 | tf_op jit(solution)/shard_map/scale_rows/pallas_call | solution.py:193
  55.1 0.8 copy-done.8
  55.8 1.7 %all-to-all-done = bf16[8,72,1024]{2,1,0:T(8,128)(2,1)S(1)} async-done(((bf16[8,72,1024]{2,1,0:T(8,128)(2,1)}), bf16[8,72,1024]{2,1,0:T(8,128)(2,1)S(1)}, u32[]{:S(2)}, u32[]{:S(2)}) %all-to-all-start) | async-done | bytes 1179680 | tf_op jit(solution)/shard_map/all_to_all | solution.py:612
  57.6 1.6 %collective-permute-start.8 = (bf16[72,4096]{1,0:T(8,128)(2,1)S(1)}, bf16[72,4096]{1,0:T(8,128)(2,1)S(1)}, u32[]{:S(2)}, u32[]{:S(2)}) collective-permute-start(bf16[72,4096]{1,0:T(8,128)(2,1)S(1)} %copy-done.18), channel_id=1, source_target_pairs={{0,2},{2,0},{1,3},{3,1},{4,6},{6,4},{5,7},{7,5},{8,10},{10,8},{9,1... | collective-permute-start | bytes 1769480 | tf_op jit(solution)/shard_map/ppermute | solution.py:593
  59.1 1.0 %copy-done.9 = bf16[2,512,256]{2,1,0:T(8,128)(2,1)S(1)} copy-done((bf16[2,512,256]{2,1,0:T(8,128)(2,1)S(1)}, bf16[2,512,256]{2,1,0:T(8,128)(2,1)}, u32[]{:S(2)}) %copy-start.9) | copy-done | bytes 524312
  60.2 0.8 partial_keys.2.refs_3_
  61.0 1.6 %partial_keys.3 = bf16[8,2,72,256]{3,2,1,0:T(8,128)(2,1)} custom-call(bf16[576,1024]{1,0:T(8,128)(2,1)S(1)} %collective-permute-done.7.refs_0_, bf16[2,512,256]{2,1,0:T(8,128)(2,1)S(1)} %copy-done.5, bf16[2,512,256]{2,1,0:T(8,128)(2,1)S(1)} %get-tuple-element.60.refs_2_, f32[2,576,256]{2,1,0:T(8,128)S(1)} %partial_keys.2.refs_3_), custom_call_target="tpu_custom_call" | custom-call | flops 603979776 | bytes 3997696 | tf_op jit(solution)/shard_map/partial_keys/pallas_call | solution.py:237
  62.6 5.0 %all-to-all-start.1 = ((bf16[16,72,256]{2,1,0:T(8,128)(2,1)}), bf16[16,72,256]{2,1,0:T(8,128)(2,1)S(1)}, u32[]{:S(2)}, u32[]{:S(2)}) async-start(bf16[16,72,256]{2,1,0:T(8,128)(2,1)} %bitcast.12), calls=%async_computation.1 | async-start | bytes 1179648 | tf_op jit(solution)/shard_map/all_to_all | solution.py:622
  67.5 6.4 %collective-permute-done.8.refs_0_ = bf16[72,4096]{1,0:T(8,128)(2,1)S(1)} collective-permute-done((bf16[72,4096]{1,0:T(8,128)(2,1)S(1)}, bf16[72,4096]{1,0:T(8,128)(2,1)S(1)}, u32[]{:S(2)}, u32[]{:S(2)}) %collective-permute-start.8) | collective-permute-done | bytes 589856 | tf_op jit(solution)/shard_map/ppermute | solution.py:593
  74.0 0.8 pad_add_fusion.1.info_ref
  74.7 1.2 %collective-permute-done.9.refs_1_ = bf16[72,4096]{1,0:T(8,128)(2,1)S(1)} collective-permute-done((bf16[72,4096]{1,0:T(8,128)(2,1)S(1)}, bf16[72,4096]{1,0:T(8,128)(2,1)S(1)}, u32[]{:S(2)}, u32[]{:S(2)}) %collective-permute-start.9) | collective-permute-done | bytes 589856 | tf_op jit(solution)/shard_map/ppermute | solution.py:508
  76.0 0.8 copy-done.17
  76.8 4.3 %base_keys.3.refs_3_ = f32[72,256]{1,0:T(8,128)} custom-call(s32[2]{0:T(128)} %pad_add_fusion.1.info_ref, bf16[16384,256]{1,0:T(8,128)(2,1)} %base_ref.3, bf16[72,4096]{1,0:T(8,128)(2,1)} %copy-done.16, bf16[72,4096]{1,0:T(8,128)(2,1)} %copy-done.17), custom_call_target="tpu_custom_call" | custom-call | bytes 1024 | tf_op jit(solution)/shard_map/base_keys/pallas_call | solution.py:151
  81.1 3.1 %all-to-all-done.1 = bf16[16,72,256]{2,1,0:T(8,128)(2,1)S(1)} async-done(((bf16[16,72,256]{2,1,0:T(8,128)(2,1)}), bf16[16,72,256]{2,1,0:T(8,128)(2,1)S(1)}, u32[]{:S(2)}, u32[]{:S(2)}) %all-to-all-start.1) | async-done | bytes 589856 | tf_op jit(solution)/shard_map/all_to_all | solution.py:622
  84.2 0.8 copy-done.15
  85.0 5.1 %attend_new.1 = (bf16[2,9,8,4096]{3,2,1,0:T(8,128)(2,1)}, bf16[2,9,8,256]{3,2,1,0:T(8,128)(2,1)}) custom-call(bf16[8,2,72,256]{3,2,1,0:T(8,128)(2,1)} %bitcast.28, f32[144,256]{1,0:T(8,128)} %copy-done.10, f32[72,256]{1,0:T(8,128)} %copy-done.11, f32[72,256]{1,0:T(8,128)} %base_keys.3.refs_3_, bf16[2,9,8,256]{3,2,1,0:T(8,128)(2,1)} %bitcast.30, ...), custom_call_target="tpu_custom_call" | custom-call | flops 603979776 | bytes 5898240 | tf_op jit(solution)/shard_map/attend_new/pallas_call | solution.py:466
  (34 shorter events, 0.1 us)
Async XLA Ops:
  0.6 4.2 %copy-start = (bf16[2,72,4096]{2,1,0:T(8,128)(2,1)S(1)}, bf16[2,72,4096]{2,1,0:T(8,128)(2,1)}, u32[]{:S(2)}) copy-start(bf16[2,72,4096]{2,1,0:T(8,128)(2,1)} %refs_0_.1) | copy-start | bytes 3538948
  0.6 4.2 %copy-start.19 = (bf16[16,2]{0,1:T(2,128)(2,1)S(1)}, bf16[16,2]{0,1:T(2,128)(2,1)}, u32[]{:S(2)}) copy-start(bf16[16,2]{0,1:T(2,128)(2,1)} %param.18) | copy-start | bytes 196
  1.9 16.4 %collective-permute-start.1 = (bf16[72,4096]{1,0:T(8,128)(2,1)S(1)}, bf16[72,4096]{1,0:T(8,128)(2,1)S(1)}, u32[]{:S(2)}, u32[]{:S(2)}) collective-permute-start(bf16[72,4096]{1,0:T(8,128)(2,1)S(1)} %constant_dynamic-slice_fusion.1), channel_id=1, source_target_pairs={{0,2},{2,0},{1,3},{3,1},{4,6},{6,4},{5,7},{7,5},{8,10},{10,8},{9,1... | collective-permute-start | bytes 1769480 | tf_op jit(solution)/shard_map/ppermute | solution.py:557
  4.9 15.5 %collective-permute-start = (bf16[144,4096]{1,0:T(8,128)(2,1)S(1)}, bf16[144,4096]{1,0:T(8,128)(2,1)S(1)}, u32[]{:S(2)}, u32[]{:S(2)}) collective-permute-start(bf16[144,4096]{1,0:T(8,128)(2,1)S(1)} %bitcast.23), channel_id=1, source_target_pairs={{0,1},{1,0},{2,3},{3,2},{4,5},{5,4},{6,7},{7,6},{8,9},{9,8},{10,11... | collective-permute-start | bytes 3538952 | tf_op jit(solution)/shard_map/ppermute | solution.py:508
  5.0 13.4 %collective-permute-start.2 = (f32[16,2]{1,0:T(8,128)S(1)}, f32[16,2]{1,0:T(8,128)S(1)}, u32[]{:S(2)}, u32[]{:S(2)}) collective-permute-start(f32[16,2]{1,0:T(8,128)S(1)} %convert_element_type.3.refs_0_), channel_id=1, source_target_pairs={{0,2},{2,0},{1,3},{3,1},{4,6},{6,4},{5,7},{7,5},{8,10},{10,8},{9,1... | collective-permute-start | bytes 392 | tf_op jit(solution)/shard_map/ppermute | solution.py:546
  6.4 14.0 %copy-start.13 = (s32[128]{0:T(128)S(1)}, s32[128]{0:T(128)}, u32[]{:S(2)}) copy-start(s32[128]{0:T(128)} %order_ref.1) | copy-start | bytes 1540
  18.4 2.0 %collective-permute-start.3 = (bf16[72,4096]{1,0:T(8,128)(2,1)S(1)}, bf16[72,4096]{1,0:T(8,128)(2,1)S(1)}, u32[]{:S(2)}, u32[]{:S(2)}) collective-permute-start(bf16[72,4096]{1,0:T(8,128)(2,1)S(1)} %collective-permute-done.1.refs_2_), channel_id=1, source_target_pairs={{0,1},{1,0},{2,3},{3,2},{4,5},{5,4},{6,7},{7,6},{8,9},{9,8},{10,11... | collective-permute-start | bytes 1769480 | tf_op jit(solution)/shard_map/ppermute | solution.py:508
  20.4 2.2 %copy-start.1 = (bf16[144,4096]{1,0:T(8,128)(2,1)}, bf16[144,4096]{1,0:T(8,128)(2,1)S(1)}, u32[]{:S(2)}) copy-start(bf16[144,4096]{1,0:T(8,128)(2,1)S(1)} %collective-permute-done.refs_1_) | copy-start | bytes 3538948
  22.6 35.0 %all-to-all-start = ((bf16[8,72,1024]{2,1,0:T(8,128)(2,1)}), bf16[8,72,1024]{2,1,0:T(8,128)(2,1)S(1)}, u32[]{:S(2)}, u32[]{:S(2)}) async-start(bf16[8,72,1024]{2,1,0:T(8,128)(2,1)} %scatter_columns.1), calls=%async_computation | async-start | bytes 2359296 | tf_op jit(solution)/shard_map/all_to_all | solution.py:612
  28.7 2.3 %collective-permute-start.4 = (bf16[2,512,256]{2,1,0:T(8,128)(2,1)}, bf16[2,512,256]{2,1,0:T(8,128)(2,1)}, u32[]{:S(2)}, u32[]{:S(2)}) collective-permute-start(bf16[2,512,256]{2,1,0:T(8,128)(2,1)} %pad_maximum_fusion.1), channel_id=1, source_target_pairs={{0,1},{1,0},{2,3},{3,2},{4,5},{5,4},{6,7},{7,6},{8,9},{9,8},{10,11... | collective-permute-start | bytes 1572872 | tf_op jit(solution)/shard_map/ppermute | solution.py:572
  28.7 20.6 %collective-permute-start.5 = (bf16[2,512,256]{2,1,0:T(8,128)(2,1)}, bf16[2,512,256]{2,1,0:T(8,128)(2,1)S(1)}, u32[]{:S(2)}, u32[]{:S(2)}) collective-permute-start(bf16[2,512,256]{2,1,0:T(8,128)(2,1)} %pad_maximum_fusion.refs_2_), channel_id=1, source_target_pairs={{0,2},{1,3},{2,0},{3,1},{4,6},{5,7},{6,4},{7,5},{8,10},{9,11},{10,... | collective-permute-start | bytes 1572872 | tf_op jit(solution)/shard_map/ppermute | solution.py:572
  30.3 23.7 %collective-permute-start.6 = (bf16[2,512,256]{2,1,0:T(8,128)(2,1)}, bf16[2,512,256]{2,1,0:T(8,128)(2,1)S(1)}, u32[]{:S(2)}, u32[]{:S(2)}) collective-permute-start(bf16[2,512,256]{2,1,0:T(8,128)(2,1)} %pad_maximum_fusion.1), channel_id=1, source_target_pairs={{0,3},{1,2},{2,1},{3,0},{4,7},{5,6},{6,5},{7,4},{8,11},{9,10},{10,... | collective-permute-start | bytes 1572872 | tf_op jit(solution)/shard_map/ppermute | solution.py:572
  30.9 1.0 %copy-start.2 = (bf16[2,512,256]{2,1,0:T(8,128)(2,1)S(1)}, bf16[2,512,256]{2,1,0:T(8,128)(2,1)}, u32[]{:S(2)}) copy-start(bf16[2,512,256]{2,1,0:T(8,128)(2,1)} %pad_maximum_fusion.refs_2_) | copy-start | bytes 1572868
  33.3 0.8 copy-start.4
  34.1 0.8 copy-start.6
  35.7 6.7 %copy-start.14 = (s32[72]{0:T(128)S(1)}, s32[72]{0:T(128)}, u32[]{:S(2)}) copy-start(s32[72]{0:T(128)} %len_ref) | copy-start | bytes 868
  41.1 0.7 copy-start.10
  41.8 0.6 copy-start.11
  42.4 15.1 %copy-start.18 = (bf16[72,4096]{1,0:T(8,128)(2,1)S(1)}, bf16[72,4096]{1,0:T(8,128)(2,1)}, u32[]{:S(2)}) copy-start(bf16[72,4096]{1,0:T(8,128)(2,1)} %constant_dynamic-slice_fusion) | copy-start | bytes 1769476
  47.7 1.0 %copy-start.3 = (bf16[9,2,256,128]{3,2,1,0:T(8,128)(2,1)}, bf16[9,2,256,128]{3,2,1,0:T(8,128)(2,1)S(1)}, u32[]{:S(2)}) copy-start(bf16[9,2,256,128]{3,2,1,0:T(8,128)(2,1)S(1)} %get-tuple-element.53.refs_5_) | copy-start | bytes 3538948
  48.7 0.6 copy-start.12
  49.3 9.8 %copy-start.7 = (bf16[2,512,256]{2,1,0:T(8,128)(2,1)S(1)}, bf16[2,512,256]{2,1,0:T(8,128)(2,1)}, u32[]{:S(2)}) copy-start(bf16[2,512,256]{2,1,0:T(8,128)(2,1)} %copy-done.6) | copy-start | bytes 1572868
  55.0 0.8 copy-start.8
  57.6 3.4 %copy-start.5 = (bf16[2,512,256]{2,1,0:T(8,128)(2,1)S(1)}, bf16[2,512,256]{2,1,0:T(8,128)(2,1)}, u32[]{:S(2)}) copy-start(bf16[2,512,256]{2,1,0:T(8,128)(2,1)} %copy-done.4) | copy-start | bytes 1572868
  57.6 3.4 %collective-permute-start.7 = (bf16[576,1024]{1,0:T(8,128)(2,1)S(1)}, bf16[576,1024]{1,0:T(8,128)(2,1)S(1)}, u32[]{:S(2)}, u32[]{:S(2)}) collective-permute-start(bf16[576,1024]{1,0:T(8,128)(2,1)S(1)} %bitcast.26), channel_id=1, source_target_pairs={{0,1},{1,0},{2,3},{3,2},{4,5},{5,4},{6,7},{7,6},{8,9},{9,8},{10,11... | collective-permute-start | bytes 3538952 | tf_op jit(solution)/shard_map/ppermute | solution.py:508
  57.6 16.4 %collective-permute-start.8 = (bf16[72,4096]{1,0:T(8,128)(2,1)S(1)}, bf16[72,4096]{1,0:T(8,128)(2,1)S(1)}, u32[]{:S(2)}, u32[]{:S(2)}) collective-permute-start(bf16[72,4096]{1,0:T(8,128)(2,1)S(1)} %copy-done.18), channel_id=1, source_target_pairs={{0,2},{2,0},{1,3},{3,1},{4,6},{6,4},{5,7},{7,5},{8,10},{10,8},{9,1... | collective-permute-start | bytes 1769480 | tf_op jit(solution)/shard_map/ppermute | solution.py:593
  59.1 1.0 %copy-start.9 = (bf16[2,512,256]{2,1,0:T(8,128)(2,1)S(1)}, bf16[2,512,256]{2,1,0:T(8,128)(2,1)}, u32[]{:S(2)}) copy-start(bf16[2,512,256]{2,1,0:T(8,128)(2,1)} %copy-done.8) | copy-start | bytes 1572868
  62.6 21.6 %all-to-all-start.1 = ((bf16[16,72,256]{2,1,0:T(8,128)(2,1)}), bf16[16,72,256]{2,1,0:T(8,128)(2,1)S(1)}, u32[]{:S(2)}, u32[]{:S(2)}) async-start(bf16[16,72,256]{2,1,0:T(8,128)(2,1)} %bitcast.12), calls=%async_computation.1 | async-start | bytes 1179648 | tf_op jit(solution)/shard_map/all_to_all | solution.py:622
  74.0 2.0 %copy-start.16 = (bf16[72,4096]{1,0:T(8,128)(2,1)}, bf16[72,4096]{1,0:T(8,128)(2,1)S(1)}, u32[]{:S(2)}) copy-start(bf16[72,4096]{1,0:T(8,128)(2,1)S(1)} %collective-permute-done.8.refs_0_) | copy-start | bytes 1769476
  74.0 2.0 %collective-permute-start.9 = (bf16[72,4096]{1,0:T(8,128)(2,1)S(1)}, bf16[72,4096]{1,0:T(8,128)(2,1)S(1)}, u32[]{:S(2)}, u32[]{:S(2)}) collective-permute-start(bf16[72,4096]{1,0:T(8,128)(2,1)S(1)} %collective-permute-done.8.refs_0_), channel_id=1, source_target_pairs={{0,1},{1,0},{2,3},{3,2},{4,5},{5,4},{6,7},{7,6},{8,9},{9,8},{10,11... | collective-permute-start | bytes 1769480 | tf_op jit(solution)/shard_map/ppermute | solution.py:508
  76.0 0.8 copy-start.17
  84.2 0.8 copy-start.15

commit v5 on v4

--- a/solution.py
+++ b/solution.py
@@ -297,7 +297,7 @@
         v = cv_ref[i * RB : (i + 1) * RB, :, h * HD : (h + 1) * HD].reshape(RB * cap, HD)
         acc_ref[i, h] = lax.dot_general(
             v, expo, CONTRACT_FIRST, preferred_element_type=jnp.float32
-        ).astype(jnp.bfloat16)
+        )
 
 
 def taken_at_once(batches):
@@ -315,7 +315,7 @@
         grid=(batches // n,),
         out_shape=(
             jax.ShapeDtypeStruct((batches, heads, many, HD), jnp.bfloat16),
-            jax.ShapeDtypeStruct((batches, heads, HD, many), jnp.bfloat16),
+            jax.ShapeDtypeStruct((batches, heads, HD, many), jnp.float32),
             jax.ShapeDtypeStruct((batches, heads, 2, many), jnp.float32),
         ),
         in_specs=[
@@ -432,7 +432,7 @@
                 )
             )
         turned = [
-            (acc_ref[i, h].astype(jnp.float32) * scale + more).astype(jnp.bfloat16)
+            (acc_ref[i, h] * scale + more).astype(jnp.bfloat16)
             for (i, h), scale, more in zip(chains, scales, added)
         ]
         for (i, h), out in zip(chains, turned):
@@ -608,7 +608,7 @@
     if split > 1:
         for earlier in (near, far, share[0]):
             scales = after(scales, earlier)
-        ws[2:] = scale_rows(scales, shifts[2:], ws[2:])
+        ws[2:] = scale_rows(scales, shifts[:1:-1], ws[:1:-1])[::-1]
     mine = lax.all_to_all(mine, "fsdp", 0, 0, tiled=True)
     xs = [mine.reshape(nf * count * RB, depth // split)]
     for earlier in (*arrived[:1], *ws[-2:], near, far, share[0]):

time: 90.6 us -> 90.8 us (level)
  transfers between devices with their start and end apart: 12 -> 12, of which waited for: 9 -> 8; matrix products, arithmetic and copies ran while one was open for 5% -> 5% of each run, Pallas kernels for 22% -> 22%
where the time goes in v5:
time: 90.8 us; the launch traced here: 90.3 us
  waiting for transfers between devices  29.2 us (32%)
  Pallas kernels  27.2 us (30%)
  starting transfers between devices  18.1 us (20%)
  local copies, waits for them, and re-layouts  12.5 us (14%)
  other arithmetic  2.49 us (3%)
    ppermute x1, waiting for transfers between devices, per_device(): came = lax.ppermute(rows_of(flat, -d % nx), 'tx', shift_of(nx, d))  10.1 us
    pallas_call x2, Pallas kernels, base_product(): pl.pallas_call(functools.partial(base_kernel, plan), out_shape=tuple((jax...  9.66 us
    unnamed x41, local copies, waits for them, and re-layouts  9.15 us
    ppermute x1, waiting for transfers between devices, per_device(): came = lax.ppermute(piece, 'tx', shift_of(nx, d))  6.5 us
    all_to_all x1, starting transfers between devices, per_device(): mine = lax.all_to_all(mine, 'fsdp', 0, 0, tiled=True)  6.09 us
    pallas_call x1, Pallas kernels, cached(): pl.pallas_call(cached_kernel, grid=(batches // n,), out_shape=(jax.ShapeD...  5.49 us
    pallas_call x1, Pallas kernels, merge(): pl.pallas_call(functools.partial(merge_kernel, parts.shape[1], n), out_sh...  5.23 us
    all_to_all x1, starting transfers between devices, per_device(): lax.all_to_all(partial.reshape(nf * nx, count * RB, cols), ('fsdp', 'tx')...  5.11 us
  transfers between devices with their start and end apart: 12, of which 8 were waited for; matrix products, arithmetic and copies ran while one was open for 5% of the time, Pallas kernels for 22%

profile of v5, /device:TPU:0, one launch (start us, length us, event | category | flops | bytes accessed | tf_op | source)
XLA Modules:
  0.0 90.3 jit_solution(7339584488102871055)
XLA Ops:
  0.6 0.0 copy-start
  0.7 1.2 %constant_dynamic-slice_fusion.1 = bf16[72,4096]{1,0:T(8,128)(2,1)S(1)} fusion(bf16[144,4096]{1,0:T(8,128)(2,1)} %bitcast.21, s32[]{:T(128)S(6)} %mul.28), kind=kLoop, calls=%fused_computation.7 | loop fusion | bytes 1179652 | tf_op jit(solution)/shard_map/dynamic_slice | solution.py:500
  1.9 3.0 %collective-permute-start.1 = (bf16[72,4096]{1,0:T(8,128)(2,1)S(1)}, bf16[72,4096]{1,0:T(8,128)(2,1)S(1)}, u32[]{:S(2)}, u32[]{:S(2)}) collective-permute-start(bf16[72,4096]{1,0:T(8,128)(2,1)S(1)} %constant_dynamic-slice_fusion.1), channel_id=1, source_target_pairs={{0,2},{2,0},{1,3},{3,1},{4,6},{6,4},{5,7},{7,5},{8,10},{10,8},{9,1... | collective-permute-start | bytes 1769480 | tf_op jit(solution)/shard_map/ppermute | solution.py:557
  4.9 0.0 collective-permute-start
  4.9 0.1 copy.12
  5.0 0.2 collective-permute-start.2
  5.1 1.3 %dynamic-slice_bitcast_fusion.1 = (bf16[1,512,256]{2,1,0:T(8,128)(2,1)S(1)}, bf16[1,512,256]{2,1,0:T(8,128)(2,1)S(1)}, bf16[1,512,256]{2,1,0:T(8,128)(2,1)S(1)}, bf16[1,512,256]{2,1,0:T(8,128)(2,1)S(1)}) fusion(bf16[512,1024]{1,0:T(8,128)(2,1)} %param.17, s32[]{:T(128)S(6)} %mul.31, s32[]{:T(128)S(6)} %mul.30, s32[]{:T(128)S(6)} %mul.29, s32[]{:T(128)S(6)} %mul.32), kind=kLoop, calls=%fused_computation.3 | loop fusion | bytes 2097168 | tf_op jit(solution)/shard_map/stack | solution.py:543
  6.4 0.0 copy-start.13
  6.4 0.9 pad_maximum_fusion.1
  7.3 0.9 pad_maximum_fusion.refs_2_
  8.1 10.1 %collective-permute-done.1.refs_2_ = bf16[72,4096]{1,0:T(8,128)(2,1)S(1)} collective-permute-done((bf16[72,4096]{1,0:T(8,128)(2,1)S(1)}, bf16[72,4096]{1,0:T(8,128)(2,1)S(1)}, u32[]{:S(2)}, u32[]{:S(2)}) %collective-permute-start.1) | collective-permute-done | bytes 589856 | tf_op jit(solution)/shard_map/ppermute | solution.py:557
  18.3 0.1 collective-permute-done.2.refs_1_
  18.4 2.0 %collective-permute-done.3.refs_3_ = bf16[72,4096]{1,0:T(8,128)(2,1)S(1)} collective-permute-done((bf16[72,4096]{1,0:T(8,128)(2,1)S(1)}, bf16[72,4096]{1,0:T(8,128)(2,1)S(1)}, u32[]{:S(2)}, u32[]{:S(2)}) %collective-permute-start.3) | collective-permute-done | bytes 589856 | tf_op jit(solution)/shard_map/ppermute | solution.py:508
  20.4 2.2 %scatter_columns.1 = bf16[8,72,1024]{2,1,0:T(8,128)(2,1)} custom-call(s32[128]{0:T(128)S(1)} %copy-done.13, bf16[2,72,4096]{2,1,0:T(8,128)(2,1)S(1)} %copy-done, bf16[2,72,4096]{2,1,0:T(8,128)(2,1)S(1)} %bitcast.25, bf16[72,4096]{1,0:T(8,128)(2,1)S(1)} %collective-permute-done.1.refs_2_, bf16[72,4096]{1,0:T(8,128)(2,1)S(1)} %collective-permute-done.3.refs_3_), custom_call_target="tpu_custom_call" | custom-call | bytes 3538944 | tf_op jit(solution)/shard_map/scatter_columns/pallas_call | solution.py:85
  22.6 6.1 %all-to-all-start = ((bf16[8,72,1024]{2,1,0:T(8,128)(2,1)}), bf16[8,72,1024]{2,1,0:T(8,128)(2,1)S(1)}, u32[]{:S(2)}, u32[]{:S(2)}) async-start(bf16[8,72,1024]{2,1,0:T(8,128)(2,1)} %scatter_columns.1), calls=%async_computation | async-start | bytes 2359296 | tf_op jit(solution)/shard_map/all_to_all | solution.py:612
  28.7 1.6 %collective-permute-start.5 = (bf16[2,512,256]{2,1,0:T(8,128)(2,1)}, bf16[2,512,256]{2,1,0:T(8,128)(2,1)S(1)}, u32[]{:S(2)}, u32[]{:S(2)}) collective-permute-start(bf16[2,512,256]{2,1,0:T(8,128)(2,1)} %pad_maximum_fusion.1), channel_id=1, source_target_pairs={{0,3},{1,2},{2,1},{3,0},{4,7},{5,6},{6,5},{7,4},{8,11},{9,10},{10,... | collective-permute-start | bytes 1572872 | tf_op jit(solution)/shard_map/ppermute | solution.py:572
  30.3 0.5 collective-permute-start.6
  30.8 0.1 pad_add_fusion.info_ref
  30.9 0.0 collective-permute-done.4.refs_3_
  30.9 1.0 %copy-done.2 = bf16[2,512,256]{2,1,0:T(8,128)(2,1)S(1)} copy-done((bf16[2,512,256]{2,1,0:T(8,128)(2,1)S(1)}, bf16[2,512,256]{2,1,0:T(8,128)(2,1)}, u32[]{:S(2)}) %copy-start.2) | copy-done | bytes 524312
  32.0 1.3 %scale_rows.2 = (bf16[2,512,256]{2,1,0:T(8,128)(2,1)S(1)}, bf16[2,512,256]{2,1,0:T(8,128)(2,1)S(1)}) custom-call(f32[16,2]{1,0:T(8,128)S(1)} %convert_element_type.3.refs_0_, f32[16,2]{1,0:T(8,128)S(1)} %collective-permute-done.2.refs_1_, bf16[2,512,256]{2,1,0:T(8,128)(2,1)S(1)} %copy-done.2, bf16[2,512,256]{2,1,0:T(8,128)(2,1)} %collective-permute-done.4.refs_3_), custom_call_target="tpu_custom_call" | custom-call | bytes 1024 | tf_op jit(solution)/shard_map/scale_rows/pallas_call | solution.py:193
  33.3 0.8 copy-done.4
  34.1 0.8 copy-done.6
  34.9 0.9 constant_dynamic-slice_fusion
  35.7 5.4 %base_keys.2 = (f32[144,256]{1,0:T(8,128)S(1)}, f32[72,256]{1,0:T(8,128)S(1)}) custom-call(s32[4]{0:T(128)S(1)} %pad_add_fusion.info_ref, bf16[16384,256]{1,0:T(8,128)(2,1)} %base_ref.3, bf16[144,4096]{1,0:T(8,128)(2,1)} %bitcast.22, bf16[144,4096]{1,0:T(8,128)(2,1)} %copy-done.1, bf16[72,4096]{1,0:T(8,128)(2,1)S(1)} %collective-permute-done.1.refs_2_, ...), custom_call_target="tpu_custom_call" | custom-call | bytes 1024 | tf_op jit(solution)/shard_map/base_keys/pallas_call | solution.py:151
  41.1 0.6 copy-done.10
  41.8 0.6 copy-done.11
  42.4 5.5 %attend_cached.1 = (bf16[9,2,256,128]{3,2,1,0:T(8,128)(2,1)S(1)}, f32[9,2,128,256]{3,2,1,0:T(8,128)}, f32[9,2,2,256]{3,2,1,0:T(2,128)S(1)}) custom-call(s32[72]{0:T(128)S(1)} %copy-done.14, bf16[2,9,8,4096]{3,2,1,0:T(8,128)(2,1)} %bitcast.29, bf16[72,32,256]{2,1,0:T(8,128)(2,1)} %ck_ref.1, bf16[72,32,256]{2,1,0:T(8,128)(2,1)} %cv_ref.1), custom_call_target="tpu_custom_call" | custom-call | bytes 1024 | tf_op jit(solution)/shard_map/attend_cached/pallas_call | solution.py:313
  47.9 1.0 %copy-done.3 = bf16[9,2,256,128]{3,2,1,0:T(8,128)(2,1)} copy-done((bf16[9,2,256,128]{3,2,1,0:T(8,128)(2,1)}, bf16[9,2,256,128]{3,2,1,0:T(8,128)(2,1)S(1)}, u32[]{:S(2)}) %copy-start.3) | copy-done | bytes 1179672
  48.9 0.6 copy-done.12
  49.6 0.0 collective-permute-done.5.refs_2_
  49.6 4.9 %collective-permute-done.6.refs_3_ = bf16[2,512,256]{2,1,0:T(8,128)(2,1)S(1)} collective-permute-done((bf16[2,512,256]{2,1,0:T(8,128)(2,1)}, bf16[2,512,256]{2,1,0:T(8,128)(2,1)S(1)}, u32[]{:S(2)}, u32[]{:S(2)}) %collective-permute-start.6) | collective-permute-done | bytes 524320 | tf_op jit(solution)/shard_map/ppermute | solution.py:572
  54.5 1.0 %scale_rows.3 = (bf16[2,512,256]{2,1,0:T(8,128)(2,1)S(1)}, bf16[2,512,256]{2,1,0:T(8,128)(2,1)S(1)}) custom-call(f32[16,2]{1,0:T(8,128)S(1)} %convert_element_type.3.refs_0_, f32[16,2]{1,0:T(8,128)S(1)} %collective-permute-done.2.refs_1_, bf16[2,512,256]{2,1,0:T(8,128)(2,1)S(1)} %collective-permute-done.5.refs_2_, ...), custom_call_target="tpu_custom_call" | custom-call | bytes 1024 | tf_op jit(solution)/shard_map/scale_rows/pallas_call | solution.py:193
  55.5 0.8 copy-done.8
  56.3 1.3 %all-to-all-done = bf16[8,72,1024]{2,1,0:T(8,128)(2,1)S(1)} async-done(((bf16[8,72,1024]{2,1,0:T(8,128)(2,1)}), bf16[8,72,1024]{2,1,0:T(8,128)(2,1)S(1)}, u32[]{:S(2)}, u32[]{:S(2)}) %all-to-all-start) | async-done | bytes 1179680 | tf_op jit(solution)/shard_map/all_to_all | solution.py:612
  57.6 1.6 %collective-permute-start.8 = (bf16[72,4096]{1,0:T(8,128)(2,1)S(1)}, bf16[72,4096]{1,0:T(8,128)(2,1)S(1)}, u32[]{:S(2)}, u32[]{:S(2)}) collective-permute-start(bf16[72,4096]{1,0:T(8,128)(2,1)S(1)} %copy-done.18), channel_id=1, source_target_pairs={{0,2},{2,0},{1,3},{3,1},{4,6},{6,4},{5,7},{7,5},{8,10},{10,8},{9,1... | collective-permute-start | bytes 1769480 | tf_op jit(solution)/shard_map/ppermute | solution.py:593
  59.1 1.0 %copy-done.9 = bf16[2,512,256]{2,1,0:T(8,128)(2,1)S(1)} copy-done((bf16[2,512,256]{2,1,0:T(8,128)(2,1)S(1)}, bf16[2,512,256]{2,1,0:T(8,128)(2,1)}, u32[]{:S(2)}) %copy-start.9) | copy-done | bytes 524312
  60.2 0.8 partial_keys.2.refs_3_
  61.0 1.6 %partial_keys.3 = bf16[8,2,72,256]{3,2,1,0:T(8,128)(2,1)} custom-call(bf16[576,1024]{1,0:T(8,128)(2,1)S(1)} %collective-permute-done.7.refs_0_, bf16[2,512,256]{2,1,0:T(8,128)(2,1)S(1)} %copy-done.5, bf16[2,512,256]{2,1,0:T(8,128)(2,1)S(1)} %get-tuple-element.60.refs_2_, f32[2,576,256]{2,1,0:T(8,128)S(1)} %partial_keys.2.refs_3_), custom_call_target="tpu_custom_call" | custom-call | flops 603979776 | bytes 3997696 | tf_op jit(solution)/shard_map/partial_keys/pallas_call | solution.py:237
  62.6 5.1 %all-to-all-start.1 = ((bf16[16,72,256]{2,1,0:T(8,128)(2,1)}), bf16[16,72,256]{2,1,0:T(8,128)(2,1)S(1)}, u32[]{:S(2)}, u32[]{:S(2)}) async-start(bf16[16,72,256]{2,1,0:T(8,128)(2,1)} %bitcast.12), calls=%async_computation.1 | async-start | bytes 1179648 | tf_op jit(solution)/shard_map/all_to_all | solution.py:622
  67.7 6.5 %collective-permute-done.8.refs_0_ = bf16[72,4096]{1,0:T(8,128)(2,1)S(1)} collective-permute-done((bf16[72,4096]{1,0:T(8,128)(2,1)S(1)}, bf16[72,4096]{1,0:T(8,128)(2,1)S(1)}, u32[]{:S(2)}, u32[]{:S(2)}) %collective-permute-start.8) | collective-permute-done | bytes 589856 | tf_op jit(solution)/shard_map/ppermute | solution.py:593
  74.2 0.7 pad_add_fusion.1.info_ref
  74.9 1.3 %collective-permute-done.9.refs_1_ = bf16[72,4096]{1,0:T(8,128)(2,1)S(1)} collective-permute-done((bf16[72,4096]{1,0:T(8,128)(2,1)S(1)}, bf16[72,4096]{1,0:T(8,128)(2,1)S(1)}, u32[]{:S(2)}, u32[]{:S(2)}) %collective-permute-start.9) | collective-permute-done | bytes 589856 | tf_op jit(solution)/shard_map/ppermute | solution.py:508
  76.2 0.8 copy-done.17
  77.0 4.3 %base_keys.3.refs_3_ = f32[72,256]{1,0:T(8,128)} custom-call(s32[2]{0:T(128)} %pad_add_fusion.1.info_ref, bf16[16384,256]{1,0:T(8,128)(2,1)} %base_ref.3, bf16[72,4096]{1,0:T(8,128)(2,1)} %copy-done.16, bf16[72,4096]{1,0:T(8,128)(2,1)} %copy-done.17), custom_call_target="tpu_custom_call" | custom-call | bytes 1024 | tf_op jit(solution)/shard_map/base_keys/pallas_call | solution.py:151
  81.3 2.9 %all-to-all-done.1 = bf16[16,72,256]{2,1,0:T(8,128)(2,1)S(1)} async-done(((bf16[16,72,256]{2,1,0:T(8,128)(2,1)}), bf16[16,72,256]{2,1,0:T(8,128)(2,1)S(1)}, u32[]{:S(2)}, u32[]{:S(2)}) %all-to-all-start.1) | async-done | bytes 589856 | tf_op jit(solution)/shard_map/all_to_all | solution.py:622
  84.2 0.8 copy-done.15
  85.1 5.2 %attend_new.1 = (bf16[2,9,8,4096]{3,2,1,0:T(8,128)(2,1)}, bf16[2,9,8,256]{3,2,1,0:T(8,128)(2,1)}) custom-call(bf16[8,2,72,256]{3,2,1,0:T(8,128)(2,1)} %bitcast.28, f32[144,256]{1,0:T(8,128)} %copy-done.10, f32[72,256]{1,0:T(8,128)} %copy-done.11, f32[72,256]{1,0:T(8,128)} %base_keys.3.refs_3_, bf16[2,9,8,256]{3,2,1,0:T(8,128)(2,1)} %bitcast.30, ...), custom_call_target="tpu_custom_call" | custom-call | flops 603979776 | bytes 5898240 | tf_op jit(solution)/shard_map/attend_new/pallas_call | solution.py:466
  (34 shorter events, 0.1 us)
Async XLA Ops:
  0.6 4.2 %copy-start = (bf16[2,72,4096]{2,1,0:T(8,128)(2,1)S(1)}, bf16[2,72,4096]{2,1,0:T(8,128)(2,1)}, u32[]{:S(2)}) copy-start(bf16[2,72,4096]{2,1,0:T(8,128)(2,1)} %refs_0_.1) | copy-start | bytes 3538948
  0.6 4.2 %copy-start.19 = (bf16[16,2]{0,1:T(2,128)(2,1)S(1)}, bf16[16,2]{0,1:T(2,128)(2,1)}, u32[]{:S(2)}) copy-start(bf16[16,2]{0,1:T(2,128)(2,1)} %param.18) | copy-start | bytes 196
  1.9 16.4 %collective-permute-start.1 = (bf16[72,4096]{1,0:T(8,128)(2,1)S(1)}, bf16[72,4096]{1,0:T(8,128)(2,1)S(1)}, u32[]{:S(2)}, u32[]{:S(2)}) collective-permute-start(bf16[72,4096]{1,0:T(8,128)(2,1)S(1)} %constant_dynamic-slice_fusion.1), channel_id=1, source_target_pairs={{0,2},{2,0},{1,3},{3,1},{4,6},{6,4},{5,7},{7,5},{8,10},{10,8},{9,1... | collective-permute-start | bytes 1769480 | tf_op jit(solution)/shard_map/ppermute | solution.py:557
  4.9 15.5 %collective-permute-start = (bf16[144,4096]{1,0:T(8,128)(2,1)S(1)}, bf16[144,4096]{1,0:T(8,128)(2,1)S(1)}, u32[]{:S(2)}, u32[]{:S(2)}) collective-permute-start(bf16[144,4096]{1,0:T(8,128)(2,1)S(1)} %bitcast.23), channel_id=1, source_target_pairs={{0,1},{1,0},{2,3},{3,2},{4,5},{5,4},{6,7},{7,6},{8,9},{9,8},{10,11... | collective-permute-start | bytes 3538952 | tf_op jit(solution)/shard_map/ppermute | solution.py:508
  5.0 13.4 %collective-permute-start.2 = (f32[16,2]{1,0:T(8,128)S(1)}, f32[16,2]{1,0:T(8,128)S(1)}, u32[]{:S(2)}, u32[]{:S(2)}) collective-permute-start(f32[16,2]{1,0:T(8,128)S(1)} %convert_element_type.3.refs_0_), channel_id=1, source_target_pairs={{0,2},{2,0},{1,3},{3,1},{4,6},{6,4},{5,7},{7,5},{8,10},{10,8},{9,1... | collective-permute-start | bytes 392 | tf_op jit(solution)/shard_map/ppermute | solution.py:546
  6.4 14.0 %copy-start.13 = (s32[128]{0:T(128)S(1)}, s32[128]{0:T(128)}, u32[]{:S(2)}) copy-start(s32[128]{0:T(128)} %order_ref.1) | copy-start | bytes 1540
  18.4 2.0 %collective-permute-start.3 = (bf16[72,4096]{1,0:T(8,128)(2,1)S(1)}, bf16[72,4096]{1,0:T(8,128)(2,1)S(1)}, u32[]{:S(2)}, u32[]{:S(2)}) collective-permute-start(bf16[72,4096]{1,0:T(8,128)(2,1)S(1)} %collective-permute-done.1.refs_2_), channel_id=1, source_target_pairs={{0,1},{1,0},{2,3},{3,2},{4,5},{5,4},{6,7},{7,6},{8,9},{9,8},{10,11... | collective-permute-start | bytes 1769480 | tf_op jit(solution)/shard_map/ppermute | solution.py:508
  20.4 2.2 %copy-start.1 = (bf16[144,4096]{1,0:T(8,128)(2,1)}, bf16[144,4096]{1,0:T(8,128)(2,1)S(1)}, u32[]{:S(2)}) copy-start(bf16[144,4096]{1,0:T(8,128)(2,1)S(1)} %collective-permute-done.refs_1_) | copy-start | bytes 3538948
  22.6 35.0 %all-to-all-start = ((bf16[8,72,1024]{2,1,0:T(8,128)(2,1)}), bf16[8,72,1024]{2,1,0:T(8,128)(2,1)S(1)}, u32[]{:S(2)}, u32[]{:S(2)}) async-start(bf16[8,72,1024]{2,1,0:T(8,128)(2,1)} %scatter_columns.1), calls=%async_computation | async-start | bytes 2359296 | tf_op jit(solution)/shard_map/all_to_all | solution.py:612
  28.7 2.3 %collective-permute-start.4 = (bf16[2,512,256]{2,1,0:T(8,128)(2,1)}, bf16[2,512,256]{2,1,0:T(8,128)(2,1)}, u32[]{:S(2)}, u32[]{:S(2)}) collective-permute-start(bf16[2,512,256]{2,1,0:T(8,128)(2,1)} %pad_maximum_fusion.1), channel_id=1, source_target_pairs={{0,1},{1,0},{2,3},{3,2},{4,5},{5,4},{6,7},{7,6},{8,9},{9,8},{10,11... | collective-permute-start | bytes 1572872 | tf_op jit(solution)/shard_map/ppermute | solution.py:572
  28.7 20.8 %collective-permute-start.5 = (bf16[2,512,256]{2,1,0:T(8,128)(2,1)}, bf16[2,512,256]{2,1,0:T(8,128)(2,1)S(1)}, u32[]{:S(2)}, u32[]{:S(2)}) collective-permute-start(bf16[2,512,256]{2,1,0:T(8,128)(2,1)} %pad_maximum_fusion.1), channel_id=1, source_target_pairs={{0,3},{1,2},{2,1},{3,0},{4,7},{5,6},{6,5},{7,4},{8,11},{9,10},{10,... | collective-permute-start | bytes 1572872 | tf_op jit(solution)/shard_map/ppermute | solution.py:572
  30.3 24.1 %collective-permute-start.6 = (bf16[2,512,256]{2,1,0:T(8,128)(2,1)}, bf16[2,512,256]{2,1,0:T(8,128)(2,1)S(1)}, u32[]{:S(2)}, u32[]{:S(2)}) collective-permute-start(bf16[2,512,256]{2,1,0:T(8,128)(2,1)} %pad_maximum_fusion.refs_2_), channel_id=1, source_target_pairs={{0,2},{1,3},{2,0},{3,1},{4,6},{5,7},{6,4},{7,5},{8,10},{9,11},{10,... | collective-permute-start | bytes 1572872 | tf_op jit(solution)/shard_map/ppermute | solution.py:572
  30.9 1.0 %copy-start.2 = (bf16[2,512,256]{2,1,0:T(8,128)(2,1)S(1)}, bf16[2,512,256]{2,1,0:T(8,128)(2,1)}, u32[]{:S(2)}) copy-start(bf16[2,512,256]{2,1,0:T(8,128)(2,1)} %pad_maximum_fusion.refs_2_) | copy-start | bytes 1572868
  33.3 0.8 copy-start.4
  34.1 0.8 copy-start.6
  35.7 6.7 %copy-start.14 = (s32[72]{0:T(128)S(1)}, s32[72]{0:T(128)}, u32[]{:S(2)}) copy-start(s32[72]{0:T(128)} %len_ref) | copy-start | bytes 868
  41.1 0.7 copy-start.10
  41.8 0.6 copy-start.11
  42.4 15.1 %copy-start.18 = (bf16[72,4096]{1,0:T(8,128)(2,1)S(1)}, bf16[72,4096]{1,0:T(8,128)(2,1)}, u32[]{:S(2)}) copy-start(bf16[72,4096]{1,0:T(8,128)(2,1)} %constant_dynamic-slice_fusion) | copy-start | bytes 1769476
  47.9 1.0 %copy-start.3 = (bf16[9,2,256,128]{3,2,1,0:T(8,128)(2,1)}, bf16[9,2,256,128]{3,2,1,0:T(8,128)(2,1)S(1)}, u32[]{:S(2)}) copy-start(bf16[9,2,256,128]{3,2,1,0:T(8,128)(2,1)S(1)} %get-tuple-element.53.refs_5_) | copy-start | bytes 3538948
  48.9 0.6 copy-start.12
  49.5 9.6 %copy-start.7 = (bf16[2,512,256]{2,1,0:T(8,128)(2,1)S(1)}, bf16[2,512,256]{2,1,0:T(8,128)(2,1)}, u32[]{:S(2)}) copy-start(bf16[2,512,256]{2,1,0:T(8,128)(2,1)} %copy-done.6) | copy-start | bytes 1572868
  55.5 0.8 copy-start.8
  57.6 3.4 %copy-start.5 = (bf16[2,512,256]{2,1,0:T(8,128)(2,1)S(1)}, bf16[2,512,256]{2,1,0:T(8,128)(2,1)}, u32[]{:S(2)}) copy-start(bf16[2,512,256]{2,1,0:T(8,128)(2,1)} %copy-done.4) | copy-start | bytes 1572868
  57.6 3.4 %collective-permute-start.7 = (bf16[576,1024]{1,0:T(8,128)(2,1)S(1)}, bf16[576,1024]{1,0:T(8,128)(2,1)S(1)}, u32[]{:S(2)}, u32[]{:S(2)}) collective-permute-start(bf16[576,1024]{1,0:T(8,128)(2,1)S(1)} %bitcast.26), channel_id=1, source_target_pairs={{0,1},{1,0},{2,3},{3,2},{4,5},{5,4},{6,7},{7,6},{8,9},{9,8},{10,11... | collective-permute-start | bytes 3538952 | tf_op jit(solution)/shard_map/ppermute | solution.py:508
  57.6 16.6 %collective-permute-start.8 = (bf16[72,4096]{1,0:T(8,128)(2,1)S(1)}, bf16[72,4096]{1,0:T(8,128)(2,1)S(1)}, u32[]{:S(2)}, u32[]{:S(2)}) collective-permute-start(bf16[72,4096]{1,0:T(8,128)(2,1)S(1)} %copy-done.18), channel_id=1, source_target_pairs={{0,2},{2,0},{1,3},{3,1},{4,6},{6,4},{5,7},{7,5},{8,10},{10,8},{9,1... | collective-permute-start | bytes 1769480 | tf_op jit(solution)/shard_map/ppermute | solution.py:593
  59.1 1.0 %copy-start.9 = (bf16[2,512,256]{2,1,0:T(8,128)(2,1)S(1)}, bf16[2,512,256]{2,1,0:T(8,128)(2,1)}, u32[]{:S(2)}) copy-start(bf16[2,512,256]{2,1,0:T(8,128)(2,1)} %copy-done.8) | copy-start | bytes 1572868
  62.6 21.7 %all-to-all-start.1 = ((bf16[16,72,256]{2,1,0:T(8,128)(2,1)}), bf16[16,72,256]{2,1,0:T(8,128)(2,1)S(1)}, u32[]{:S(2)}, u32[]{:S(2)}) async-start(bf16[16,72,256]{2,1,0:T(8,128)(2,1)} %bitcast.12), calls=%async_computation.1 | async-start | bytes 1179648 | tf_op jit(solution)/shard_map/all_to_all | solution.py:622
  74.2 2.0 %copy-start.16 = (bf16[72,4096]{1,0:T(8,128)(2,1)}, bf16[72,4096]{1,0:T(8,128)(2,1)S(1)}, u32[]{:S(2)}) copy-start(bf16[72,4096]{1,0:T(8,128)(2,1)S(1)} %collective-permute-done.8.refs_0_) | copy-start | bytes 1769476
  74.2 2.0 %collective-permute-start.9 = (bf16[72,4096]{1,0:T(8,128)(2,1)S(1)}, bf16[72,4096]{1,0:T(8,128)(2,1)S(1)}, u32[]{:S(2)}, u32[]{:S(2)}) collective-permute-start(bf16[72,4096]{1,0:T(8,128)(2,1)S(1)} %collective-permute-done.8.refs_0_), channel_id=1, source_target_pairs={{0,1},{1,0},{2,3},{3,2},{4,5},{5,4},{6,7},{7,6},{8,9},{9,8},{10,11... | collective-permute-start | bytes 1769480 | tf_op jit(solution)/shard_map/ppermute | solution.py:508
  76.2 0.8 copy-start.17
  84.2 0.8 copy-start.15
